TPU v7x, 512 devices: a whole 4x8x8 slice. The times are simulated.
512 devices in a mesh: grp: 16 (over z, core), ex: 32 (over y, x).
Axes of the slice: x: 4, y: 8, z: 8, core: 2. Of those that a mesh axis runs over, the one named last changes fastest.
Arguments:
- tokens: bfloat16 [8192, 2880], P('ex', 'grp'), may hold values from -6 to 6
- out_grad: bfloat16 [8192, 2880], P('ex', 'grp'), may hold values from -6 to 6
- expert_ids: int32 [8192, 4], P('ex'), may hold values from 0 to 127, all different within a row; in each aligned block of 256 rows (0 to 255, 256 to 511, ...) at most 16 rows name the same one
- gate_values: bfloat16 [8192, 4], P('ex'), may hold values from 0.049804688 to 0.59765625
- w_gate: bfloat16 [32, 2880, 2880], P('ex', 'grp'), may hold values from -0.109375 to 0.109375
- w_up: bfloat16 [32, 2880, 2880], P('ex', 'grp'), may hold values from -0.109375 to 0.109375
- w_down: bfloat16 [32, 2880, 2880], P('ex', 'grp'), may hold values from -0.109375 to 0.109375
Outputs:
- token_grad: bfloat16 [8192, 2880], P('ex', 'grp')
- gate_grad: float32 [8192, 4], P('ex')
Inputs may be any that keep to these rules, and one draw needn't show every extreme that they name: `expert_ids`: each row names 4 different experts. Among the rows of one index of ex no expert is named more than 16 times, a bound that some block reaches there.
All inputs are finite; a program needn't handle non-finite values.
Results may differ from a plain program's by a relative error of at most 0.019.
Values may be sent and summed in bfloat16 or wider, within the bound.
No kernel may reach another device: no remote copies, remote signals or barrier semaphores. Data moves between devices by JAX's collectives and lax.ppermute only.
A program may use at most 64 MiB of HBM per device.

v0:
```python
import jax
import jax.numpy as jnp
from jax import lax
from jax.sharding import PartitionSpec as P

TOP = 4
CAP = 16


def contract_last(left, right):
    return lax.dot_general(
        left, right, (((1,), (1,)), ((), ())), preferred_element_type=jnp.float32
    )


def contract_first(left, right):
    return lax.dot_general(
        left, right, (((0,), (0,)), ((), ())), preferred_element_type=jnp.float32, precision=None
    )


def per_device(tokens, out_grad, expert_ids, gate_values, w_gate, w_up, w_down):
    highest = lax.Precision.HIGHEST
    wgate = w_gate[0]
    wup = w_up[0]
    wdown = w_down[0]
    experts_here = lax.axis_size("ex")
    num_slots = experts_here * CAP
    tok_count = tokens.shape[0]
    flat_ids = expert_ids.reshape(-1)
    onehot = (flat_ids[:, None] == jnp.arange(experts_here, dtype=jnp.int32)[None, :]).astype(
        jnp.int32
    )
    before = jnp.cumsum(onehot, axis=0) - onehot
    place = jnp.sum(before * onehot, axis=1)
    target = jnp.where(flat_ids < experts_here, flat_ids * CAP + place, -1).reshape(tok_count, TOP)
    slot_index = jnp.arange(num_slots, dtype=jnp.int32)
    picks = (target.T[:, None, :] == slot_index[None, :, None]).astype(jnp.float32)
    select = jnp.sum(picks, axis=0)
    select_half = select.astype(jnp.bfloat16)
    slot_gate = jnp.einsum("kst,tk->s", picks, gate_values.astype(jnp.float32), precision=highest)
    send_gate = slot_gate.astype(jnp.bfloat16).reshape(experts_here, CAP)
    full_tok, full_grad = (
        lax.all_gather(tokens, "grp", axis=1, tiled=True),
        lax.all_gather(out_grad, "grp", axis=1, tiled=True),
    )
    send_tok = jnp.dot(select_half, full_tok, preferred_element_type=jnp.float32).astype(
        jnp.bfloat16
    )
    send_grad = jnp.dot(select_half, full_grad, preferred_element_type=jnp.float32).astype(
        jnp.bfloat16
    )
    recv_tok, recv_grad, recv_gate = (
        lax.all_to_all(
            send_tok.reshape(experts_here, CAP, -1), "ex", split_axis=0, concat_axis=0, tiled=True
        ),
        lax.all_to_all(
            send_grad.reshape(experts_here, CAP, -1), "ex", split_axis=0, concat_axis=0, tiled=True
        ),
        lax.all_to_all(send_gate, "ex", split_axis=0, concat_axis=0, tiled=True),
    )
    rows_tok = recv_tok.reshape(num_slots, -1)
    rows_grad = recv_grad.reshape(num_slots, -1)
    pre_gate = contract_last(rows_tok, wgate)
    pre_up = contract_last(rows_tok, wup)
    back = contract_last(rows_grad, wdown)
    weight = recv_gate.reshape(num_slots).astype(jnp.float32)
    sig = jax.nn.sigmoid(pre_gate)
    act = pre_gate * sig
    prob_grad = jnp.sum(back * act * pre_up, axis=1)
    hid_grad = weight[:, None] * back
    d_gate = (hid_grad * pre_up * sig * (1.0 + pre_gate * (1.0 - sig))).astype(jnp.bfloat16)
    d_up = (hid_grad * act).astype(jnp.bfloat16)
    group_terms = (
        jnp.dot(d_gate, wgate, preferred_element_type=jnp.float32)
        + jnp.dot(d_up, wup, preferred_element_type=jnp.float32)
    ).astype(jnp.bfloat16)
    back_terms = lax.all_to_all(
        group_terms.reshape(experts_here, CAP, -1), "ex", split_axis=0, concat_axis=0, tiled=True
    )
    prob_all = lax.psum(prob_grad, "grp")
    prob_back = lax.all_to_all(
        prob_all.reshape(experts_here, CAP), "ex", split_axis=0, concat_axis=0, tiled=True
    )
    local_sum = contract_first(select_half, back_terms.reshape(num_slots, -1))
    token_grad = lax.psum_scatter(
        local_sum.astype(jnp.bfloat16), "grp", scatter_dimension=1, tiled=True
    )
    prob_slots = prob_back.reshape(num_slots)
    gate_grad = jnp.einsum("kst,s->tk", picks, prob_slots, precision=highest)
    return (token_grad, gate_grad)


def solution(mesh):
    return jax.shard_map(
        per_device,
        mesh=mesh,
        in_specs=(
            P("ex", "grp"),
            P("ex", "grp"),
            P("ex", None),
            P("ex", None),
            P("ex", "grp", None),
            P("ex", "grp", None),
            P("ex", "grp", None),
        ),
        out_specs=(P("ex", "grp"), P("ex", None)),
        check_vma=False,
    )
```

profile of v0, /device:TPU:1, one launch (start us, length us, event | category | flops | bytes accessed | tf_op | source)
XLA Modules:
  0.0 414.9 jit_solution(9085655840712154682)
XLA Ops:
  7.2 0.0 copy-start
  7.2 0.0 all-gather.7.cloned.1.call-start
  7.2 0.7 all-gather.7.cloned.1.call-update
  7.9 0.8 copy.49
  8.7 0.1 eq.42
  8.9 0.1 eq.38
  9.0 9.0 %reduce-window.6 = s32[32,8,128]{2,1,0:T(8,128)S(1)} reduce-window(s32[32,8,128]{2,1,0:T(8,128)S(1)} %fusion.21, s32[]{:T(128)} %constant.4.clone.1), window={size=1x1x128 pad=0_0x0_0x127_0}, to_apply=%region_0.0 | reduce-window | flops 4161536 | bytes 262148 | tf_op jit(solution)/shard_map/reduce-window
  18.0 0.1 slice.8
  18.1 0.1 copy.51
  18.3 0.1 copy.52
  18.4 0.1 broadcast_add_fusion
  18.5 0.1 reduce_sum.30
  18.7 0.1 copy.53
  18.7 0.7 select_bitcast_fusion
  19.4 1.1 fusion.2
  20.6 0.7 all_to_all.28
  21.3 10.5 %all-to-all-start = ((bf16[32,1,16]{2,1,0:T(2,128)(2,1)}), bf16[32,1,16]{2,1,0:T(2,128)(2,1)S(1)}, u32[]{:S(2)}, u32[]{:S(2)}) async-start(bf16[32,1,16]{2,1,0:T(2,128)(2,1)} %all_to_all.28), calls=%async_computation | async-start | bytes 32768 | tf_op jit(solution)/shard_map/all_to_all | solution.py:60
  31.8 0.3 convert_reduce_fusion
  32.1 26.5 %all-gather.7.cloned.1.call-done = bf16[16,180,256]{2,1,0:T(8,128)(2,1)} async-done(((bf16[1,180,256]{2,1,0:T(8,128)(2,1)}), bf16[16,180,256]{2,1,0:T(8,128)(2,1)}) %all-gather.7.cloned.1.call-update) | async-done | bytes 1474576 | tf_op jit(solution)/shard_map/all_gather | solution.py:44
  58.6 2.3 reshape.76
  60.8 2.6 convolution_convert_fusion
  63.4 4.6 %copy.56 = bf16[512,2880]{1,0:T(8,128)(2,1)} copy(bf16[512,2880]{0,1:T(8,128)(2,1)} %convolution_convert_fusion) | data formatting | bytes 5898240 | tf_op jit(solution)/shard_map/convert_element_type | solution.py:47
  68.0 0.0 all-to-all-done
  68.0 9.3 %all-to-all-start.2 = ((bf16[32,16,2880]{2,1,0:T(8,128)(2,1)}), bf16[32,16,2880]{2,1,0:T(8,128)(2,1)}, u32[]{:S(2)}, u32[]{:S(2)}) async-start(bf16[32,16,2880]{2,1,0:T(8,128)(2,1)} %bitcast.68), calls=%async_computation.2 | async-start | bytes 6029312 | tf_op jit(solution)/shard_map/all_to_all | solution.py:54
  77.4 0.0 all-gather.5.cloned.1.call-start
  77.4 0.7 all-gather.5.cloned.1.call-update
  78.1 43.3 %all-gather.5.cloned.1.call-done = bf16[16,180,256]{2,1,0:T(8,128)(2,1)} async-done(((bf16[1,180,256]{2,1,0:T(8,128)(2,1)}), bf16[16,180,256]{2,1,0:T(8,128)(2,1)}) %all-gather.5.cloned.1.call-update) | async-done | bytes 1474576 | tf_op jit(solution)/shard_map/all_gather | solution.py:45
  121.4 2.3 reshape.74
  123.7 2.6 convolution_convert_fusion.1
  126.3 4.7 %copy.55 = bf16[512,2880]{1,0:T(8,128)(2,1)} copy(bf16[512,2880]{0,1:T(8,128)(2,1)} %convolution_convert_fusion.1) | data formatting | bytes 5898240 | tf_op jit(solution)/shard_map/convert_element_type | solution.py:50
  130.9 14.6 %all-to-all-done.2 = bf16[32,16,2880]{2,1,0:T(8,128)(2,1)} async-done(((bf16[32,16,2880]{2,1,0:T(8,128)(2,1)}), bf16[32,16,2880]{2,1,0:T(8,128)(2,1)}, u32[]{:S(2)}, u32[]{:S(2)}) %all-to-all-start.2) | async-done | bytes 2949152 | tf_op jit(solution)/shard_map/all_to_all | solution.py:54
  145.5 0.0 copy-start.1
  145.5 7.8 %all-to-all-start.1 = ((bf16[32,16,2880]{2,1,0:T(8,128)(2,1)}), bf16[32,16,2880]{2,1,0:T(8,128)(2,1)}, u32[]{:S(2)}, u32[]{:S(2)}) async-start(bf16[32,16,2880]{2,1,0:T(8,128)(2,1)} %bitcast.70), calls=%async_computation.1 | async-start | bytes 6029312 | tf_op jit(solution)/shard_map/all_to_all | solution.py:57
  153.3 0.1 convert_reduce_fusion.1
  153.4 0.1 reshape.72
  153.5 0.0 copy-done.1
  153.5 3.0 fusion.5
  156.5 64.3 %all-to-all-done.1 = bf16[32,16,2880]{2,1,0:T(8,128)(2,1)} async-done(((bf16[32,16,2880]{2,1,0:T(8,128)(2,1)}), bf16[32,16,2880]{2,1,0:T(8,128)(2,1)}, u32[]{:S(2)}, u32[]{:S(2)}) %all-to-all-start.1) | async-done | bytes 2949152 | tf_op jit(solution)/shard_map/all_to_all | solution.py:57
  220.8 3.3 fusion.10
  224.1 0.0 copy-done
  224.2 3.0 multiply_reduce_fusion
  227.2 0.1 all_to_all.26
  227.3 45.1 %psum.7 = f32[32,1,16]{2,0,1:T(8,128)} all-reduce(f32[32,1,16]{2,0,1:T(8,128)S(1)} %all_to_all.26), channel_id=1, replica_groups=mesh['grp'=16,'ex'=32] {'grp'}, use_global_device_ids=true, to_apply=%region_6.7 | all-reduce | flops 512 | bytes 4096 | tf_op jit(solution)/shard_map/psum | solution.py:81
  272.4 6.5 %all-to-all-start.4 = ((f32[32,1,16]{2,1,0:T(1,128)}), f32[32,1,16]{2,1,0:T(1,128)S(1)}, u32[]{:S(2)}, u32[]{:S(2)}) async-start(f32[32,1,16]{2,1,0:T(1,128)} %bitcast.18), calls=%async_computation.4 | async-start | bytes 32768 | tf_op jit(solution)/shard_map/all_to_all | solution.py:82
  278.9 2.3 fusion.3
  281.2 2.7 add_convert_fusion
  283.9 4.6 %copy.57 = bf16[512,2880]{1,0:T(8,128)(2,1)} copy(bf16[512,2880]{0,1:T(8,128)(2,1)} %add_convert_fusion) | data formatting | bytes 5898240 | tf_op jit(solution)/shard_map/convert_element_type | solution.py:77
  288.5 0.0 all-to-all-done.4
  288.5 9.5 %all-to-all-start.3 = ((bf16[32,16,2880]{2,1,0:T(8,128)(2,1)}), bf16[32,16,2880]{2,1,0:T(8,128)(2,1)}, u32[]{:S(2)}, u32[]{:S(2)}) async-start(bf16[32,16,2880]{2,1,0:T(8,128)(2,1)} %bitcast.69), calls=%async_computation.3 | async-start | bytes 6029312 | tf_op jit(solution)/shard_map/all_to_all | solution.py:78
  298.0 1.3 dynamic-slice.4
  299.9 0.5 broadcast.42
  300.4 0.7 reduce.7
  301.1 0.1 reshape.79
  301.2 59.1 %all-to-all-done.3 = bf16[32,16,2880]{2,1,0:T(8,128)(2,1)} async-done(((bf16[32,16,2880]{2,1,0:T(8,128)(2,1)}), bf16[32,16,2880]{2,1,0:T(8,128)(2,1)}, u32[]{:S(2)}, u32[]{:S(2)}) %all-to-all-start.3) | async-done | bytes 2949152 | tf_op jit(solution)/shard_map/all_to_all | solution.py:78
  360.3 3.1 convolution_convert_fusion.2
  363.4 37.7 %fusion = bf16[256,184]{0,1:T(8,128)(2,1)S(1)} fusion(bf16[256,2880]{0,1:T(8,128)(2,1)S(1)} %convolution_convert_fusion.2), kind=kCustom, calls=%all-reduce-scatter | all-reduce-scatter fusion | flops 753665 | bytes 1570816
  401.1 3.6 collective-permute-start
  404.7 0.7 fusion.1
  405.4 0.6 copy.66
  406.0 1.1 collective-permute-done
  407.1 0.2 concatenate
  407.4 0.7 constant_dynamic-slice_fusion
  (6 shorter events, 0.1 us)
Async XLA Ops:
  7.2 217.0 %copy-start = (bf16[1,180,2880]{2,1,0:T(8,128)(2,1)S(1)}, bf16[1,180,2880]{2,1,0:T(8,128)(2,1)}, u32[]{:S(2)}) copy-start(bf16[1,180,2880]{2,1,0:T(8,128)(2,1)} %param.12) | copy-start | bytes 3110404
  7.2 51.4 %all-gather.7.cloned.1.call-start = ((), (), s32[]{:S(2)}) async-start(), calls=%async_computation.6 | async-start | bytes 1601536 | tf_op jit(solution)/shard_map/all_gather | solution.py:44
  21.3 46.7 %all-to-all-start = ((bf16[32,1,16]{2,1,0:T(2,128)(2,1)}), bf16[32,1,16]{2,1,0:T(2,128)(2,1)S(1)}, u32[]{:S(2)}, u32[]{:S(2)}) async-start(bf16[32,1,16]{2,1,0:T(2,128)(2,1)} %all_to_all.28), calls=%async_computation | async-start | bytes 32768 | tf_op jit(solution)/shard_map/all_to_all | solution.py:60
  68.0 77.5 %all-to-all-start.2 = ((bf16[32,16,2880]{2,1,0:T(8,128)(2,1)}), bf16[32,16,2880]{2,1,0:T(8,128)(2,1)}, u32[]{:S(2)}, u32[]{:S(2)}) async-start(bf16[32,16,2880]{2,1,0:T(8,128)(2,1)} %bitcast.68), calls=%async_computation.2 | async-start | bytes 6029312 | tf_op jit(solution)/shard_map/all_to_all | solution.py:54
  77.4 44.1 %all-gather.5.cloned.1.call-start = ((), (), s32[]{:S(2)}) async-start(), calls=%async_computation.5 | async-start | bytes 1601536 | tf_op jit(solution)/shard_map/all_gather | solution.py:45
  145.5 7.9 %copy-start.1 = (bf16[1,180,2880]{2,1,0:T(8,128)(2,1)S(1)}, bf16[1,180,2880]{2,1,0:T(8,128)(2,1)}, u32[]{:S(2)}) copy-start(bf16[1,180,2880]{2,1,0:T(8,128)(2,1)} %param.11) | copy-start | bytes 3110404
  145.5 75.3 %all-to-all-start.1 = ((bf16[32,16,2880]{2,1,0:T(8,128)(2,1)}), bf16[32,16,2880]{2,1,0:T(8,128)(2,1)}, u32[]{:S(2)}, u32[]{:S(2)}) async-start(bf16[32,16,2880]{2,1,0:T(8,128)(2,1)} %bitcast.70), calls=%async_computation.1 | async-start | bytes 6029312 | tf_op jit(solution)/shard_map/all_to_all | solution.py:57
  272.4 16.1 %all-to-all-start.4 = ((f32[32,1,16]{2,1,0:T(1,128)}), f32[32,1,16]{2,1,0:T(1,128)S(1)}, u32[]{:S(2)}, u32[]{:S(2)}) async-start(f32[32,1,16]{2,1,0:T(1,128)} %bitcast.18), calls=%async_computation.4 | async-start | bytes 32768 | tf_op jit(solution)/shard_map/all_to_all | solution.py:82
  288.5 71.8 %all-to-all-start.3 = ((bf16[32,16,2880]{2,1,0:T(8,128)(2,1)}), bf16[32,16,2880]{2,1,0:T(8,128)(2,1)}, u32[]{:S(2)}, u32[]{:S(2)}) async-start(bf16[32,16,2880]{2,1,0:T(8,128)(2,1)} %bitcast.69), calls=%async_computation.3 | async-start | bytes 6029312 | tf_op jit(solution)/shard_map/all_to_all | solution.py:78
  401.1 6.0 %collective-permute-start = (bf16[256,60]{0,1:T(8,128)(2,1)S(1)}, bf16[256,60]{0,1:T(8,128)(2,1)S(1)}, u32[]{:S(2)}, u32[]{:S(2)}) collective-permute-start(bf16[256,60]{0,1:T(8,128)(2,1)S(1)} %slice.10), channel_id=1, source_target_pairs={{0,32},{32,64},{64,96},{96,128},{128,160},{160,192},{192,224},{224... | collective-permute-start | bytes 92168
Sparse Core Ops, SparseCore 0:
  10.1 48.4 all-gather.6
  80.3 41.0 all-gather.4
where the time goes:
time: 416 us; the launch traced here: 415 us
  waiting for transfers between devices  210 us (50%)
  blocking collectives  82.8 us (20%)
  starting transfers between devices  47.2 us (11%)
  matrix products  24.5 us (6%)
  local copies, waits for them, and re-layouts  24.1 us (6%)
  between operations  14.9 us (4%)
  other arithmetic  10.9 us (3%)
    all_to_all x1, waiting for transfers between devices, per_device(): lax.all_to_all(send_grad.reshape(experts_here, CAP, -1), 'ex', split_axis...  64.3 us
    all_to_all x1, waiting for transfers between devices, per_device(): lax.all_to_all(group_terms.reshape(experts_here, CAP, -1), 'ex', split_ax...  59.1 us
    psum x1, blocking collectives, per_device(): prob_all = lax.psum(prob_grad, 'grp')  45.1 us
    all_gather x1, waiting for transfers between devices, per_device(): lax.all_gather(out_grad, 'grp', axis=1, tiled=True)  43.3 us
    unnamed x1, blocking collectives  37.7 us
    all_gather x1, waiting for transfers between devices, per_device(): lax.all_gather(tokens, 'grp', axis=1, tiled=True)  26.5 us
    all_to_all x1, waiting for transfers between devices, per_device(): lax.all_to_all(send_tok.reshape(experts_here, CAP, -1), 'ex', split_axis=...  14.6 us
    all_to_all x1, starting transfers between devices, per_device(): lax.all_to_all(send_gate, 'ex', split_axis=0, concat_axis=0, tiled=True)  10.5 us
  transfers between devices with their start and end apart: 8, of which 6 were waited for; matrix products, arithmetic and copies ran while one was open for 12% of the time, Pallas kernels for 0%

commit v1 on v0

v1 whole, which is shorter than its diff:
```python
import jax
import jax.numpy as jnp
from jax import lax
from jax.experimental import pallas as pl
from jax.experimental.pallas import tpu as pltpu
from jax.sharding import PartitionSpec as P

TOP = 4
CAP = 16
FEATS = 180
HIDDEN = 180
BLOCKS = 7
SEND = 384
HID = 192
NT = (((1,), (1,)), ((), ()))
TN = (((0,), (0,)), ((), ()))
F32 = jnp.float32
BF16 = jnp.bfloat16


def dispatch_kernel(ids_ref, gate_ref, feat_ref, rows_ref, sel_ref):
    experts = rows_ref.shape[0] // CAP
    count = ids_ref.shape[1]
    gates = gate_ref[...].astype(F32)
    expert = lax.broadcasted_iota(jnp.int32, (experts, count), 0)
    member = jnp.zeros((experts, count), F32)
    weight = jnp.zeros((experts, count), F32)
    for k in range(TOP):
        named = ids_ref[k : k + 1, :] == expert
        member = jnp.where(named, 1.0, member)
        weight = jnp.where(named, gates[k : k + 1, :], weight)
    earlier = lax.broadcasted_iota(jnp.int32, (count, count), 0) < lax.broadcasted_iota(
        jnp.int32, (count, count), 1
    )
    place = jnp.dot(
        member.astype(BF16), earlier.astype(F32).astype(BF16), preferred_element_type=F32
    )
    code = jnp.where(member > 0.0, place, -1.0)
    slot = lax.broadcasted_iota(jnp.int32, (experts, CAP, count), 1).astype(F32)
    picked = code[:, None, :] == slot
    select = jnp.where(picked, 1.0, 0.0).reshape(experts * CAP, count).astype(BF16)
    slot_weight = jnp.sum(
        jnp.where(picked, weight[:, None, :], 0.0).reshape(experts * CAP, count),
        axis=1,
        keepdims=True,
    )
    sel_ref[...] = select
    rows = lax.dot_general(select, feat_ref[...], NT, preferred_element_type=F32)
    lane = lax.broadcasted_iota(jnp.int32, rows.shape, 1)
    rows_ref[...] = jnp.where(lane == 2 * FEATS, slot_weight, rows).astype(BF16)


def expert_kernel(rows_ref, w1_ref, w3_ref, w2_ref, out_ref, acc_ref, grad_ref):
    step = pl.program_id(0)
    groups = pl.num_programs(0) - BLOCKS

    @pl.when(step == 0)
    def _():
        acc_ref[...] = jnp.zeros_like(acc_ref)

    @pl.when(step < groups)
    def _():
        rows = rows_ref[0]
        acc_ref[: 2 * HID, :] += lax.dot_general(
            w1_ref[0], rows[:, :256], NT, preferred_element_type=F32
        )
        acc_ref[2 * HID :, :] += lax.dot_general(
            w3_ref[0], rows[:, 128:], NT, preferred_element_type=F32
        )

    @pl.when(step == groups - 1)
    def _():
        hid = HIDDEN
        pre_gate = acc_ref[:HID, :]
        pre_up = acc_ref[HID : 2 * HID, :]
        back = acc_ref[2 * HID :, :]
        weight = acc_ref[2 * HID + hid : 2 * HID + hid + 1, :]
        sig = jax.nn.sigmoid(pre_gate)
        act = pre_gate * sig
        prob = jnp.sum(back * (act * pre_up), axis=0, keepdims=True)
        hid_grad = weight * back
        d_gate = hid_grad * pre_up * sig * (1.0 + pre_gate * (1.0 - sig))
        d_up = hid_grad * act
        high = prob.astype(BF16).astype(F32)
        row = lax.broadcasted_iota(jnp.int32, d_gate.shape, 0)
        d_gate = jnp.where(row < hid, d_gate, 0.0)
        d_gate = jnp.where(row == hid, high, d_gate)
        d_gate = jnp.where(row == hid + 1, prob - high, d_gate)
        grad_ref[:HID, :] = d_gate.astype(BF16)
        grad_ref[HID:, :] = jnp.where(row < hid, d_up, 0.0).astype(BF16)

    @pl.when(step >= groups)
    def _():
        out_ref[...] = jnp.dot(
            w2_ref[...], grad_ref[...], preferred_element_type=F32
        ).astype(BF16)


def combine_kernel(ret_ref, sel_ref, ids_ref, tok_ref, gate_ref):
    feats, count = tok_ref.shape
    slots = sel_ref.shape[0]
    experts = slots // CAP
    ret = ret_ref[...]
    total = lax.dot_general(ret, sel_ref[...], TN, preferred_element_type=F32)
    tok_ref[...] = total[:feats, :].astype(BF16)
    prob = ret[:, feats : feats + 1].astype(F32) + ret[:, feats + 1 : feats + 2].astype(F32)
    spread = (sel_ref[...].astype(F32) * prob).reshape(experts, CAP, count)
    per_expert = jnp.sum(spread, axis=1)
    expert = lax.broadcasted_iota(jnp.int32, (experts, count), 0)
    for k in range(TOP):
        named = ids_ref[k : k + 1, :] == expert
        gate_ref[k : k + 1, :] = jnp.sum(
            jnp.where(named, per_expert, 0.0), axis=0, keepdims=True
        )


def pack_first(w, groups, lead, rows):
    hid, width = w.shape
    feats = width // groups
    w = w.reshape(hid, groups, feats).transpose(1, 0, 2)
    return jnp.pad(w, ((0, 0), (0, rows - hid), (lead, 256 - feats - lead)))


def pack_second(w, groups):
    hid, width = w.shape
    feats = width // groups
    w = w.T.reshape(groups, feats, hid)
    return jnp.pad(w, ((0, 0), (0, 2), (0, HID - hid)))


def per_device(tokens, out_grad, expert_ids, gate_values, w_gate, w_up, w_down):
    experts = lax.axis_size("ex")
    groups = lax.axis_size("grp")
    slots = experts * CAP
    count, feats = tokens.shape
    hid = w_gate.shape[1]
    ids = expert_ids.T
    gates = gate_values.T
    feat = jnp.concatenate(
        [tokens.T, out_grad.T, jnp.zeros((SEND - 2 * feats, count), BF16)], axis=0
    )
    rows, select = pl.pallas_call(
        dispatch_kernel,
        out_shape=(
            jax.ShapeDtypeStruct((slots, SEND), BF16),
            jax.ShapeDtypeStruct((slots, count), BF16),
        ),
        name="dispatch",
    )(ids, gates, feat)
    rows = lax.all_to_all(
        rows.reshape(experts, CAP, SEND), "ex", split_axis=0, concat_axis=0, tiled=True
    ).reshape(slots, SEND)
    all_rows = lax.all_gather(rows, "grp")

    w1 = jnp.concatenate(
        [pack_first(w_gate[0], groups, 0, HID), pack_first(w_up[0], groups, 0, HID)], axis=1
    )
    w3 = pack_first(w_down[0], groups, 2 * feats - 128 - feats, HID)
    w3 = w3.at[0, hid, 2 * feats - 128].set(1.0)
    w2 = jnp.concatenate([pack_second(w_gate[0], groups), pack_second(w_up[0], groups)], axis=2)
    w2 = w2.at[:, feats, hid].set(1.0).at[:, feats + 1, hid + 1].set(1.0)
    chunk = feats + 2
    w2 = w2.reshape(groups * chunk, 2 * HID)
    block = groups * chunk // BLOCKS
    terms = pl.pallas_call(
        expert_kernel,
        grid=(groups + BLOCKS,),
        in_specs=[
            pl.BlockSpec((1, slots, SEND), lambda i: (jnp.minimum(i, groups - 1), 0, 0)),
            pl.BlockSpec((1, 2 * HID, 256), lambda i: (jnp.minimum(i, groups - 1), 0, 0)),
            pl.BlockSpec((1, HID, 256), lambda i: (jnp.minimum(i, groups - 1), 0, 0)),
            pl.BlockSpec((block, 2 * HID), lambda i: (jnp.maximum(i - groups, 0), 0)),
        ],
        out_specs=pl.BlockSpec((block, slots), lambda i: (jnp.maximum(i - groups, 0), 0)),
        out_shape=jax.ShapeDtypeStruct((groups * chunk, slots), BF16),
        scratch_shapes=[
            pltpu.VMEM((3 * HID, slots), F32),
            pltpu.VMEM((2 * HID, slots), BF16),
        ],
        compiler_params=pltpu.CompilerParams(vmem_limit_bytes=24 * 1024 * 1024),
        name="expert",
    )(all_rows, w1, w3, w2)

    part = lax.psum_scatter(terms, "grp", scatter_dimension=0, tiled=True)
    ret = lax.all_to_all(
        part.T.reshape(experts, CAP, chunk), "ex", split_axis=0, concat_axis=0, tiled=True
    ).reshape(slots, chunk)
    tok, gate = pl.pallas_call(
        combine_kernel,
        out_shape=(
            jax.ShapeDtypeStruct((feats, count), BF16),
            jax.ShapeDtypeStruct((TOP, count), F32),
        ),
        name="combine",
    )(ret, select, ids)
    return tok.T, gate.T


def solution(mesh):
    return jax.shard_map(
        per_device,
        mesh=mesh,
        in_specs=(
            P("ex", "grp"),
            P("ex", "grp"),
            P("ex", None),
            P("ex", None),
            P("ex", "grp", None),
            P("ex", "grp", None),
            P("ex", "grp", None),
        ),
        out_specs=(P("ex", "grp"), P("ex", None)),
        check_vma=False,
    )
```

time: 416 us -> 170 us (0.41)
  waiting for transfers between devices: 210 us -> 9.94 us
  starting transfers between devices: 47.2 us -> 2.13 us
  matrix products: 24.5 us -> 0 us
  local copies, waits for them, and re-layouts: 24.1 us -> 47.2 us
  Pallas kernels: 0 us -> 13.3 us
  blocking collectives: 82.8 us -> 75.5 us
  other arithmetic: 10.9 us -> 5.19 us
    all_to_all x5 -> x0, waiting for transfers between devices: 138 us -> none  [the longest x1 64.3 us: per_device(): lax.all_to_all(send_grad.reshape(experts_here, CAP, -1), 'ex', split_axis...]
    all_gather x2 -> x1, waiting for transfers between devices: 69.8 us -> 9.37 us  [per_device(): all_rows = lax.all_gather(rows, 'grp')]
    psum x1 -> x0, blocking collectives: 45.1 us -> none  [per_device(): prob_all = lax.psum(prob_grad, 'grp')]
    all_to_all x0 -> x2, blocking collectives: none -> 44 us  [the longest x1 24.4 us: per_device(): lax.all_to_all(rows.reshape(experts, CAP, SEND), 'ex', split_axis=0, conc...]
    all_to_all x5 -> x0, starting transfers between devices: 43.6 us -> none  [the longest x1 10.5 us: per_device(): lax.all_to_all(send_gate, 'ex', split_axis=0, concat_axis=0, tiled=True)]
    dot_general x10 -> x0, matrix products: 24.5 us -> none  [the longest x3 9.37 us: contract_last(): lax.dot_general(left, right, (((1,), (1,)), ((), ())), preferred_element_...]
    another operation x2 -> x5, local copies, waits for them, and re-layouts: 0.08 us -> 15.7 us  [the longest x4 15.7 us: pack_first(): w = w.reshape(hid, groups, feats).transpose(1, 0, 2)]
    reshape x1 -> x5, local copies, waits for them, and re-layouts: 0.08 us -> 15.3 us  [the longest x4 13.1 us: pack_second(): w = w.T.reshape(groups, feats, hid)]
  transfers between devices with their start and end apart: 8 -> 2, of which waited for: 6 -> 2; matrix products, arithmetic and copies ran while one was open for 12% -> 25% of each run, Pallas kernels for 0% -> 0%
where the time goes in v1:
time: 170 us; the launch traced here: 168 us
  blocking collectives  75.5 us (44%)
  local copies, waits for them, and re-layouts  47.2 us (28%)
  between operations  14.9 us (9%)
  Pallas kernels  13.3 us (8%)
  waiting for transfers between devices  9.94 us (6%)
  other arithmetic  5.19 us (3%)
  starting transfers between devices  2.13 us (1%)
    unnamed x1, blocking collectives  31.5 us
    all_to_all x1, blocking collectives, per_device(): lax.all_to_all(rows.reshape(experts, CAP, SEND), 'ex', split_axis=0, conc...  24.4 us
    all_to_all x1, blocking collectives, per_device(): lax.all_to_all(part.T.reshape(experts, CAP, chunk), 'ex', split_axis=0, c...  19.6 us
    another operation x4, local copies, waits for them, and re-layouts, pack_first(): w = w.reshape(hid, groups, feats).transpose(1, 0, 2)  15.7 us
    reshape x4, local copies, waits for them, and re-layouts, pack_second(): w = w.T.reshape(groups, feats, hid)  13.1 us
    unnamed x22, local copies, waits for them, and re-layouts  9.67 us
    all_gather x1, waiting for transfers between devices, per_device(): all_rows = lax.all_gather(rows, 'grp')  9.37 us
    pallas_call x1, Pallas kernels, per_device(): pl.pallas_call(expert_kernel, grid=(groups + BLOCKS,), in_specs=[pl.Block...  9.09 us
  transfers between devices with their start and end apart: 2, of which 2 were waited for; matrix products, arithmetic and copies ran while one was open for 25% of the time, Pallas kernels for 0%

profile of v1, /device:TPU:1, one launch (start us, length us, event | category | flops | bytes accessed | tf_op | source)
XLA Modules:
  0.0 168.1 jit_solution(11876849430983537629)
XLA Ops:
  7.2 0.0 copy-start.6
  7.2 0.0 all-gather.2.cloned.1.call-start
  7.2 0.1 pad.39.clone
  7.3 1.8 %maximum_maximum_fusion.feat_ref = bf16[384,256]{1,0:T(8,128)(2,1)} fusion(bf16[180,256]{1,0:T(8,128)(2,1)} %bitcast.39, bf16[180,256]{1,0:T(8,128)(2,1)} %bitcast.40, bf16[384]{0:T(512)(128)(2,1)S(1)} %pad.39.clone), kind=kLoop, calls=%fused_computation.13 | loop fusion | flops 589824 | bytes 381696 | tf_op jit(solution)/shard_map/concatenate | solution.py:139
  9.1 2.2 %dispatch.1 = (bf16[512,384]{1,0:T(8,128)(2,1)}, bf16[512,256]{1,0:T(8,128)(2,1)}) custom-call(s32[4,256]{1,0:T(4,128)} %bitcast.41, bf16[4,256]{1,0:T(4,128)(2,1)} %bitcast.43, bf16[384,256]{1,0:T(8,128)(2,1)} %maximum_maximum_fusion.feat_ref), custom_call_target="tpu_custom_call" | custom-call | tf_op jit(solution)/shard_map/dispatch/pallas_call | solution.py:142
  11.3 24.4 %all_to_all.10 = bf16[32,16,384]{2,1,0:T(8,128)(2,1)} all-to-all(bf16[32,16,384]{2,1,0:T(8,128)(2,1)} %bitcast.38), channel_id=1, replica_groups=mesh['grp'=16,'ex'=32] {'ex'}, dimensions={0} | all-to-all | bytes 786432 | tf_op jit(solution)/shard_map/all_to_all | solution.py:150
  35.7 0.0 all-gather.2.cloned.1.call-update
  35.7 0.0 copy-done.6
  35.7 5.5 %reshape_squeeze.9 = bf16[180,16,180]{2,1,0:T(8,128)(2,1)} reshape(bf16[1,180,2880]{2,1,0:T(8,128)(2,1)S(1)} %copy-done.6) | data formatting | bytes 2073600 | tf_op jit(solution)/shard_map/reshape;squeeze | solution.py:120
  41.2 4.3 %reshape.106 = bf16[16,180,180]{1,0,2:T(8,128)(2,1)S(1)} reshape(bf16[2880,180]{0,1:T(8,128)(2,1)S(1)} %bitcast.33) | data formatting | bytes 2073600 | tf_op jit(solution)/shard_map/reshape | solution.py:127
  45.5 0.0 copy-start.7
  45.5 2.2 %copy.21 = bf16[16,180,180]{2,1,0:T(8,128)(2,1)} copy(bf16[16,180,180]{1,0,2:T(8,128)(2,1)S(1)} %reshape.106) | data formatting | bytes 2073600 | tf_op jit(solution)/shard_map/reshape | solution.py:127
  47.7 0.0 copy-done.7
  47.7 5.4 %reshape_squeeze.10 = bf16[180,16,180]{2,1,0:T(8,128)(2,1)} reshape(bf16[1,180,2880]{2,1,0:T(8,128)(2,1)S(1)} %copy-done.7) | data formatting | bytes 2073600 | tf_op jit(solution)/shard_map/reshape;squeeze | solution.py:120
  53.2 4.3 %reshape.107 = bf16[16,180,180]{1,0,2:T(8,128)(2,1)S(1)} reshape(bf16[2880,180]{0,1:T(8,128)(2,1)S(1)} %bitcast.34) | data formatting | bytes 2073600 | tf_op jit(solution)/shard_map/reshape | solution.py:127
  57.5 2.3 %copy.22 = bf16[16,180,180]{2,1,0:T(8,128)(2,1)} copy(bf16[16,180,180]{1,0,2:T(8,128)(2,1)S(1)} %reshape.107) | data formatting | bytes 2073600 | tf_op jit(solution)/shard_map/reshape | solution.py:127
  59.8 2.8 %fusion.6 = bf16[16,182,384]{2,1,0:T(8,128)(2,1)S(1)} fusion(bf16[16,180,180]{2,1,0:T(8,128)(2,1)} %copy.22, bf16[16,180,180]{2,1,0:T(8,128)(2,1)} %copy.21), kind=kLoop, calls=%fused_computation.9 | loop fusion | flops 8945664 | bytes 4310016 | tf_op jit(solution)/shard_map/concatenate | solution.py:160
  62.6 1.2 scatter.11
  63.8 0.0 copy-start.8
  63.8 1.2 scatter.14
  65.1 2.2 %reshape.108.w2_ref = bf16[2912,384]{1,0:T(8,128)(2,1)} reshape(bf16[16,182,384]{2,1,0:T(8,128)(2,1)S(1)} %scatter.14) | data formatting | bytes 4472832 | tf_op jit(solution)/shard_map/reshape | solution.py:163
  67.3 0.0 copy-done.8
  67.3 4.3 %reshape_squeeze.11 = bf16[180,16,180]{2,1,0:T(8,128)(2,1)S(1)} reshape(bf16[1,180,2880]{2,1,0:T(8,128)(2,1)S(1)} %copy-done.8) | data formatting | bytes 2073600 | tf_op jit(solution)/shard_map/reshape;squeeze | solution.py:120
  71.6 0.5 copy.27
  72.1 0.0 copy-start.5
  72.1 0.7 pad.30
  72.8 0.1 scatter.10.w3_ref
  72.9 0.6 copy-done.5
  73.5 0.0 copy-start.3
  73.5 3.0 %copy_bitcast_fusion.1 = (bf16[16,180,180]{2,1,0:T(8,128)(2,1)S(1)}, bf16[16,180,180]{2,1,0:T(8,128)(2,1)S(1)}) fusion(bf16[180,16,180]{2,1,0:T(8,128)(2,1)} %reshape_squeeze.10, bf16[180,16,180]{2,1,0:T(8,128)(2,1)S(1)} %copy-done.5), kind=kLoop, calls=%fused_computation.11 | loop fusion | bytes 4147200 | tf_op jit(solution)/shard_map/transpose | solution.py:120
  76.6 0.0 copy-done.3
  76.6 0.6 fusion.5.w1_ref
  77.2 9.4 %all-gather.2.cloned.1.call-done.rows_ref = bf16[16,512,384]{2,1,0:T(8,128)(2,1)} async-done(((bf16[1,512,384]{2,1,0:T(8,128)(2,1)}), bf16[16,512,384]{2,1,0:T(8,128)(2,1)}) %all-gather.2.cloned.1.call-update) | async-done | bytes 6291472 | tf_op jit(solution)/shard_map/all_gather | solution.py:153
  86.5 0.0 copy-start.1
  86.5 1.6 copy-done.1
  88.2 0.0 copy-start.2
  88.2 2.8 %copy-done.2 = bf16[16,512,384]{2,1,0:T(8,128)(2,1)S(1)} copy-done((bf16[16,512,384]{2,1,0:T(8,128)(2,1)S(1)}, bf16[16,512,384]{2,1,0:T(8,128)(2,1)}, u32[]{:S(2)}) %copy-start.2) | copy-done | bytes 6291480
  90.9 0.0 copy-start.4
  90.9 1.4 copy-done.4
  92.3 9.1 %expert.1 = bf16[2912,512]{1,0:T(8,128)(2,1)S(1)} custom-call(bf16[16,512,384]{2,1,0:T(8,128)(2,1)S(1)} %copy-done.2, bf16[16,384,256]{2,1,0:T(8,128)(2,1)S(1)} %fusion.5.w1_ref, bf16[16,192,256]{2,1,0:T(8,128)(2,1)S(1)} %copy-done.4, bf16[2912,384]{1,0:T(8,128)(2,1)S(1)} %copy-done.1), custom_call_target="tpu_custom_call" | custom-call | tf_op jit(solution)/shard_map/expert/pallas_call | solution.py:165
  101.4 0.0 copy-start
  101.4 1.6 copy-done
  103.0 31.5 %fusion = bf16[184,512]{1,0:T(8,128)(2,1)S(1)} fusion(bf16[2912,512]{1,0:T(8,128)(2,1)} %copy-done), kind=kCustom, calls=%all-reduce-scatter | all-reduce-scatter fusion | flops 1507329 | bytes 3172352
  134.6 2.1 %collective-permute-start = (bf16[30,512]{1,0:T(8,128)(2,1)S(1)}, bf16[30,512]{1,0:T(8,128)(2,1)S(1)}, u32[]{:S(2)}, u32[]{:S(2)}) collective-permute-start(bf16[30,512]{1,0:T(8,128)(2,1)S(1)} %slice.66), channel_id=1, source_target_pairs={{0,32},{32,64},{64,96},{96,128},{128,160},{160,192},{192,224},{224... | collective-permute-start | bytes 92168
  136.7 1.3 dynamic-slice.25
  138.6 0.6 collective-permute-done
  139.2 0.3 concatenate.19
  139.5 0.1 constant_dynamic-slice_fusion
  139.5 0.1 copy.23
  139.7 19.6 %all_to_all.11 = bf16[32,16,182]{2,1,0:T(8,128)(2,1)} all-to-all(bf16[32,16,182]{2,1,0:T(8,128)(2,1)S(1)} %bitcast.36), channel_id=1, replica_groups=mesh['grp'=16,'ex'=32] {'ex'}, dimensions={0} | all-to-all | bytes 372736 | tf_op jit(solution)/shard_map/all_to_all | solution.py:185
  159.3 2.0 %combine.1 = (bf16[180,256]{1,0:T(8,128)(2,1)}, f32[4,256]{1,0:T(4,128)}) custom-call(bf16[512,182]{1,0:T(8,128)(2,1)} %bitcast.37, bf16[512,256]{1,0:T(8,128)(2,1)} %get-tuple-element.43.sel_ref, s32[4,256]{1,0:T(4,128)} %bitcast.42), custom_call_target="tpu_custom_call" | custom-call | tf_op jit(solution)/shard_map/combine/pallas_call | solution.py:188
  (3 shorter events, 0.0 us)
Async XLA Ops:
  7.2 28.5 %copy-start.6 = (bf16[1,180,2880]{2,1,0:T(8,128)(2,1)S(1)}, bf16[1,180,2880]{2,1,0:T(8,128)(2,1)}, u32[]{:S(2)}) copy-start(bf16[1,180,2880]{2,1,0:T(8,128)(2,1)} %param.17) | copy-start | bytes 3110404
  7.2 79.3 %all-gather.2.cloned.1.call-start = ((), (), s32[]{:S(2)}) async-start(), calls=%async_computation.2 | async-start | bytes 6684672 | tf_op jit(solution)/shard_map/all_gather | solution.py:153
  45.5 2.2 %copy-start.7 = (bf16[1,180,2880]{2,1,0:T(8,128)(2,1)S(1)}, bf16[1,180,2880]{2,1,0:T(8,128)(2,1)}, u32[]{:S(2)}) copy-start(bf16[1,180,2880]{2,1,0:T(8,128)(2,1)} %param.18) | copy-start | bytes 3110404
  63.8 3.5 %copy-start.8 = (bf16[1,180,2880]{2,1,0:T(8,128)(2,1)S(1)}, bf16[1,180,2880]{2,1,0:T(8,128)(2,1)}, u32[]{:S(2)}) copy-start(bf16[1,180,2880]{2,1,0:T(8,128)(2,1)} %param.19) | copy-start | bytes 3110404
  72.1 1.4 copy-start.5
  73.5 3.0 %copy-start.3 = (bf16[16,192,256]{2,1,0:T(8,128)(2,1)}, bf16[16,192,256]{2,1,0:T(8,128)(2,1)S(1)}, u32[]{:S(2)}) copy-start(bf16[16,192,256]{2,1,0:T(8,128)(2,1)S(1)} %scatter.10.w3_ref) | copy-start | bytes 4718596
  86.5 1.6 copy-start.1
  88.2 2.8 %copy-start.2 = (bf16[16,512,384]{2,1,0:T(8,128)(2,1)S(1)}, bf16[16,512,384]{2,1,0:T(8,128)(2,1)}, u32[]{:S(2)}) copy-start(bf16[16,512,384]{2,1,0:T(8,128)(2,1)} %all-gather.2.cloned.1.call-done.rows_ref) | copy-start | bytes 18874372
  90.9 1.4 copy-start.4
  101.4 1.6 copy-start
  134.6 4.6 %collective-permute-start = (bf16[30,512]{1,0:T(8,128)(2,1)S(1)}, bf16[30,512]{1,0:T(8,128)(2,1)S(1)}, u32[]{:S(2)}, u32[]{:S(2)}) collective-permute-start(bf16[30,512]{1,0:T(8,128)(2,1)S(1)} %slice.66), channel_id=1, source_target_pairs={{0,32},{32,64},{64,96},{96,128},{128,160},{160,192},{192,224},{224... | collective-permute-start | bytes 92168
Sparse Core Ops, SparseCore 0:
  35.8 50.6 all-gather.1

commit v2 on v0

v2 whole, which is shorter than its diff:
```python
import jax
import jax.numpy as jnp
from jax import lax
from jax.experimental import pallas as pl
from jax.experimental.pallas import tpu as pltpu
from jax.sharding import PartitionSpec as P

TOP = 4
CAP = 16
HALF = CAP // 2
FEATS = 180
HIDDEN = 180
HID = 192
WIDE = 384
CHIP = 2 * FEATS
NT = (((1,), (1,)), ((), ()))
TN = (((0,), (0,)), ((), ()))
F32 = jnp.float32
BF16 = jnp.bfloat16


def iota(shape, dim):
    return lax.broadcasted_iota(jnp.int32, shape, dim)


def dispatch_kernel(core_ref, ids_ref, gate_ref, own_ref, peer_ref, rows_ref, sel_ref, feat_ref):
    slots, count = sel_ref.shape
    experts = slots // HALF
    core = core_ref[0]
    gates = gate_ref[...].astype(F32)
    expert = iota((experts, count), 0)
    member = jnp.zeros((experts, count), F32)
    weight = jnp.zeros((experts, count), F32)
    for k in range(TOP):
        named = ids_ref[k : k + 1, :] == expert
        member = jnp.where(named, 1.0, member)
        weight = jnp.where(named, gates[k : k + 1, :], weight)
    earlier = jnp.where(iota((count, count), 0) < iota((count, count), 1), 1.0, 0.0)
    place = jnp.dot(member.astype(BF16), earlier.astype(BF16), preferred_element_type=F32)
    code = jnp.where(member > 0.0, place - (HALF * core).astype(F32), -1.0)
    picked = code[:, None, :] == iota((experts, HALF, count), 1).astype(F32)
    select = jnp.where(picked, 1.0, 0.0).reshape(slots, count).astype(BF16)
    slot_weight = jnp.sum(
        jnp.where(picked, weight[:, None, :], 0.0).reshape(slots, count), axis=1, keepdims=True
    )
    sel_ref[...] = select
    feat_ref[...] = jnp.zeros_like(feat_ref)
    for part in range(2):
        own = own_ref[part].astype(F32)
        peer = peer_ref[part].astype(F32)
        base = part * WIDE
        feat_ref[base : base + FEATS, :] = jnp.where(core == 0, own, peer)
        feat_ref[base + FEATS : base + CHIP, :] = jnp.where(core == 0, peer, own)
    rows = lax.dot_general(
        select, feat_ref[...].astype(BF16), NT, preferred_element_type=F32
    )
    rows_ref[...] = jnp.where(iota(rows.shape, 1) == CHIP, slot_weight, rows).astype(BF16)


def pack_kernel(gate_ref, up_ref, down_ref, out_ref):
    chips = out_ref.shape[0]
    spare = HID - HIDDEN
    spot = iota((spare, WIDE), 1) == iota((spare, WIDE), 0) + CHIP
    mark = jnp.where(jnp.logical_and(spot, iota((spare, WIDE), 0) < 2), 1.0, 0.0)
    lane = iota((HID, WIDE), 1)
    for chip in range(chips):
        start = chip * CHIP
        low = start // 128 * 128
        high = min(low + 512, gate_ref.shape[1])
        for part, ref in enumerate((gate_ref, up_ref, down_ref)):
            w = ref[:, low:high].astype(F32)
            w = w[:, start - low : start - low + CHIP]
            w = jnp.concatenate([w, jnp.zeros((HIDDEN, WIDE - CHIP), F32)], axis=1)
            tail = mark if part == 0 else jnp.zeros_like(mark)
            w = jnp.concatenate([w, tail], axis=0)
            out_ref[chip, part * HID : (part + 1) * HID, :] = w.astype(BF16)


def expert_kernel(order_ref, *refs):
    blocks, last = refs[:7], refs[7:9]
    own_w, peer_w, out_ref, own_acc, peer_acc, own_d, peer_d, terms = refs[9:]
    step = pl.program_id(0)
    chips = pl.num_programs(0) // 2

    def add(rows):
        for w_ref, acc in ((own_w, own_acc), (peer_w, peer_acc)):
            acc[: 2 * HID, :] += lax.dot_general(
                w_ref[0, : 2 * HID, :], rows[:, :WIDE], NT, preferred_element_type=F32
            )
            acc[2 * HID :, :] += lax.dot_general(
                w_ref[0, 2 * HID :, :], rows[:, WIDE:], NT, preferred_element_type=F32
            )

    @pl.when(step == 0)
    def _():
        own_acc[...] = jnp.zeros_like(own_acc)
        peer_acc[...] = jnp.zeros_like(peer_acc)

    for k in range(7):

        @pl.when(step == k)
        def _(k=k):
            add(blocks[k][...])

    @pl.when(step == 7)
    def _():
        add(jnp.concatenate([last[0][...], last[1][...]], axis=0))
        probs = []
        for acc, grad in ((own_acc, own_d), (peer_acc, peer_d)):
            pre_gate = acc[:HID, :]
            pre_up = acc[HID : 2 * HID, :]
            back = acc[2 * HID :, :]
            weight = acc[HIDDEN : HIDDEN + 1, :] * (1.0 / chips)
            sig = jax.nn.sigmoid(pre_gate)
            act = pre_gate * sig
            live = iota(act.shape, 0) < HIDDEN
            probs.append(
                jnp.sum(jnp.where(live, back * (act * pre_up), 0.0), axis=0, keepdims=True)
            )
            hid_grad = weight * back
            d_gate = hid_grad * pre_up * sig * (1.0 + pre_gate * (1.0 - sig))
            d_up = hid_grad * act
            grad[:HID, :] = jnp.where(live, d_gate, 0.0).astype(BF16)
            grad[HID:, :] = jnp.where(live, d_up, 0.0).astype(BF16)
        prob = probs[0] + probs[1]
        high = prob.astype(BF16).astype(F32)
        spare = iota((16, prob.shape[1]), 0)
        tail = own_d[HID - 16 : HID, :].astype(F32)
        tail = jnp.where(spare == HIDDEN - HID + 16, high, tail)
        tail = jnp.where(spare == HIDDEN - HID + 17, prob - high, tail)
        own_d[HID - 16 : HID, :] = tail.astype(BF16)

    chunk = CHIP + 2
    for k in range(8):

        @pl.when(step == 8 + k)
        def _(k=k):
            value = lax.dot_general(
                own_w[0, : 2 * HID, :], own_d[...], TN, preferred_element_type=F32
            ) + lax.dot_general(
                peer_w[0, : 2 * HID, :], peer_d[...], TN, preferred_element_type=F32
            )
            terms[k * chunk : (k + 1) * chunk, :] = value[:chunk, :]

    @pl.when(step == 15)
    def _():
        out_ref[...] = terms[...].astype(BF16)


def combine_kernel(core_ref, ret_ref, sel_ref, ids_ref, keep_ref, send_ref):
    slots, count = sel_ref.shape
    experts = slots // HALF
    core = core_ref[0]
    ret = ret_ref[...]
    select = sel_ref[...]
    total = lax.dot_general(ret, select, TN, preferred_element_type=F32)
    first, second = total[:FEATS, :], total[FEATS:CHIP, :]
    keep_ref[:FEATS, :] = jnp.where(core == 0, first, second)
    send_ref[:FEATS, :] = jnp.where(core == 0, second, first)
    prob = ret[:, CHIP : CHIP + 1].astype(F32) + ret[:, CHIP + 1 : CHIP + 2].astype(F32)
    per_expert = jnp.sum((select.astype(F32) * prob).reshape(experts, HALF, count), axis=1)
    expert = iota((experts, count), 0)
    for k in range(TOP):
        named = ids_ref[k : k + 1, :] == expert
        value = jnp.sum(jnp.where(named, per_expert, 0.0), axis=0, keepdims=True)
        keep_ref[FEATS + k : FEATS + k + 1, :] = value
        send_ref[FEATS + k : FEATS + k + 1, :] = value


VMEM = pl.BlockSpec(memory_space=pltpu.VMEM)
SMEM = pl.BlockSpec(memory_space=pltpu.SMEM)


def per_device(tokens, out_grad, expert_ids, gate_values, w_gate, w_up, w_down):
    experts = lax.axis_size("ex")
    groups = lax.axis_size("grp")
    chips = groups // 2
    slots = experts * HALF
    count = tokens.shape[0]
    me = lax.axis_index("grp")
    core, z = me % 2, me // 2
    swap = [(i, i ^ 1) for i in range(groups)]
    up = [(i, (i + 2 - 4 * (i % 2)) % groups) for i in range(groups)]
    down = [(t, s) for s, t in up]
    core_arg = core.astype(jnp.int32).reshape(1)
    ids = expert_ids.T
    gates = gate_values.T

    own = jnp.stack([tokens.T, out_grad.T])
    peer = lax.ppermute(own, "grp", swap)
    rows, select = pl.pallas_call(
        dispatch_kernel,
        in_specs=[SMEM] + [VMEM] * 4,
        out_shape=(
            jax.ShapeDtypeStruct((slots, 2 * WIDE), BF16),
            jax.ShapeDtypeStruct((slots, count), BF16),
        ),
        scratch_shapes=[pltpu.VMEM((2 * WIDE, count), F32)],
        name="dispatch",
    )(core_arg, ids, gates, own, peer)

    own_w = pl.pallas_call(
        pack_kernel,
        out_shape=jax.ShapeDtypeStruct((chips, 3 * HID, WIDE), BF16),
        compiler_params=pltpu.CompilerParams(vmem_limit_bytes=32 * 1024 * 1024),
        name="pack",
    )(w_gate[0], w_up[0], w_down[0])
    peer_w = lax.ppermute(own_w, "grp", swap)

    rows = lax.all_to_all(
        rows.reshape(experts, HALF, 2 * WIDE), "ex", split_axis=0, concat_axis=0, tiled=True
    ).reshape(slots, 2 * WIDE)
    blocks, a, b = [rows], rows, rows
    for _ in range(3):
        a = lax.ppermute(a, "grp", up)
        b = lax.ppermute(b, "grp", down)
        blocks += [a, b]
    a = lax.ppermute(a[: slots // 2], "grp", up)
    b = lax.ppermute(b[slots // 2 :], "grp", down)
    turn = 1 - 2 * core
    order = jnp.stack(
        [(z + d * turn) % chips for d in (0, -1, 1, -2, 2, -3, 3, 4)]
    ).astype(jnp.int32)

    chunk = CHIP + 2
    pick = lambda i, order: (jnp.where(i < chips, order[jnp.minimum(i, chips - 1)], i - chips), 0, 0)
    whole = lambda s: pl.BlockSpec(s, lambda i, order: (0, 0))
    terms = pl.pallas_call(
        expert_kernel,
        grid_spec=pltpu.PrefetchScalarGridSpec(
            num_scalar_prefetch=1,
            grid=(2 * chips,),
            in_specs=[whole((slots, 2 * WIDE))] * 7
            + [whole((slots // 2, 2 * WIDE))] * 2
            + [pl.BlockSpec((1, 3 * HID, WIDE), pick)] * 2,
            out_specs=whole((chips * chunk, slots)),
            scratch_shapes=[
                pltpu.VMEM((3 * HID, slots), F32),
                pltpu.VMEM((3 * HID, slots), F32),
                pltpu.VMEM((2 * HID, slots), BF16),
                pltpu.VMEM((2 * HID, slots), BF16),
                pltpu.VMEM((chips * chunk, slots), F32),
            ],
        ),
        out_shape=jax.ShapeDtypeStruct((chips * chunk, slots), BF16),
        compiler_params=pltpu.CompilerParams(vmem_limit_bytes=32 * 1024 * 1024),
        name="expert",
    )(order, *blocks, a, b, own_w, peer_w)

    same_core = [list(range(c, groups, 2)) for c in range(2)]
    part = lax.psum_scatter(
        terms, "grp", scatter_dimension=0, axis_index_groups=same_core, tiled=True
    )
    ret = lax.all_to_all(
        part.T.reshape(experts, HALF, chunk), "ex", split_axis=0, concat_axis=0, tiled=True
    ).reshape(slots, chunk)
    keep, send = pl.pallas_call(
        combine_kernel,
        in_specs=[SMEM] + [VMEM] * 3,
        out_shape=(jax.ShapeDtypeStruct((FEATS + TOP, count), F32),) * 2,
        name="combine",
    )(core_arg, ret, select, ids)
    total = keep + lax.ppermute(send, "grp", swap)
    return total[:FEATS].astype(BF16).T, total[FEATS:].T


def solution(mesh):
    return jax.shard_map(
        per_device,
        mesh=mesh,
        in_specs=(
            P("ex", "grp"),
            P("ex", "grp"),
            P("ex", None),
            P("ex", None),
            P("ex", "grp", None),
            P("ex", "grp", None),
            P("ex", "grp", None),
        ),
        out_specs=(P("ex", "grp"), P("ex", None)),
        check_vma=False,
    )
```

time: 416 us -> 181 us (0.44)
  waiting for transfers between devices: 210 us -> 25.6 us
  blocking collectives: 82.8 us -> 51.9 us
  matrix products: 24.5 us -> 0 us
  Pallas kernels: 0 us -> 19.4 us
  between operations: 14.9 us -> 1.69 us
  starting transfers between devices: 47.2 us -> 58.4 us
  other arithmetic: 10.9 us -> 1.65 us
    all_to_all x5 -> x0, waiting for transfers between devices: 138 us -> none  [the longest x1 64.3 us: per_device(): lax.all_to_all(send_grad.reshape(experts_here, CAP, -1), 'ex', split_axis...]
    all_gather x2 -> x0, waiting for transfers between devices: 69.8 us -> none  [the longest x1 43.3 us: per_device(): lax.all_gather(out_grad, 'grp', axis=1, tiled=True)]
    ppermute x0 -> x11, starting transfers between devices: none -> 55.9 us  [the longest x3 20.5 us: per_device(): a = lax.ppermute(a, 'grp', up)]
    psum x1 -> x0, blocking collectives: 45.1 us -> none  [per_device(): prob_all = lax.psum(prob_grad, 'grp')]
    all_to_all x5 -> x0, starting transfers between devices: 43.6 us -> none  [the longest x1 10.5 us: per_device(): lax.all_to_all(send_gate, 'ex', split_axis=0, concat_axis=0, tiled=True)]
    all_to_all x0 -> x2, blocking collectives: none -> 32.4 us  [the longest x1 18.2 us: per_device(): lax.all_to_all(rows.reshape(experts, HALF, 2 * WIDE), 'ex', split_axis=0,...]
    ppermute x0 -> x11, waiting for transfers between devices: none -> 25.6 us  [the longest x3 11.2 us: per_device(): b = lax.ppermute(b, 'grp', down)]
    dot_general x10 -> x0, matrix products: 24.5 us -> none  [the longest x3 9.37 us: contract_last(): lax.dot_general(left, right, (((1,), (1,)), ((), ())), preferred_element_...]
  transfers between devices with their start and end apart: 8 -> 12, of which waited for: 6 -> 8; matrix products, arithmetic and copies ran while one was open for 12% -> 2% of each run, Pallas kernels for 0% -> 1%
where the time goes in v2:
time: 181 us; the launch traced here: 180 us
  starting transfers between devices  58.4 us (32%)
  blocking collectives  51.9 us (29%)
  waiting for transfers between devices  25.6 us (14%)
  local copies, waits for them, and re-layouts  21.1 us (12%)
  Pallas kernels  19.4 us (11%)
    ppermute x3, starting transfers between devices, per_device(): a = lax.ppermute(a, 'grp', up)  20.5 us
    unnamed x1, blocking collectives  19.5 us
    unnamed x44, local copies, waits for them, and re-layouts  18.3 us
    all_to_all x1, blocking collectives, per_device(): lax.all_to_all(rows.reshape(experts, HALF, 2 * WIDE), 'ex', split_axis=0,...  18.2 us
    all_to_all x1, blocking collectives, per_device(): lax.all_to_all(part.T.reshape(experts, HALF, chunk), 'ex', split_axis=0,...  14.2 us
    pallas_call x1, Pallas kernels, per_device(): pl.pallas_call(expert_kernel, grid_spec=pltpu.PrefetchScalarGridSpec(num_...  14 us
    ppermute x1, starting transfers between devices, per_device(): total = keep + lax.ppermute(send, 'grp', swap)  12 us
    ppermute x3, waiting for transfers between devices, per_device(): b = lax.ppermute(b, 'grp', down)  11.2 us
  transfers between devices with their start and end apart: 12, of which 8 were waited for; matrix products, arithmetic and copies ran while one was open for 2% of the time, Pallas kernels for 1%

profile of v2, /device:TPU:1, one launch (start us, length us, event | category | flops | bytes accessed | tf_op | source)
XLA Modules:
  0.0 179.8 jit_solution(5534732064813263817)
XLA Ops:
  0.6 0.0 copy-start.3
  0.6 1.2 copy-done.3
  1.9 1.2 copy-done.4
  3.1 1.2 copy-done.5
  4.3 1.1 pack.1.refs_9_
  5.4 8.8 %collective-permute-start.9 = (bf16[8,576,384]{2,1,0:T(8,128)(2,1)S(1)}, bf16[8,576,384]{2,1,0:T(8,128)(2,1)}, u32[]{:S(2)}, u32[]{:S(2)}) collective-permute-start(bf16[8,576,384]{2,1,0:T(8,128)(2,1)S(1)} %pack.1.refs_9_), channel_id=1, source_target_pairs={{0,32},{32,0},{64,96},{96,64},{128,160},{160,128},{192,224},{224,1... | collective-permute-start | bytes 10616840 | tf_op jit(solution)/shard_map/ppermute | solution.py:208
  14.2 0.0 copy-done.18
  14.2 0.0 copy-done.19
  14.2 0.7 pad_maximum_fusion.own_ref
  14.9 1.9 %collective-permute-start = (bf16[2,180,256]{2,1,0:T(8,128)(2,1)}, bf16[2,180,256]{2,1,0:T(8,128)(2,1)}, u32[]{:S(2)}, u32[]{:S(2)}) collective-permute-start(bf16[2,180,256]{2,1,0:T(8,128)(2,1)} %pad_maximum_fusion.own_ref), channel_id=1, source_target_pairs={{0,32},{32,0},{64,96},{96,64},{128,160},{160,128},{192,224},{224,1... | collective-permute-start | bytes 552968 | tf_op jit(solution)/shard_map/ppermute | solution.py:190
  16.9 3.8 %collective-permute-done.peer_ref = bf16[2,180,256]{2,1,0:T(8,128)(2,1)} collective-permute-done((bf16[2,180,256]{2,1,0:T(8,128)(2,1)}, bf16[2,180,256]{2,1,0:T(8,128)(2,1)}, u32[]{:S(2)}, u32[]{:S(2)}) %collective-permute-start) | collective-permute-done | bytes 184352 | tf_op jit(solution)/shard_map/ppermute | solution.py:190
  20.7 2.2 %dispatch.1 = (bf16[256,768]{1,0:T(8,128)(2,1)}, bf16[256,256]{1,0:T(8,128)(2,1)}) custom-call(s32[1]{0:T(128)} %bitcast.core_ref, s32[4,256]{1,0:T(4,128)} %bitcast.44, bf16[4,256]{1,0:T(4,128)(2,1)} %bitcast.46, bf16[2,180,256]{2,1,0:T(8,128)(2,1)} %pad_maximum_fusion.own_ref, bf16[2,180,256]{2,1,0:T(8,128)(2,1)} %collective-permute-done.peer_ref), custom_call_target="tpu_custom_call" | custom-call | tf_op jit(solution)/shard_map/dispatch/pallas_call | solution.py:191
  22.9 18.2 %all_to_all.10 = bf16[32,8,768]{2,1,0:T(8,128)(2,1)S(1)} all-to-all(bf16[32,8,768]{2,1,0:T(8,128)(2,1)} %bitcast.41), channel_id=1, replica_groups=mesh['grp'=16,'ex'=32] {'ex'}, dimensions={0} | all-to-all | bytes 786432 | tf_op jit(solution)/shard_map/all_to_all | solution.py:210
  41.0 10.7 %collective-permute-start.1 = (bf16[256,768]{1,0:T(8,128)(2,1)S(1)}, bf16[256,768]{1,0:T(8,128)(2,1)S(1)}, u32[]{:S(2)}, u32[]{:S(2)}) collective-permute-start(bf16[256,768]{1,0:T(8,128)(2,1)S(1)} %bitcast.33), channel_id=1, source_target_pairs={{0,64},{32,480},{64,128},{96,32},{128,192},{160,96},{192,256},{224... | collective-permute-start | bytes 1179656 | tf_op jit(solution)/shard_map/ppermute | solution.py:215
  51.7 1.9 %collective-permute-start.2 = (bf16[256,768]{1,0:T(8,128)(2,1)S(1)}, bf16[256,768]{1,0:T(8,128)(2,1)S(1)}, u32[]{:S(2)}, u32[]{:S(2)}) collective-permute-start(bf16[256,768]{1,0:T(8,128)(2,1)S(1)} %bitcast.34), channel_id=1, source_target_pairs={{64,0},{480,32},{128,64},{32,96},{192,128},{96,160},{256,192},{160... | collective-permute-start | bytes 1179656 | tf_op jit(solution)/shard_map/ppermute | solution.py:216
  53.6 0.8 copy-done.1
  54.4 2.0 %collective-permute-done.1.refs_1_ = bf16[256,768]{1,0:T(8,128)(2,1)S(1)} collective-permute-done((bf16[256,768]{1,0:T(8,128)(2,1)S(1)}, bf16[256,768]{1,0:T(8,128)(2,1)S(1)}, u32[]{:S(2)}, u32[]{:S(2)}) %collective-permute-start.1) | collective-permute-done | bytes 393248 | tf_op jit(solution)/shard_map/ppermute | solution.py:215
  56.4 5.0 %collective-permute-start.3 = (bf16[256,768]{1,0:T(8,128)(2,1)S(1)}, bf16[256,768]{1,0:T(8,128)(2,1)S(1)}, u32[]{:S(2)}, u32[]{:S(2)}) collective-permute-start(bf16[256,768]{1,0:T(8,128)(2,1)S(1)} %collective-permute-done.1.refs_1_), channel_id=1, source_target_pairs={{0,64},{32,480},{64,128},{96,32},{128,192},{160,96},{192,256},{224... | collective-permute-start | bytes 1179656 | tf_op jit(solution)/shard_map/ppermute | solution.py:215
  61.4 0.7 copy-done.10
  62.2 1.4 collective-permute-done.2.refs_2_
  63.6 1.9 %collective-permute-start.4 = (bf16[256,768]{1,0:T(8,128)(2,1)S(1)}, bf16[256,768]{1,0:T(8,128)(2,1)S(1)}, u32[]{:S(2)}, u32[]{:S(2)}) collective-permute-start(bf16[256,768]{1,0:T(8,128)(2,1)S(1)} %collective-permute-done.2.refs_2_), channel_id=1, source_target_pairs={{64,0},{480,32},{128,64},{32,96},{192,128},{96,160},{256,192},{160... | collective-permute-start | bytes 1179656 | tf_op jit(solution)/shard_map/ppermute | solution.py:216
  65.5 0.0 copy-start.12
  65.5 0.7 copy-done.12
  66.3 0.0 collective-permute-done.3.refs_3_
  66.3 4.9 %collective-permute-start.5 = (bf16[256,768]{1,0:T(8,128)(2,1)S(1)}, bf16[256,768]{1,0:T(8,128)(2,1)S(1)}, u32[]{:S(2)}, u32[]{:S(2)}) collective-permute-start(bf16[256,768]{1,0:T(8,128)(2,1)S(1)} %collective-permute-done.3.refs_3_), channel_id=1, source_target_pairs={{0,64},{32,480},{64,128},{96,32},{128,192},{160,96},{192,256},{224... | collective-permute-start | bytes 1179656 | tf_op jit(solution)/shard_map/ppermute | solution.py:215
  71.2 0.8 copy-done.14
  71.9 4.9 %collective-permute-done.4.refs_4_ = bf16[256,768]{1,0:T(8,128)(2,1)S(1)} collective-permute-done((bf16[256,768]{1,0:T(8,128)(2,1)S(1)}, bf16[256,768]{1,0:T(8,128)(2,1)S(1)}, u32[]{:S(2)}, u32[]{:S(2)}) %collective-permute-start.4) | collective-permute-done | bytes 393248 | tf_op jit(solution)/shard_map/ppermute | solution.py:216
  76.9 1.9 %collective-permute-start.6 = (bf16[256,768]{1,0:T(8,128)(2,1)S(1)}, bf16[256,768]{1,0:T(8,128)(2,1)S(1)}, u32[]{:S(2)}, u32[]{:S(2)}) collective-permute-start(bf16[256,768]{1,0:T(8,128)(2,1)S(1)} %collective-permute-done.4.refs_4_), channel_id=1, source_target_pairs={{64,0},{480,32},{128,64},{32,96},{192,128},{96,160},{256,192},{160... | collective-permute-start | bytes 1179656 | tf_op jit(solution)/shard_map/ppermute | solution.py:216
  78.8 0.6 collective-permute-done.5.refs_5_
  79.3 0.7 slice.17
  80.0 0.7 copy-done.6
  80.8 5.0 %collective-permute-start.7 = (bf16[128,768]{1,0:T(8,128)(2,1)}, bf16[128,768]{1,0:T(8,128)(2,1)}, u32[]{:S(2)}, u32[]{:S(2)}) collective-permute-start(bf16[128,768]{1,0:T(8,128)(2,1)} %slice.17), channel_id=1, source_target_pairs={{0,64},{32,480},{64,128},{96,32},{128,192},{160,96},{192,256},{224... | collective-permute-start | bytes 589832 | tf_op jit(solution)/shard_map/ppermute | solution.py:218
  85.8 4.8 %collective-permute-done.6.refs_6_ = bf16[256,768]{1,0:T(8,128)(2,1)S(1)} collective-permute-done((bf16[256,768]{1,0:T(8,128)(2,1)S(1)}, bf16[256,768]{1,0:T(8,128)(2,1)S(1)}, u32[]{:S(2)}, u32[]{:S(2)}) %collective-permute-start.6) | collective-permute-done | bytes 393248 | tf_op jit(solution)/shard_map/ppermute | solution.py:216
  90.6 0.7 slice.18
  91.3 0.0 copy-done.16
  91.3 0.7 copy-done.8
  92.1 1.9 %collective-permute-start.8 = (bf16[128,768]{1,0:T(8,128)(2,1)}, bf16[128,768]{1,0:T(8,128)(2,1)}, u32[]{:S(2)}, u32[]{:S(2)}) collective-permute-start(bf16[128,768]{1,0:T(8,128)(2,1)} %slice.18), channel_id=1, source_target_pairs={{64,0},{480,32},{128,64},{32,96},{192,128},{96,160},{256,192},{160... | collective-permute-start | bytes 589832 | tf_op jit(solution)/shard_map/ppermute | solution.py:219
  94.1 0.1 stack.44.order_ref
  94.2 0.0 collective-permute-done.7.refs_7_
  94.2 6.8 %collective-permute-done.8.refs_8_ = bf16[128,768]{1,0:T(8,128)(2,1)} collective-permute-done((bf16[128,768]{1,0:T(8,128)(2,1)}, bf16[128,768]{1,0:T(8,128)(2,1)}, u32[]{:S(2)}, u32[]{:S(2)}) %collective-permute-start.8) | collective-permute-done | bytes 196640 | tf_op jit(solution)/shard_map/ppermute | solution.py:219
  101.0 0.0 collective-permute-done.9.refs_10_
  101.1 1.0 copy-done.2
  102.0 1.0 copy-done.7
  103.0 1.0 copy-done.9
  104.0 1.0 copy-done.11
  105.0 1.0 copy-done.13
  106.0 1.0 copy-done.15
  107.0 1.0 copy-done.17
  108.0 14.0 %expert.1 = bf16[2896,256]{1,0:T(8,128)(2,1)S(1)} custom-call(s32[8]{0:T(128)S(1)} %stack.44.order_ref, bf16[256,768]{1,0:T(8,128)(2,1)S(1)} %bitcast.35, bf16[256,768]{1,0:T(8,128)(2,1)S(1)} %copy-done.11, bf16[256,768]{1,0:T(8,128)(2,1)S(1)} %copy-done.13, bf16[256,768]{1,0:T(8,128)(2,1)S(1)} %copy-done.15, bf16[256,768]{1,0:T(8,128)(2,1)S(1)} %copy-done.17, ...), custom_call_target="tpu_custom_call" | custom-call | tf_op jit(solution)/shard_map/expert/pallas_call | solution.py:228
  122.1 1.1 copy-done
  123.2 19.5 %fusion = bf16[368,256]{1,0:T(8,128)(2,1)S(1)} fusion(bf16[2896,256]{1,0:T(8,128)(2,1)} %copy-done), kind=kCustom, calls=%all-reduce-scatter | all-reduce-scatter fusion | flops 753665 | bytes 1673216
  142.8 2.5 %collective-permute-start.11 = (bf16[42,256]{1,0:T(8,128)(2,1)S(1)}, bf16[42,256]{1,0:T(8,128)(2,1)S(1)}, u32[]{:S(2)}, u32[]{:S(2)}) collective-permute-start(bf16[42,256]{1,0:T(8,128)(2,1)S(1)} %slice.21), channel_id=1, source_target_pairs={{0,64},{64,128},{128,192},{192,256},{256,320},{320,384},{384,448},... | collective-permute-start | bytes 64520
  145.3 1.3 dynamic-slice.4
  147.2 0.0 collective-permute-done.11
  147.2 0.6 concatenate
  147.9 0.1 constant_dynamic-slice_fusion
  147.9 0.2 copy.11
  148.1 14.2 %all_to_all.11 = bf16[32,8,362]{2,1,0:T(8,128)(2,1)} all-to-all(bf16[32,8,362]{2,1,0:T(8,128)(2,1)S(1)} %bitcast.39), channel_id=1, replica_groups=mesh['grp'=16,'ex'=32] {'ex'}, dimensions={0} | all-to-all | bytes 370688 | tf_op jit(solution)/shard_map/all_to_all | solution.py:254
  162.3 2.1 %combine.1 = (f32[184,256]{1,0:T(8,128)}, f32[184,256]{1,0:T(8,128)}) custom-call(s32[1]{0:T(128)} %bitcast.core_ref, bf16[256,362]{1,0:T(8,128)(2,1)} %bitcast.40, bf16[256,256]{1,0:T(8,128)(2,1)} %get-tuple-element.7.sel_ref, s32[4,256]{1,0:T(4,128)} %bitcast.45), custom_call_target="tpu_custom_call" | custom-call | tf_op jit(solution)/shard_map/combine/pallas_call | solution.py:257
  164.3 12.0 %collective-permute-start.10 = (f32[184,256]{1,0:T(8,128)}, f32[184,256]{1,0:T(8,128)S(1)}, u32[]{:S(2)}, u32[]{:S(2)}) collective-permute-start(f32[184,256]{1,0:T(8,128)} %get-tuple-element.9), channel_id=1, source_target_pairs={{0,32},{32,0},{64,96},{96,64},{128,160},{160,128},{192,224},{224,1... | collective-permute-start | bytes 565256 | tf_op jit(solution)/shard_map/ppermute | solution.py:263
  176.4 1.2 collective-permute-done.10
  177.6 1.0 add.71
  178.6 0.6 fusion.1
  179.2 0.6 slice_bitcast_fusion
  (19 shorter events, 0.0 us)
Async XLA Ops:
  0.6 1.2 copy-start.3
  1.9 1.2 copy-start.4
  3.1 1.2 copy-start.5
  4.3 9.9 %copy-start.18 = (bf16[256,180]{0,1:T(8,128)(2,1)S(1)}, bf16[256,180]{0,1:T(8,128)(2,1)}, u32[]{:S(2)}) copy-start(bf16[256,180]{0,1:T(8,128)(2,1)} %param.8) | copy-start | bytes 276484
  4.3 9.9 %copy-start.19 = (bf16[256,180]{0,1:T(8,128)(2,1)S(1)}, bf16[256,180]{0,1:T(8,128)(2,1)}, u32[]{:S(2)}) copy-start(bf16[256,180]{0,1:T(8,128)(2,1)} %param.7) | copy-start | bytes 276484
  5.4 95.6 %collective-permute-start.9 = (bf16[8,576,384]{2,1,0:T(8,128)(2,1)S(1)}, bf16[8,576,384]{2,1,0:T(8,128)(2,1)}, u32[]{:S(2)}, u32[]{:S(2)}) collective-permute-start(bf16[8,576,384]{2,1,0:T(8,128)(2,1)S(1)} %pack.1.refs_9_), channel_id=1, source_target_pairs={{0,32},{32,0},{64,96},{96,64},{128,160},{160,128},{192,224},{224,1... | collective-permute-start | bytes 10616840 | tf_op jit(solution)/shard_map/ppermute | solution.py:208
  14.9 5.7 %collective-permute-start = (bf16[2,180,256]{2,1,0:T(8,128)(2,1)}, bf16[2,180,256]{2,1,0:T(8,128)(2,1)}, u32[]{:S(2)}, u32[]{:S(2)}) collective-permute-start(bf16[2,180,256]{2,1,0:T(8,128)(2,1)} %pad_maximum_fusion.own_ref), channel_id=1, source_target_pairs={{0,32},{32,0},{64,96},{96,64},{128,160},{160,128},{192,224},{224,1... | collective-permute-start | bytes 552968 | tf_op jit(solution)/shard_map/ppermute | solution.py:190
  41.0 15.4 %collective-permute-start.1 = (bf16[256,768]{1,0:T(8,128)(2,1)S(1)}, bf16[256,768]{1,0:T(8,128)(2,1)S(1)}, u32[]{:S(2)}, u32[]{:S(2)}) collective-permute-start(bf16[256,768]{1,0:T(8,128)(2,1)S(1)} %bitcast.33), channel_id=1, source_target_pairs={{0,64},{32,480},{64,128},{96,32},{128,192},{160,96},{192,256},{224... | collective-permute-start | bytes 1179656 | tf_op jit(solution)/shard_map/ppermute | solution.py:215
  51.7 11.9 %collective-permute-start.2 = (bf16[256,768]{1,0:T(8,128)(2,1)S(1)}, bf16[256,768]{1,0:T(8,128)(2,1)S(1)}, u32[]{:S(2)}, u32[]{:S(2)}) collective-permute-start(bf16[256,768]{1,0:T(8,128)(2,1)S(1)} %bitcast.34), channel_id=1, source_target_pairs={{64,0},{480,32},{128,64},{32,96},{192,128},{96,160},{256,192},{160... | collective-permute-start | bytes 1179656 | tf_op jit(solution)/shard_map/ppermute | solution.py:216
  53.6 0.8 copy-start.1
  56.4 9.9 %collective-permute-start.3 = (bf16[256,768]{1,0:T(8,128)(2,1)S(1)}, bf16[256,768]{1,0:T(8,128)(2,1)S(1)}, u32[]{:S(2)}, u32[]{:S(2)}) collective-permute-start(bf16[256,768]{1,0:T(8,128)(2,1)S(1)} %collective-permute-done.1.refs_1_), channel_id=1, source_target_pairs={{0,64},{32,480},{64,128},{96,32},{128,192},{160,96},{192,256},{224... | collective-permute-start | bytes 1179656 | tf_op jit(solution)/shard_map/ppermute | solution.py:215
  61.4 0.7 copy-start.10
  63.6 13.2 %collective-permute-start.4 = (bf16[256,768]{1,0:T(8,128)(2,1)S(1)}, bf16[256,768]{1,0:T(8,128)(2,1)S(1)}, u32[]{:S(2)}, u32[]{:S(2)}) collective-permute-start(bf16[256,768]{1,0:T(8,128)(2,1)S(1)} %collective-permute-done.2.refs_2_), channel_id=1, source_target_pairs={{64,0},{480,32},{128,64},{32,96},{192,128},{96,160},{256,192},{160... | collective-permute-start | bytes 1179656 | tf_op jit(solution)/shard_map/ppermute | solution.py:216
  65.5 0.8 copy-start.12
  66.3 13.1 %collective-permute-start.5 = (bf16[256,768]{1,0:T(8,128)(2,1)S(1)}, bf16[256,768]{1,0:T(8,128)(2,1)S(1)}, u32[]{:S(2)}, u32[]{:S(2)}) collective-permute-start(bf16[256,768]{1,0:T(8,128)(2,1)S(1)} %collective-permute-done.3.refs_3_), channel_id=1, source_target_pairs={{0,64},{32,480},{64,128},{96,32},{128,192},{160,96},{192,256},{224... | collective-permute-start | bytes 1179656 | tf_op jit(solution)/shard_map/ppermute | solution.py:215
  71.1 0.8 copy-start.14
  76.9 14.5 %copy-start.16 = (bf16[256,768]{1,0:T(8,128)(2,1)}, bf16[256,768]{1,0:T(8,128)(2,1)S(1)}, u32[]{:S(2)}) copy-start(bf16[256,768]{1,0:T(8,128)(2,1)S(1)} %collective-permute-done.4.refs_4_) | copy-start | bytes 1179652
  76.9 13.8 %collective-permute-start.6 = (bf16[256,768]{1,0:T(8,128)(2,1)S(1)}, bf16[256,768]{1,0:T(8,128)(2,1)S(1)}, u32[]{:S(2)}, u32[]{:S(2)}) collective-permute-start(bf16[256,768]{1,0:T(8,128)(2,1)S(1)} %collective-permute-done.4.refs_4_), channel_id=1, source_target_pairs={{64,0},{480,32},{128,64},{32,96},{192,128},{96,160},{256,192},{160... | collective-permute-start | bytes 1179656 | tf_op jit(solution)/shard_map/ppermute | solution.py:216
  80.0 0.7 copy-start.6
  80.8 13.4 %collective-permute-start.7 = (bf16[128,768]{1,0:T(8,128)(2,1)}, bf16[128,768]{1,0:T(8,128)(2,1)}, u32[]{:S(2)}, u32[]{:S(2)}) collective-permute-start(bf16[128,768]{1,0:T(8,128)(2,1)} %slice.17), channel_id=1, source_target_pairs={{0,64},{32,480},{64,128},{96,32},{128,192},{160,96},{192,256},{224... | collective-permute-start | bytes 589832 | tf_op jit(solution)/shard_map/ppermute | solution.py:218
  91.3 0.7 copy-start.8
  92.1 9.0 %collective-permute-start.8 = (bf16[128,768]{1,0:T(8,128)(2,1)}, bf16[128,768]{1,0:T(8,128)(2,1)}, u32[]{:S(2)}, u32[]{:S(2)}) collective-permute-start(bf16[128,768]{1,0:T(8,128)(2,1)} %slice.18), channel_id=1, source_target_pairs={{64,0},{480,32},{128,64},{32,96},{192,128},{96,160},{256,192},{160... | collective-permute-start | bytes 589832 | tf_op jit(solution)/shard_map/ppermute | solution.py:219
  101.0 1.0 copy-start.2
  102.0 1.0 copy-start.7
  103.0 1.0 copy-start.9
  104.0 1.0 copy-start.11
  105.0 1.0 copy-start.13
  106.0 1.0 copy-start.15
  107.0 1.0 copy-start.17
  122.1 1.2 copy-start
  142.8 4.5 %collective-permute-start.11 = (bf16[42,256]{1,0:T(8,128)(2,1)S(1)}, bf16[42,256]{1,0:T(8,128)(2,1)S(1)}, u32[]{:S(2)}, u32[]{:S(2)}) collective-permute-start(bf16[42,256]{1,0:T(8,128)(2,1)S(1)} %slice.21), channel_id=1, source_target_pairs={{0,64},{64,128},{128,192},{192,256},{256,320},{320,384},{384,448},... | collective-permute-start | bytes 64520
  164.3 13.3 %collective-permute-start.10 = (f32[184,256]{1,0:T(8,128)}, f32[184,256]{1,0:T(8,128)S(1)}, u32[]{:S(2)}, u32[]{:S(2)}) collective-permute-start(f32[184,256]{1,0:T(8,128)} %get-tuple-element.9), channel_id=1, source_target_pairs={{0,32},{32,0},{64,96},{96,64},{128,160},{160,128},{192,224},{224,1... | collective-permute-start | bytes 565256 | tf_op jit(solution)/shard_map/ppermute | solution.py:263

commit v3 on v2

v3 whole, which is shorter than its diff:
```python
import functools

import jax
import jax.numpy as jnp
from jax import lax
from jax.experimental import pallas as pl
from jax.experimental.pallas import tpu as pltpu
from jax.sharding import PartitionSpec as P

TOP = 4
CAP = 16
HALF = CAP // 2
FEATS = 180
HIDDEN = 180
HID = 192
WIDE = 384
CHIP = 2 * FEATS
NT = (((1,), (1,)), ((), ()))
TN = (((0,), (0,)), ((), ()))
F32 = jnp.float32
BF16 = jnp.bfloat16


def iota(shape, dim):
    return lax.broadcasted_iota(jnp.int32, shape, dim)


def route_kernel(me_ref, ids_ref, gate_ref, sel_ref, weight_ref):
    slots, count = sel_ref.shape
    experts = slots // HALF
    gates = gate_ref[...].astype(F32)
    expert = iota((experts, count), 0)
    member = jnp.zeros((experts, count), F32)
    weight = jnp.zeros((experts, count), F32)
    for k in range(TOP):
        named = ids_ref[k : k + 1, :] == expert
        member = jnp.where(named, 1.0, member)
        weight = jnp.where(named, gates[k : k + 1, :], weight)
    earlier = jnp.where(iota((count, count), 0) < iota((count, count), 1), 1.0, 0.0)
    place = jnp.dot(member.astype(BF16), earlier.astype(BF16), preferred_element_type=F32)
    code = jnp.where(member > 0.0, place - (HALF * lax.rem(me_ref[0], 2)).astype(F32), -1.0)
    picked = code[:, None, :] == iota((experts, HALF, count), 1).astype(F32)
    sel_ref[...] = jnp.where(picked, 1.0, 0.0).reshape(slots, count).astype(BF16)
    weight_ref[...] = weight


def dispatch_kernel(me_ref, sel_ref, weight_ref, own_ref, peer_ref, rows_ref, feat_ref):
    slots, count = sel_ref.shape
    experts = slots // HALF
    core = lax.rem(me_ref[0], 2)
    select = sel_ref[...]
    spread = select.astype(F32).reshape(experts, HALF, count) * weight_ref[...][:, None, :]
    slot_weight = jnp.sum(spread.reshape(slots, count), axis=1, keepdims=True)
    feat_ref[...] = jnp.zeros_like(feat_ref)
    for part in range(2):
        own = own_ref[part].astype(F32)
        peer = peer_ref[part].astype(F32)
        base = part * WIDE
        feat_ref[base : base + FEATS, :] = jnp.where(core == 0, own, peer)
        feat_ref[base + FEATS : base + CHIP, :] = jnp.where(core == 0, peer, own)
    rows = lax.dot_general(
        select, feat_ref[...].astype(BF16), NT, preferred_element_type=F32
    )
    rows_ref[...] = jnp.where(iota(rows.shape, 1) == CHIP, slot_weight, rows).astype(BF16)


def pack_kernel(gate_ref, up_ref, down_ref, out_ref, source, packed, sems_in, sems_out):
    chips = packed.shape[0]
    loads = [
        pltpu.make_async_copy(ref, source.at[part], sems_in.at[part])
        for part, ref in enumerate((gate_ref, up_ref, down_ref))
    ]
    for load in loads:
        load.start()
    spare = HID - HIDDEN
    spot = iota((spare, WIDE), 1) == iota((spare, WIDE), 0) + CHIP
    mark = jnp.where(jnp.logical_and(spot, iota((spare, WIDE), 0) < 2), 1.0, 0.0)
    for part in range(3):
        loads[part].wait()
        for chip in range(chips):
            start = chip * CHIP
            low = start // 128 * 128
            high = min(low + 512, source.shape[2])
            w = source[part, :, low:high].astype(F32)
            w = w[:, start - low : start - low + CHIP]
            w = jnp.concatenate([w, jnp.zeros((HIDDEN, WIDE - CHIP), F32)], axis=1)
            tail = mark if part == 0 else jnp.zeros_like(mark)
            w = jnp.concatenate([w, tail], axis=0)
            packed[chip, part * HID : (part + 1) * HID, :] = w.astype(BF16)
    stores = [
        pltpu.make_async_copy(packed.at[chip], out_ref.at[chip], sems_out.at[chip])
        for chip in range(chips)
    ]
    for store in stores:
        store.start()
    for store in stores:
        store.wait()


def project(w, rows, total):
    fresh = (
        lax.dot_general(w[: 2 * HID, :], rows[:, :WIDE], NT, preferred_element_type=F32),
        lax.dot_general(w[2 * HID :, :], rows[:, WIDE:], NT, preferred_element_type=F32),
    )
    return fresh if total is None else (total[0] + fresh[0], total[1] + fresh[1])


def chip_of(me_ref, distance, chips):
    me = me_ref[0]
    return lax.rem(me // 2 + distance * (1 - 2 * lax.rem(me, 2)) + chips, chips)


def forward_kernel(places, me_ref, *refs):
    count = len(places)
    blocks, weights, sources, sums = refs[:count], refs[count : count + 2], refs[count + 2 : -2], refs[-2:]
    chips = weights[0].shape[0]
    totals = [(ref[: 2 * HID, :], ref[2 * HID :, :]) for ref in sources] or [None, None]
    for ref, place in zip(blocks, places):
        chip = chip_of(me_ref, place, chips)
        for i in range(2):
            totals[i] = project(weights[i][chip], ref[...], totals[i])
    for i in range(2):
        sums[i][: 2 * HID, :] = totals[i][0]
        sums[i][2 * HID :, :] = totals[i][1]


def backward_kernel(me_ref, rows_ref, own_w, peer_w, own_sum, peer_sum, out_ref, terms):
    weights = own_w, peer_w
    chips = own_w.shape[0]
    chip = chip_of(me_ref, chips // 2, chips)
    totals = [
        project(w_ref[chip], rows_ref[...], (sum_ref[: 2 * HID, :], sum_ref[2 * HID :, :]))
        for w_ref, sum_ref in zip(weights, (own_sum, peer_sum))
    ]
    grads, probs = [], []
    for pre, back in totals:
        pre_gate, pre_up = pre[:HID], pre[HID:]
        weight = pre_gate[HIDDEN : HIDDEN + 1] * (1.0 / chips)
        sig = jax.nn.sigmoid(pre_gate)
        act = pre_gate * sig
        live = iota(act.shape, 0) < HIDDEN
        probs.append(jnp.sum(jnp.where(live, back * (act * pre_up), 0.0), axis=0, keepdims=True))
        hid_grad = weight * back
        d_gate = hid_grad * pre_up * sig * (1.0 + pre_gate * (1.0 - sig))
        d_up = hid_grad * act
        grads.append([jnp.where(live, d_gate, 0.0), jnp.where(live, d_up, 0.0)])
    prob = probs[0] + probs[1]
    high = prob.astype(BF16).astype(F32)
    row = iota(grads[0][0].shape, 0)
    d_gate = jnp.where(row == HIDDEN, high, grads[0][0])
    grads[0][0] = jnp.where(row == HIDDEN + 1, prob - high, d_gate)
    grads = [jnp.concatenate(g, axis=0).astype(BF16) for g in grads]
    chunk = CHIP + 2
    for k in range(chips):
        value = None
        for i in range(2):
            term = lax.dot_general(
                weights[i][k, : 2 * HID, :], grads[i], TN, preferred_element_type=F32
            )
            value = term if value is None else value + term
        terms[k * chunk : (k + 1) * chunk, :] = value[:chunk, :]
    out_ref[...] = terms[...].astype(BF16)


def combine_kernel(me_ref, ret_ref, sel_ref, ids_ref, keep_ref, send_ref):
    slots, count = sel_ref.shape
    experts = slots // HALF
    core = lax.rem(me_ref[0], 2)
    ret = ret_ref[...]
    select = sel_ref[...]
    total = lax.dot_general(ret, select, TN, preferred_element_type=F32)
    first, second = total[:FEATS, :], total[FEATS:CHIP, :]
    keep_ref[:FEATS, :] = jnp.where(core == 0, first, second)
    send_ref[:FEATS, :] = jnp.where(core == 0, second, first)
    prob = ret[:, CHIP : CHIP + 1].astype(F32) + ret[:, CHIP + 1 : CHIP + 2].astype(F32)
    per_expert = jnp.sum((select.astype(F32) * prob).reshape(experts, HALF, count), axis=1)
    expert = iota((experts, count), 0)
    for k in range(TOP):
        named = ids_ref[k : k + 1, :] == expert
        value = jnp.sum(jnp.where(named, per_expert, 0.0), axis=0, keepdims=True)
        keep_ref[FEATS + k : FEATS + k + 1, :] = value
        send_ref[FEATS + k : FEATS + k + 1, :] = value


def finish_kernel(keep_ref, come_ref, tok_ref, gate_ref):
    total = keep_ref[...] + come_ref[...]
    tok_ref[...] = total[:FEATS, :].astype(BF16)
    gate_ref[...] = total[FEATS:, :]


VMEM = pl.BlockSpec(memory_space=pltpu.VMEM)
SMEM = pl.BlockSpec(memory_space=pltpu.SMEM)
HBM = pl.BlockSpec(memory_space=pltpu.HBM)
DMA = pltpu.SemaphoreType.DMA
SMALL = pltpu.CompilerParams(vmem_limit_bytes=16 * 1024 * 1024)
LARGE = pltpu.CompilerParams(vmem_limit_bytes=32 * 1024 * 1024)


def after(*values):
    return lax.optimization_barrier(values)


def per_device(tokens, out_grad, expert_ids, gate_values, w_gate, w_up, w_down):
    experts = lax.axis_size("ex")
    groups = lax.axis_size("grp")
    chips = groups // 2
    slots = experts * HALF
    count = tokens.shape[0]
    me = lax.axis_index("grp")
    swap = [(i, i ^ 1) for i in range(groups)]
    up = [(i, (i + 2 - 4 * (i % 2)) % groups) for i in range(groups)]
    cross = [(s ^ 1, t) for s, t in up]
    me_arg = me.astype(jnp.int32).reshape(1)
    ids = expert_ids.T
    gates = gate_values.T

    own = jnp.stack([tokens.T, out_grad.T])
    peer = lax.ppermute(own, "grp", swap)
    select, weight = pl.pallas_call(
        route_kernel,
        in_specs=[SMEM, VMEM, VMEM],
        out_shape=(
            jax.ShapeDtypeStruct((slots, count), BF16),
            jax.ShapeDtypeStruct((experts, count), F32),
        ),
        compiler_params=SMALL,
        name="route",
    )(me_arg, ids, gates)
    own_w = pl.pallas_call(
        pack_kernel,
        in_specs=[HBM] * 3,
        out_specs=HBM,
        out_shape=jax.ShapeDtypeStruct((chips, 3 * HID, WIDE), BF16),
        scratch_shapes=[
            pltpu.VMEM((3,) + w_gate.shape[1:], BF16),
            pltpu.VMEM((chips, 3 * HID, WIDE), BF16),
            DMA((3,)),
            DMA((chips,)),
        ],
        compiler_params=pltpu.CompilerParams(vmem_limit_bytes=60 * 1024 * 1024),
        name="pack",
    )(w_gate[0], w_up[0], w_down[0])
    peer, own_w = after(peer, own_w)
    peer_w = lax.ppermute(own_w, "grp", swap)
    rows = pl.pallas_call(
        dispatch_kernel,
        in_specs=[SMEM] + [VMEM] * 4,
        out_shape=jax.ShapeDtypeStruct((slots, 2 * WIDE), BF16),
        scratch_shapes=[pltpu.VMEM((2 * WIDE, count), F32)],
        compiler_params=SMALL,
        name="dispatch",
    )(me_arg, select, weight, own, peer)
    rows = lax.all_to_all(
        rows.reshape(experts, HALF, 2 * WIDE), "ex", split_axis=0, concat_axis=0, tiled=True
    ).reshape(slots, 2 * WIDE)

    mine1 = lax.ppermute(rows, "grp", up)
    other1 = lax.ppermute(rows, "grp", cross)
    mine2 = lax.ppermute(mine1, "grp", up)
    other2 = lax.ppermute(other1, "grp", up)
    came1 = lax.ppermute(other1, "grp", swap)
    mine3 = lax.ppermute(mine2, "grp", up)
    other2, came1 = after(other2, came1)
    other3 = lax.ppermute(other2, "grp", up)
    mine4 = lax.ppermute(mine3, "grp", up)
    came2 = lax.ppermute(other2, "grp", swap)
    came3 = lax.ppermute(other3, "grp", swap)

    def forward(blocks, places, sums):
        n = len(blocks)
        return pl.pallas_call(
            functools.partial(forward_kernel, places),
            in_specs=[SMEM] + [VMEM] * (n + 2 + len(sums)),
            out_specs=[VMEM] * 2,
            out_shape=[jax.ShapeDtypeStruct((3 * HID, slots), F32)] * 2,
            compiler_params=LARGE,
            cost_estimate=pl.CostEstimate(
                flops=n * 4 * slots * 3 * HID * WIDE,
                bytes_accessed=n * (slots + 3 * HID) * 4 * WIDE + 8 * 3 * HID * slots,
                transcendentals=0,
            ),
            name="forward",
        )(me_arg, *blocks, own_w, peer_w, *sums)

    sums = forward([rows, mine1, came1, mine2, came2], (0, -1, 1, -2, 2), ())
    sums = forward([mine3, came3], (-3, 3), sums)
    chunk = CHIP + 2
    terms = pl.pallas_call(
        backward_kernel,
        in_specs=[SMEM] + [VMEM] * 5,
        out_specs=VMEM,
        out_shape=jax.ShapeDtypeStruct((chips * chunk, slots), BF16),
        scratch_shapes=[pltpu.VMEM((chips * chunk, slots), F32)],
        compiler_params=LARGE,
        name="backward",
    )(me_arg, mine4, own_w, peer_w, *sums)

    same_core = [list(range(c, groups, 2)) for c in range(2)]
    part = lax.psum_scatter(
        terms, "grp", scatter_dimension=0, axis_index_groups=same_core, tiled=True
    )
    ret = lax.all_to_all(
        part.T.reshape(experts, HALF, chunk), "ex", split_axis=0, concat_axis=0, tiled=True
    ).reshape(slots, chunk)
    keep, send = pl.pallas_call(
        combine_kernel,
        in_specs=[SMEM] + [VMEM] * 3,
        out_shape=(jax.ShapeDtypeStruct((FEATS + TOP, count), F32),) * 2,
        compiler_params=SMALL,
        name="combine",
    )(me_arg, ret, select, ids)
    tok, gate = pl.pallas_call(
        finish_kernel,
        out_shape=(
            jax.ShapeDtypeStruct((FEATS, count), BF16),
            jax.ShapeDtypeStruct((TOP, count), F32),
        ),
        compiler_params=SMALL,
        name="finish",
    )(keep, lax.ppermute(send, "grp", swap))
    return tok.T, gate.T


def solution(mesh):
    return jax.shard_map(
        per_device,
        mesh=mesh,
        in_specs=(
            P("ex", "grp"),
            P("ex", "grp"),
            P("ex", None),
            P("ex", None),
            P("ex", "grp", None),
            P("ex", "grp", None),
            P("ex", "grp", None),
        ),
        out_specs=(P("ex", "grp"), P("ex", None)),
        check_vma=False,
    )
```

time: 181 us -> 148 us (0.82)
  waiting for transfers between devices: 25.6 us -> 2.72 us
  local copies, waits for them, and re-layouts: 21.1 us -> 7.81 us
  starting transfers between devices: 58.4 us -> 69.5 us
  Pallas kernels: 19.4 us -> 10.9 us
  blocking collectives: 51.9 us -> 53.8 us
    ppermute x9 -> x11, waiting for transfers between devices: 21.8 us -> 2.71 us  [the longest x1 1.04 us: per_device(): lax.ppermute(send, 'grp', swap)]
    ppermute x9 -> x11, starting transfers between devices: 45.2 us -> 56.8 us  [the longest x1 11.2 us: per_device(): other2 = lax.ppermute(other1, 'grp', up)]
    unnamed x44 -> x24, local copies, waits for them, and re-layouts: 18.3 us -> 7.64 us
    ppermute x1, starting transfers between devices: 8.79 us -> 1.91 us  [per_device(): peer_w = lax.ppermute(own_w, 'grp', swap)]
    ppermute x1, starting transfers between devices: 1.91 us -> 8.79 us  [per_device(): peer = lax.ppermute(own, 'grp', swap)]
    pallas_call x3 -> x7, Pallas kernels: 17.3 us -> 10.6 us  [the longest x1 4.32 us: per_device(): pl.pallas_call(pack_kernel, in_specs=[HBM] * 3, out_specs=HBM, out_shape=...]
    ppermute x1, waiting for transfers between devices: 3.79 us -> 0.01 us  [per_device(): peer = lax.ppermute(own, 'grp', swap)]
    unnamed x1, blocking collectives: 19.5 us -> 22.1 us
  transfers between devices with their start and end apart: 12 -> 14, of which waited for: 8 -> 3; matrix products, arithmetic and copies ran while one was open for 2% -> 1% of each run, Pallas kernels for 1% -> 5%
where the time goes in v3:
time: 148 us; the launch traced here: 147 us
  starting transfers between devices  69.5 us (47%)
  blocking collectives  53.8 us (36%)
  Pallas kernels  10.9 us (7%)
  local copies, waits for them, and re-layouts  7.81 us (5%)
  waiting for transfers between devices  2.72 us (2%)
  between operations  1.66 us (1%)
    unnamed x1, blocking collectives  22.1 us
    all_to_all x1, blocking collectives, per_device(): lax.all_to_all(rows.reshape(experts, HALF, 2 * WIDE), 'ex', split_axis=0,...  17.9 us
    all_to_all x1, blocking collectives, per_device(): lax.all_to_all(part.T.reshape(experts, HALF, chunk), 'ex', split_axis=0,...  13.8 us
    ppermute x1, starting transfers between devices, per_device(): other2 = lax.ppermute(other1, 'grp', up)  11.2 us
    ppermute x1, starting transfers between devices, per_device(): lax.ppermute(send, 'grp', swap)  10.8 us
    ppermute x1, starting transfers between devices, per_device(): peer = lax.ppermute(own, 'grp', swap)  8.79 us
    unnamed x24, local copies, waits for them, and re-layouts  7.64 us
    ppermute x1, starting transfers between devices, per_device(): other1 = lax.ppermute(rows, 'grp', cross)  6.36 us
  transfers between devices with their start and end apart: 14, of which 3 were waited for; matrix products, arithmetic and copies ran while one was open for 1% of the time, Pallas kernels for 5%

profile of v3, /device:TPU:1, one launch (start us, length us, event | category | flops | bytes accessed | tf_op | source)
XLA Modules:
  0.0 147.5 jit_solution(17491724805310819761)
XLA Ops:
  0.6 1.0 pad_maximum_fusion.own_ref
  1.6 0.0 copy-start.2
  1.6 8.8 %collective-permute-start = (bf16[2,180,256]{2,1,0:T(8,128)(2,1)S(1)}, bf16[2,180,256]{2,1,0:T(8,128)(2,1)S(1)}, u32[]{:S(2)}, u32[]{:S(2)}) collective-permute-start(bf16[2,180,256]{2,1,0:T(8,128)(2,1)S(1)} %pad_maximum_fusion.own_ref), channel_id=1, source_target_pairs={{0,32},{32,0},{64,96},{96,64},{128,160},{160,128},{192,224},{224,1... | collective-permute-start | bytes 552968 | tf_op jit(solution)/shard_map/ppermute | solution.py:218
  10.4 0.0 copy-start.8
  10.4 0.0 copy-start.9
  10.4 4.3 %pack.1.refs_5_.refs_2_.own_w = bf16[8,576,384]{2,1,0:T(8,128)(2,1)} custom-call(bf16[180,2880]{1,0:T(8,128)(2,1)} %bitcast.31, bf16[180,2880]{1,0:T(8,128)(2,1)} %bitcast.32, bf16[180,2880]{1,0:T(8,128)(2,1)} %bitcast.33), custom_call_target="tpu_custom_call" | custom-call | tf_op jit(solution)/shard_map/pack/pallas_call | solution.py:229
  14.7 0.0 copy-done.2
  14.8 0.0 collective-permute-done.peer_ref
  14.8 0.0 copy-start.6
  14.8 0.7 copy-done.6
  15.4 1.9 %collective-permute-start.5 = (bf16[8,576,384]{2,1,0:T(8,128)(2,1)}, bf16[8,576,384]{2,1,0:T(8,128)(2,1)S(1)}, u32[]{:S(2)}, u32[]{:S(2)}) collective-permute-start(bf16[8,576,384]{2,1,0:T(8,128)(2,1)} %pack.1.refs_5_.refs_2_.own_w), channel_id=1, source_target_pairs={{0,32},{32,0},{64,96},{96,64},{128,160},{160,128},{192,224},{224,1... | collective-permute-start | bytes 10616840 | tf_op jit(solution)/shard_map/ppermute | solution.py:244
  17.4 0.0 copy-done.8
  17.4 0.0 copy-done.9
  17.4 0.2 route.1
  17.6 0.0 copy-start.4
  17.6 0.0 copy-start.3
  17.6 1.0 copy-done.3
  18.6 0.0 copy-start.7
  18.6 0.9 copy-done.7
  19.5 0.3 dispatch.1
  19.8 17.9 %all_to_all.10 = bf16[32,8,768]{2,1,0:T(8,128)(2,1)S(1)} all-to-all(bf16[32,8,768]{2,1,0:T(8,128)(2,1)S(1)} %bitcast.26), channel_id=1, replica_groups=mesh['grp'=16,'ex'=32] {'ex'}, dimensions={0} | all-to-all | bytes 786432 | tf_op jit(solution)/shard_map/all_to_all | solution.py:253
  37.7 6.4 %collective-permute-start.6 = (bf16[256,768]{1,0:T(8,128)(2,1)S(1)}, bf16[256,768]{1,0:T(8,128)(2,1)S(1)}, u32[]{:S(2)}, u32[]{:S(2)}) collective-permute-start(bf16[256,768]{1,0:T(8,128)(2,1)S(1)} %bitcast.23), channel_id=1, source_target_pairs={{32,64},{0,480},{96,128},{64,32},{160,192},{128,96},{224,256},{192... | collective-permute-start | bytes 1179656 | tf_op jit(solution)/shard_map/ppermute | solution.py:258
  44.1 6.2 %collective-permute-start.1 = (bf16[256,768]{1,0:T(8,128)(2,1)S(1)}, bf16[256,768]{1,0:T(8,128)(2,1)S(1)}, u32[]{:S(2)}, u32[]{:S(2)}) collective-permute-start(bf16[256,768]{1,0:T(8,128)(2,1)S(1)} %bitcast.24), channel_id=1, source_target_pairs={{0,64},{32,480},{64,128},{96,32},{128,192},{160,96},{192,256},{224... | collective-permute-start | bytes 1179656 | tf_op jit(solution)/shard_map/ppermute | solution.py:257
  50.3 0.0 collective-permute-done.6
  50.3 11.2 %collective-permute-start.7 = (bf16[256,768]{1,0:T(8,128)(2,1)S(1)}, bf16[256,768]{1,0:T(8,128)(2,1)S(1)}, u32[]{:S(2)}, u32[]{:S(2)}) collective-permute-start(bf16[256,768]{1,0:T(8,128)(2,1)S(1)} %collective-permute-done.6), channel_id=1, source_target_pairs={{0,64},{32,480},{64,128},{96,32},{128,192},{160,96},{192,256},{224... | collective-permute-start | bytes 1179656 | tf_op jit(solution)/shard_map/ppermute | solution.py:260
  61.5 1.9 %collective-permute-start.8 = (bf16[256,768]{1,0:T(8,128)(2,1)S(1)}, bf16[256,768]{1,0:T(8,128)(2,1)S(1)}, u32[]{:S(2)}, u32[]{:S(2)}) collective-permute-start(bf16[256,768]{1,0:T(8,128)(2,1)S(1)} %collective-permute-done.6), channel_id=1, source_target_pairs={{0,32},{32,0},{64,96},{96,64},{128,160},{160,128},{192,224},{224,1... | collective-permute-start | bytes 1179656 | tf_op jit(solution)/shard_map/ppermute | solution.py:261
  63.4 0.0 collective-permute-done.1.refs_1_
  63.4 2.1 %collective-permute-start.2 = (bf16[256,768]{1,0:T(8,128)(2,1)S(1)}, bf16[256,768]{1,0:T(8,128)(2,1)S(1)}, u32[]{:S(2)}, u32[]{:S(2)}) collective-permute-start(bf16[256,768]{1,0:T(8,128)(2,1)S(1)} %collective-permute-done.1.refs_1_), channel_id=1, source_target_pairs={{0,64},{32,480},{64,128},{96,32},{128,192},{160,96},{192,256},{224... | collective-permute-start | bytes 1179656 | tf_op jit(solution)/shard_map/ppermute | solution.py:259
  65.6 0.6 collective-permute-done.7
  66.2 0.0 collective-permute-done.8.refs_2_
  66.2 5.0 %collective-permute-start.9 = (bf16[256,768]{1,0:T(8,128)(2,1)S(1)}, bf16[256,768]{1,0:T(8,128)(2,1)S(1)}, u32[]{:S(2)}, u32[]{:S(2)}) collective-permute-start(bf16[256,768]{1,0:T(8,128)(2,1)S(1)} %collective-permute-done.7), channel_id=1, source_target_pairs={{0,64},{32,480},{64,128},{96,32},{128,192},{160,96},{192,256},{224... | collective-permute-start | bytes 1179656 | tf_op jit(solution)/shard_map/ppermute | solution.py:264
  71.2 1.0 collective-permute-done.2.refs_3_
  72.2 3.2 %collective-permute-start.3 = (bf16[256,768]{1,0:T(8,128)(2,1)S(1)}, bf16[256,768]{1,0:T(8,128)(2,1)S(1)}, u32[]{:S(2)}, u32[]{:S(2)}) collective-permute-start(bf16[256,768]{1,0:T(8,128)(2,1)S(1)} %collective-permute-done.2.refs_3_), channel_id=1, source_target_pairs={{0,64},{32,480},{64,128},{96,32},{128,192},{160,96},{192,256},{224... | collective-permute-start | bytes 1179656 | tf_op jit(solution)/shard_map/ppermute | solution.py:262
  75.4 3.2 %collective-permute-start.11 = (bf16[256,768]{1,0:T(8,128)(2,1)S(1)}, bf16[256,768]{1,0:T(8,128)(2,1)S(1)}, u32[]{:S(2)}, u32[]{:S(2)}) collective-permute-start(bf16[256,768]{1,0:T(8,128)(2,1)S(1)} %collective-permute-done.7), channel_id=1, source_target_pairs={{0,32},{32,0},{64,96},{96,64},{128,160},{160,128},{192,224},{224,1... | collective-permute-start | bytes 1179656 | tf_op jit(solution)/shard_map/ppermute | solution.py:266
  78.6 0.0 collective-permute-done.9
  78.6 2.3 %collective-permute-start.10 = (bf16[256,768]{1,0:T(8,128)(2,1)S(1)}, bf16[256,768]{1,0:T(8,128)(2,1)S(1)}, u32[]{:S(2)}, u32[]{:S(2)}) collective-permute-start(bf16[256,768]{1,0:T(8,128)(2,1)S(1)} %collective-permute-done.9), channel_id=1, source_target_pairs={{0,32},{32,0},{64,96},{96,64},{128,160},{160,128},{192,224},{224,1... | collective-permute-start | bytes 1179656 | tf_op jit(solution)/shard_map/ppermute | solution.py:267
  80.9 0.0 collective-permute-done.3.refs_0_
  80.9 4.5 %collective-permute-start.4 = (bf16[256,768]{1,0:T(8,128)(2,1)S(1)}, bf16[256,768]{1,0:T(8,128)(2,1)S(1)}, u32[]{:S(2)}, u32[]{:S(2)}) collective-permute-start(bf16[256,768]{1,0:T(8,128)(2,1)S(1)} %collective-permute-done.3.refs_0_), channel_id=1, source_target_pairs={{0,64},{32,480},{64,128},{96,32},{128,192},{160,96},{192,256},{224... | collective-permute-start | bytes 1179656 | tf_op jit(solution)/shard_map/ppermute | solution.py:265
  85.4 0.0 collective-permute-done.11.refs_4_
  85.5 0.0 copy-done.4
  85.5 0.0 collective-permute-done.5.refs_6_.refs_3_.peer_w
  85.5 0.0 copy-start
  85.5 2.0 %copy-done = bf16[8,576,384]{2,1,0:T(8,128)(2,1)S(1)} copy-done((bf16[8,576,384]{2,1,0:T(8,128)(2,1)S(1)}, bf16[8,576,384]{2,1,0:T(8,128)(2,1)}, u32[]{:S(2)}) %copy-start) | copy-done | bytes 3538968
  87.5 1.8 %forward.2 = (f32[576,256]{1,0:T(8,128)S(1)}, f32[576,256]{1,0:T(8,128)S(1)}) custom-call(s32[1]{0:T(128)} %bitcast.me_ref, bf16[256,768]{1,0:T(8,128)(2,1)S(1)} %bitcast.25, bf16[256,768]{1,0:T(8,128)(2,1)S(1)} %collective-permute-done.1.refs_1_, bf16[256,768]{1,0:T(8,128)(2,1)S(1)} %collective-permute-done.8.refs_2_, ...), custom_call_target="tpu_custom_call" | custom-call | flops 1132462080 | bytes 7569408 | tf_op jit(solution)/shard_map/forward/pallas_call | solution.py:271
  89.3 0.0 collective-permute-done.10.refs_1_
  89.3 0.9 forward.3
  90.2 0.0 collective-permute-done.4.rows_ref
  90.2 2.4 %backward.1 = bf16[2896,256]{1,0:T(8,128)(2,1)S(1)} custom-call(s32[1]{0:T(128)} %bitcast.me_ref, bf16[256,768]{1,0:T(8,128)(2,1)S(1)} %collective-permute-done.4.rows_ref, bf16[8,576,384]{2,1,0:T(8,128)(2,1)S(1)} %copy-done, bf16[8,576,384]{2,1,0:T(8,128)(2,1)S(1)} %collective-permute-done.5.refs_6_.refs_3_.peer_w, ...), custom_call_target="tpu_custom_call" | custom-call | tf_op jit(solution)/shard_map/backward/pallas_call | solution.py:288
  92.6 0.0 copy-start.1
  92.6 1.1 copy-done.1
  93.7 0.0 copy-start.5
  93.7 22.1 %fusion = bf16[368,256]{1,0:T(8,128)(2,1)S(1)} fusion(bf16[2896,256]{1,0:T(8,128)(2,1)} %copy-done.1), kind=kCustom, calls=%all-reduce-scatter | all-reduce-scatter fusion | flops 753665 | bytes 1673216
  115.9 2.1 %collective-permute-start.13 = (bf16[42,256]{1,0:T(8,128)(2,1)S(1)}, bf16[42,256]{1,0:T(8,128)(2,1)S(1)}, u32[]{:S(2)}, u32[]{:S(2)}) collective-permute-start(bf16[42,256]{1,0:T(8,128)(2,1)S(1)} %slice), channel_id=1, source_target_pairs={{0,64},{64,128},{128,192},{192,256},{256,320},{320,384},{384,448},... | collective-permute-start | bytes 64520
  118.0 1.3 dynamic-slice.4
  119.9 0.0 collective-permute-done.13
  119.9 0.6 concatenate
  120.5 0.1 constant_dynamic-slice_fusion
  120.6 0.2 copy.11
  120.7 13.8 %all_to_all.11 = bf16[32,8,362]{2,1,0:T(8,128)(2,1)S(1)} all-to-all(bf16[32,8,362]{2,1,0:T(8,128)(2,1)S(1)} %bitcast.34), channel_id=1, replica_groups=mesh['grp'=16,'ex'=32] {'ex'}, dimensions={0} | all-to-all | bytes 370688 | tf_op jit(solution)/shard_map/all_to_all | solution.py:302
  134.5 0.0 copy-done.5
  134.6 0.3 combine.1
  134.9 10.8 %collective-permute-start.12 = (f32[184,256]{1,0:T(8,128)S(1)}, f32[184,256]{1,0:T(8,128)S(1)}, u32[]{:S(2)}, u32[]{:S(2)}) collective-permute-start(f32[184,256]{1,0:T(8,128)S(1)} %get-tuple-element.27), channel_id=1, source_target_pairs={{0,32},{32,0},{64,96},{96,64},{128,160},{160,128},{192,224},{224,1... | collective-permute-start | bytes 565256 | tf_op jit(solution)/shard_map/ppermute | solution.py:320
  145.7 1.0 collective-permute-done.12.come_ref
  146.8 0.7 finish.1
  (1 shorter events, 0.0 us)
Async XLA Ops:
  1.6 13.2 %copy-start.2 = (bf16[2,180,256]{2,1,0:T(8,128)(2,1)}, bf16[2,180,256]{2,1,0:T(8,128)(2,1)S(1)}, u32[]{:S(2)}) copy-start(bf16[2,180,256]{2,1,0:T(8,128)(2,1)S(1)} %pad_maximum_fusion.own_ref) | copy-start | bytes 552964
  1.6 13.2 %collective-permute-start = (bf16[2,180,256]{2,1,0:T(8,128)(2,1)S(1)}, bf16[2,180,256]{2,1,0:T(8,128)(2,1)S(1)}, u32[]{:S(2)}, u32[]{:S(2)}) collective-permute-start(bf16[2,180,256]{2,1,0:T(8,128)(2,1)S(1)} %pad_maximum_fusion.own_ref), channel_id=1, source_target_pairs={{0,32},{32,0},{64,96},{96,64},{128,160},{160,128},{192,224},{224,1... | collective-permute-start | bytes 552968 | tf_op jit(solution)/shard_map/ppermute | solution.py:218
  10.4 7.0 %copy-start.8 = (s32[256,4]{0,1:T(4,128)S(1)}, s32[256,4]{0,1:T(4,128)}, u32[]{:S(2)}) copy-start(s32[256,4]{0,1:T(4,128)} %param.9) | copy-start | bytes 12292
  10.4 7.0 %copy-start.9 = (bf16[256,4]{0,1:T(4,128)(2,1)S(1)}, bf16[256,4]{0,1:T(4,128)(2,1)}, u32[]{:S(2)}) copy-start(bf16[256,4]{0,1:T(4,128)(2,1)} %param.10) | copy-start | bytes 6148
  14.8 0.7 copy-start.6
  15.4 70.0 %collective-permute-start.5 = (bf16[8,576,384]{2,1,0:T(8,128)(2,1)}, bf16[8,576,384]{2,1,0:T(8,128)(2,1)S(1)}, u32[]{:S(2)}, u32[]{:S(2)}) collective-permute-start(bf16[8,576,384]{2,1,0:T(8,128)(2,1)} %pack.1.refs_5_.refs_2_.own_w), channel_id=1, source_target_pairs={{0,32},{32,0},{64,96},{96,64},{128,160},{160,128},{192,224},{224,1... | collective-permute-start | bytes 10616840 | tf_op jit(solution)/shard_map/ppermute | solution.py:244
  17.6 67.9 %copy-start.4 = (bf16[256,256]{1,0:T(8,128)(2,1)}, bf16[256,256]{1,0:T(8,128)(2,1)S(1)}, u32[]{:S(2)}) copy-start(bf16[256,256]{1,0:T(8,128)(2,1)S(1)} %get-tuple-element.16.sel_ref) | copy-start | bytes 393220
  17.6 1.0 copy-start.3
  18.6 0.9 copy-start.7
  37.7 12.6 %collective-permute-start.6 = (bf16[256,768]{1,0:T(8,128)(2,1)S(1)}, bf16[256,768]{1,0:T(8,128)(2,1)S(1)}, u32[]{:S(2)}, u32[]{:S(2)}) collective-permute-start(bf16[256,768]{1,0:T(8,128)(2,1)S(1)} %bitcast.23), channel_id=1, source_target_pairs={{32,64},{0,480},{96,128},{64,32},{160,192},{128,96},{224,256},{192... | collective-permute-start | bytes 1179656 | tf_op jit(solution)/shard_map/ppermute | solution.py:258
  44.1 19.3 %collective-permute-start.1 = (bf16[256,768]{1,0:T(8,128)(2,1)S(1)}, bf16[256,768]{1,0:T(8,128)(2,1)S(1)}, u32[]{:S(2)}, u32[]{:S(2)}) collective-permute-start(bf16[256,768]{1,0:T(8,128)(2,1)S(1)} %bitcast.24), channel_id=1, source_target_pairs={{0,64},{32,480},{64,128},{96,32},{128,192},{160,96},{192,256},{224... | collective-permute-start | bytes 1179656 | tf_op jit(solution)/shard_map/ppermute | solution.py:257
  50.3 15.9 %collective-permute-start.7 = (bf16[256,768]{1,0:T(8,128)(2,1)S(1)}, bf16[256,768]{1,0:T(8,128)(2,1)S(1)}, u32[]{:S(2)}, u32[]{:S(2)}) collective-permute-start(bf16[256,768]{1,0:T(8,128)(2,1)S(1)} %collective-permute-done.6), channel_id=1, source_target_pairs={{0,64},{32,480},{64,128},{96,32},{128,192},{160,96},{192,256},{224... | collective-permute-start | bytes 1179656 | tf_op jit(solution)/shard_map/ppermute | solution.py:260
  61.5 4.7 %collective-permute-start.8 = (bf16[256,768]{1,0:T(8,128)(2,1)S(1)}, bf16[256,768]{1,0:T(8,128)(2,1)S(1)}, u32[]{:S(2)}, u32[]{:S(2)}) collective-permute-start(bf16[256,768]{1,0:T(8,128)(2,1)S(1)} %collective-permute-done.6), channel_id=1, source_target_pairs={{0,32},{32,0},{64,96},{96,64},{128,160},{160,128},{192,224},{224,1... | collective-permute-start | bytes 1179656 | tf_op jit(solution)/shard_map/ppermute | solution.py:261
  63.4 8.8 %collective-permute-start.2 = (bf16[256,768]{1,0:T(8,128)(2,1)S(1)}, bf16[256,768]{1,0:T(8,128)(2,1)S(1)}, u32[]{:S(2)}, u32[]{:S(2)}) collective-permute-start(bf16[256,768]{1,0:T(8,128)(2,1)S(1)} %collective-permute-done.1.refs_1_), channel_id=1, source_target_pairs={{0,64},{32,480},{64,128},{96,32},{128,192},{160,96},{192,256},{224... | collective-permute-start | bytes 1179656 | tf_op jit(solution)/shard_map/ppermute | solution.py:259
  66.2 12.5 %collective-permute-start.9 = (bf16[256,768]{1,0:T(8,128)(2,1)S(1)}, bf16[256,768]{1,0:T(8,128)(2,1)S(1)}, u32[]{:S(2)}, u32[]{:S(2)}) collective-permute-start(bf16[256,768]{1,0:T(8,128)(2,1)S(1)} %collective-permute-done.7), channel_id=1, source_target_pairs={{0,64},{32,480},{64,128},{96,32},{128,192},{160,96},{192,256},{224... | collective-permute-start | bytes 1179656 | tf_op jit(solution)/shard_map/ppermute | solution.py:264
  72.2 8.7 %collective-permute-start.3 = (bf16[256,768]{1,0:T(8,128)(2,1)S(1)}, bf16[256,768]{1,0:T(8,128)(2,1)S(1)}, u32[]{:S(2)}, u32[]{:S(2)}) collective-permute-start(bf16[256,768]{1,0:T(8,128)(2,1)S(1)} %collective-permute-done.2.refs_3_), channel_id=1, source_target_pairs={{0,64},{32,480},{64,128},{96,32},{128,192},{160,96},{192,256},{224... | collective-permute-start | bytes 1179656 | tf_op jit(solution)/shard_map/ppermute | solution.py:262
  75.4 10.0 %collective-permute-start.11 = (bf16[256,768]{1,0:T(8,128)(2,1)S(1)}, bf16[256,768]{1,0:T(8,128)(2,1)S(1)}, u32[]{:S(2)}, u32[]{:S(2)}) collective-permute-start(bf16[256,768]{1,0:T(8,128)(2,1)S(1)} %collective-permute-done.7), channel_id=1, source_target_pairs={{0,32},{32,0},{64,96},{96,64},{128,160},{160,128},{192,224},{224,1... | collective-permute-start | bytes 1179656 | tf_op jit(solution)/shard_map/ppermute | solution.py:266
  78.6 10.7 %collective-permute-start.10 = (bf16[256,768]{1,0:T(8,128)(2,1)S(1)}, bf16[256,768]{1,0:T(8,128)(2,1)S(1)}, u32[]{:S(2)}, u32[]{:S(2)}) collective-permute-start(bf16[256,768]{1,0:T(8,128)(2,1)S(1)} %collective-permute-done.9), channel_id=1, source_target_pairs={{0,32},{32,0},{64,96},{96,64},{128,160},{160,128},{192,224},{224,1... | collective-permute-start | bytes 1179656 | tf_op jit(solution)/shard_map/ppermute | solution.py:267
  80.9 9.3 %collective-permute-start.4 = (bf16[256,768]{1,0:T(8,128)(2,1)S(1)}, bf16[256,768]{1,0:T(8,128)(2,1)S(1)}, u32[]{:S(2)}, u32[]{:S(2)}) collective-permute-start(bf16[256,768]{1,0:T(8,128)(2,1)S(1)} %collective-permute-done.3.refs_0_), channel_id=1, source_target_pairs={{0,64},{32,480},{64,128},{96,32},{128,192},{160,96},{192,256},{224... | collective-permute-start | bytes 1179656 | tf_op jit(solution)/shard_map/ppermute | solution.py:265
  85.5 2.0 %copy-start = (bf16[8,576,384]{2,1,0:T(8,128)(2,1)S(1)}, bf16[8,576,384]{2,1,0:T(8,128)(2,1)}, u32[]{:S(2)}) copy-start(bf16[8,576,384]{2,1,0:T(8,128)(2,1)} %pack.1.refs_5_.refs_2_.own_w) | copy-start | bytes 10616836
  92.6 1.1 copy-start.1
  93.7 40.8 %copy-start.5 = (bf16[256,256]{1,0:T(8,128)(2,1)S(1)}, bf16[256,256]{1,0:T(8,128)(2,1)}, u32[]{:S(2)}) copy-start(bf16[256,256]{1,0:T(8,128)(2,1)} %copy-done.4) | copy-start | bytes 393220
  115.9 4.0 %collective-permute-start.13 = (bf16[42,256]{1,0:T(8,128)(2,1)S(1)}, bf16[42,256]{1,0:T(8,128)(2,1)S(1)}, u32[]{:S(2)}, u32[]{:S(2)}) collective-permute-start(bf16[42,256]{1,0:T(8,128)(2,1)S(1)} %slice), channel_id=1, source_target_pairs={{0,64},{64,128},{128,192},{192,256},{256,320},{320,384},{384,448},... | collective-permute-start | bytes 64520
  134.9 11.9 %collective-permute-start.12 = (f32[184,256]{1,0:T(8,128)S(1)}, f32[184,256]{1,0:T(8,128)S(1)}, u32[]{:S(2)}, u32[]{:S(2)}) collective-permute-start(f32[184,256]{1,0:T(8,128)S(1)} %get-tuple-element.27), channel_id=1, source_target_pairs={{0,32},{32,0},{64,96},{96,64},{128,160},{160,128},{192,224},{224,1... | collective-permute-start | bytes 565256 | tf_op jit(solution)/shard_map/ppermute | solution.py:320

commit v4 on v3

--- a/solution.py
+++ b/solution.py
@@ -15,6 +15,7 @@
 HID = 192
 WIDE = 384
 CHIP = 2 * FEATS
+BACK = FEATS + 2
 NT = (((1,), (1,)), ((), ()))
 TN = (((0,), (0,)), ((), ()))
 F32 = jnp.float32
@@ -25,9 +26,10 @@
     return lax.broadcasted_iota(jnp.int32, shape, dim)
 
 
-def route_kernel(me_ref, ids_ref, gate_ref, sel_ref, weight_ref):
+def dispatch_kernel(ids_ref, gate_ref, tok_ref, grad_ref, rows_ref, sel_ref, feat_ref):
     slots, count = sel_ref.shape
-    experts = slots // HALF
+    half = slots // 2
+    experts = half // HALF
     gates = gate_ref[...].astype(F32)
     expert = iota((experts, count), 0)
     member = jnp.zeros((experts, count), F32)
@@ -38,30 +40,31 @@
         weight = jnp.where(named, gates[k : k + 1, :], weight)
     earlier = jnp.where(iota((count, count), 0) < iota((count, count), 1), 1.0, 0.0)
     place = jnp.dot(member.astype(BF16), earlier.astype(BF16), preferred_element_type=F32)
-    code = jnp.where(member > 0.0, place - (HALF * lax.rem(me_ref[0], 2)).astype(F32), -1.0)
-    picked = code[:, None, :] == iota((experts, HALF, count), 1).astype(F32)
-    sel_ref[...] = jnp.where(picked, 1.0, 0.0).reshape(slots, count).astype(BF16)
-    weight_ref[...] = weight
-
-
-def dispatch_kernel(me_ref, sel_ref, weight_ref, own_ref, peer_ref, rows_ref, feat_ref):
-    slots, count = sel_ref.shape
-    experts = slots // HALF
-    core = lax.rem(me_ref[0], 2)
-    select = sel_ref[...]
-    spread = select.astype(F32).reshape(experts, HALF, count) * weight_ref[...][:, None, :]
-    slot_weight = jnp.sum(spread.reshape(slots, count), axis=1, keepdims=True)
+    code = jnp.where(member > 0.0, place, -1.0)
     feat_ref[...] = jnp.zeros_like(feat_ref)
-    for part in range(2):
-        own = own_ref[part].astype(F32)
-        peer = peer_ref[part].astype(F32)
-        base = part * WIDE
-        feat_ref[base : base + FEATS, :] = jnp.where(core == 0, own, peer)
-        feat_ref[base + FEATS : base + CHIP, :] = jnp.where(core == 0, peer, own)
-    rows = lax.dot_general(
-        select, feat_ref[...].astype(BF16), NT, preferred_element_type=F32
-    )
-    rows_ref[...] = jnp.where(iota(rows.shape, 1) == CHIP, slot_weight, rows).astype(BF16)
+    feat_ref[:FEATS, :] = tok_ref[...].astype(F32)
+    feat_ref[FEATS:CHIP, :] = grad_ref[...].astype(F32)
+    feats = feat_ref[...].astype(BF16)
+    for core in range(2):
+        slot = iota((experts, HALF, count), 1).astype(F32) + float(HALF * core)
+        picked = code[:, None, :] == slot
+        select = jnp.where(picked, 1.0, 0.0).reshape(half, count).astype(BF16)
+        slot_weight = jnp.sum(
+            jnp.where(picked, weight[:, None, :], 0.0).reshape(half, count), axis=1, keepdims=True
+        )
+        rows = lax.dot_general(select, feats, NT, preferred_element_type=F32)
+        rows = jnp.where(iota(rows.shape, 1) == CHIP, slot_weight, rows)
+        sel_ref[core * half : (core + 1) * half, :] = select
+        rows_ref[core * half : (core + 1) * half, :] = rows.astype(BF16)
+
+
+def join_kernel(parts_ref, rows_ref):
+    first, second = parts_ref[0].astype(F32), parts_ref[1].astype(F32)
+    rest = first[:, CHIP:WIDE]
+    tok = jnp.concatenate([first[:, :FEATS], second[:, :FEATS], rest], axis=1)
+    grad = jnp.concatenate([first[:, FEATS:CHIP], second[:, FEATS:CHIP], rest], axis=1)
+    rows_ref[:, :WIDE] = tok.astype(BF16)
+    rows_ref[:, WIDE:] = grad.astype(BF16)
 
 
 def pack_kernel(gate_ref, up_ref, down_ref, out_ref, source, packed, sems_in, sems_out):
@@ -75,6 +78,7 @@
     spare = HID - HIDDEN
     spot = iota((spare, WIDE), 1) == iota((spare, WIDE), 0) + CHIP
     mark = jnp.where(jnp.logical_and(spot, iota((spare, WIDE), 0) < 2), 1.0, 0.0)
+    stores = []
     for part in range(3):
         loads[part].wait()
         for chip in range(chips):
@@ -87,12 +91,13 @@
             tail = mark if part == 0 else jnp.zeros_like(mark)
             w = jnp.concatenate([w, tail], axis=0)
             packed[chip, part * HID : (part + 1) * HID, :] = w.astype(BF16)
-    stores = [
-        pltpu.make_async_copy(packed.at[chip], out_ref.at[chip], sems_out.at[chip])
-        for chip in range(chips)
-    ]
-    for store in stores:
-        store.start()
+        rows = pl.ds(part * HID, HID)
+        stores.append(
+            pltpu.make_async_copy(
+                packed.at[:, rows, :], out_ref.at[:, rows, :], sems_out.at[part]
+            )
+        )
+        stores[part].start()
     for store in stores:
         store.wait()
 
@@ -150,7 +155,6 @@
     d_gate = jnp.where(row == HIDDEN, high, grads[0][0])
     grads[0][0] = jnp.where(row == HIDDEN + 1, prob - high, d_gate)
     grads = [jnp.concatenate(g, axis=0).astype(BF16) for g in grads]
-    chunk = CHIP + 2
     for k in range(chips):
         value = None
         for i in range(2):
@@ -158,34 +162,29 @@
                 weights[i][k, : 2 * HID, :], grads[i], TN, preferred_element_type=F32
             )
             value = term if value is None else value + term
-        terms[k * chunk : (k + 1) * chunk, :] = value[:chunk, :]
+        for part in range(2):
+            start = (2 * k + part) * BACK
+            terms[start : start + FEATS, :] = value[part * FEATS : (part + 1) * FEATS, :]
+            terms[start + FEATS : start + BACK, :] = value[CHIP : CHIP + 2, :]
     out_ref[...] = terms[...].astype(BF16)
 
 
-def combine_kernel(me_ref, ret_ref, sel_ref, ids_ref, keep_ref, send_ref):
+def combine_kernel(ret_ref, sel_ref, ids_ref, tok_ref, gate_ref):
     slots, count = sel_ref.shape
-    experts = slots // HALF
-    core = lax.rem(me_ref[0], 2)
+    experts = slots // CAP
     ret = ret_ref[...]
     select = sel_ref[...]
     total = lax.dot_general(ret, select, TN, preferred_element_type=F32)
-    first, second = total[:FEATS, :], total[FEATS:CHIP, :]
-    keep_ref[:FEATS, :] = jnp.where(core == 0, first, second)
-    send_ref[:FEATS, :] = jnp.where(core == 0, second, first)
-    prob = ret[:, CHIP : CHIP + 1].astype(F32) + ret[:, CHIP + 1 : CHIP + 2].astype(F32)
-    per_expert = jnp.sum((select.astype(F32) * prob).reshape(experts, HALF, count), axis=1)
+    tok_ref[...] = total[:FEATS, :].astype(BF16)
+    prob = ret[:, FEATS : FEATS + 1].astype(F32) + ret[:, FEATS + 1 : FEATS + 2].astype(F32)
+    spread = (select.astype(F32) * prob).reshape(2, experts, HALF, count)
+    per_expert = jnp.sum(spread[0] + spread[1], axis=1)
     expert = iota((experts, count), 0)
     for k in range(TOP):
         named = ids_ref[k : k + 1, :] == expert
-        value = jnp.sum(jnp.where(named, per_expert, 0.0), axis=0, keepdims=True)
-        keep_ref[FEATS + k : FEATS + k + 1, :] = value
-        send_ref[FEATS + k : FEATS + k + 1, :] = value
-
-
-def finish_kernel(keep_ref, come_ref, tok_ref, gate_ref):
-    total = keep_ref[...] + come_ref[...]
-    tok_ref[...] = total[:FEATS, :].astype(BF16)
-    gate_ref[...] = total[FEATS:, :]
+        gate_ref[k : k + 1, :] = jnp.sum(
+            jnp.where(named, per_expert, 0.0), axis=0, keepdims=True
+        )
 
 
 VMEM = pl.BlockSpec(memory_space=pltpu.VMEM)
@@ -206,26 +205,34 @@
     chips = groups // 2
     slots = experts * HALF
     count = tokens.shape[0]
-    me = lax.axis_index("grp")
+    me_arg = lax.axis_index("grp").astype(jnp.int32).reshape(1)
     swap = [(i, i ^ 1) for i in range(groups)]
     up = [(i, (i + 2 - 4 * (i % 2)) % groups) for i in range(groups)]
     cross = [(s ^ 1, t) for s, t in up]
-    me_arg = me.astype(jnp.int32).reshape(1)
-    ids = expert_ids.T
-    gates = gate_values.T
-
-    own = jnp.stack([tokens.T, out_grad.T])
-    peer = lax.ppermute(own, "grp", swap)
-    select, weight = pl.pallas_call(
-        route_kernel,
-        in_specs=[SMEM, VMEM, VMEM],
+    both_cores = [list(range(2 * z * experts, 2 * (z + 1) * experts)) for z in range(chips)]
+    ids, me_arg = after(expert_ids.T, me_arg)
+
+    def exchange(rows):
+        return lax.all_to_all(
+            rows.reshape(2 * experts, HALF, rows.shape[-1]),
+            ("grp", "ex"),
+            split_axis=0,
+            concat_axis=0,
+            axis_index_groups=both_cores,
+            tiled=True,
+        )
+
+    rows, select = pl.pallas_call(
+        dispatch_kernel,
+        in_specs=[VMEM] * 4,
         out_shape=(
-            jax.ShapeDtypeStruct((slots, count), BF16),
-            jax.ShapeDtypeStruct((experts, count), F32),
+            jax.ShapeDtypeStruct((2 * slots, WIDE), BF16),
+            jax.ShapeDtypeStruct((2 * slots, count), BF16),
         ),
+        scratch_shapes=[pltpu.VMEM((WIDE, count), F32)],
         compiler_params=SMALL,
-        name="route",
-    )(me_arg, ids, gates)
+        name="dispatch",
+    )(ids, gate_values.T, tokens.T, out_grad.T)
     own_w = pl.pallas_call(
         pack_kernel,
         in_specs=[HBM] * 3,
@@ -235,34 +242,34 @@
             pltpu.VMEM((3,) + w_gate.shape[1:], BF16),
             pltpu.VMEM((chips, 3 * HID, WIDE), BF16),
             DMA((3,)),
-            DMA((chips,)),
+            DMA((3,)),
         ],
         compiler_params=pltpu.CompilerParams(vmem_limit_bytes=60 * 1024 * 1024),
         name="pack",
     )(w_gate[0], w_up[0], w_down[0])
-    peer, own_w = after(peer, own_w)
+    rows, own_w = after(rows, own_w)
+    rows = pl.pallas_call(
+        join_kernel,
+        in_specs=[VMEM],
+        out_specs=VMEM,
+        out_shape=jax.ShapeDtypeStruct((slots, 2 * WIDE), BF16),
+        compiler_params=SMALL,
+        name="join",
+    )(exchange(rows).reshape(2, slots, WIDE))
+
+    rows, own_w = after(rows, own_w)
     peer_w = lax.ppermute(own_w, "grp", swap)
-    rows = pl.pallas_call(
-        dispatch_kernel,
-        in_specs=[SMEM] + [VMEM] * 4,
-        out_shape=jax.ShapeDtypeStruct((slots, 2 * WIDE), BF16),
-        scratch_shapes=[pltpu.VMEM((2 * WIDE, count), F32)],
-        compiler_params=SMALL,
-        name="dispatch",
-    )(me_arg, select, weight, own, peer)
-    rows = lax.all_to_all(
-        rows.reshape(experts, HALF, 2 * WIDE), "ex", split_axis=0, concat_axis=0, tiled=True
-    ).reshape(slots, 2 * WIDE)
-
     mine1 = lax.ppermute(rows, "grp", up)
     other1 = lax.ppermute(rows, "grp", cross)
     mine2 = lax.ppermute(mine1, "grp", up)
     other2 = lax.ppermute(other1, "grp", up)
+    other1, mine2 = after(other1, mine2)
     came1 = lax.ppermute(other1, "grp", swap)
     mine3 = lax.ppermute(mine2, "grp", up)
-    other2, came1 = after(other2, came1)
     other3 = lax.ppermute(other2, "grp", up)
+    mine3, came1 = after(mine3, came1)
     mine4 = lax.ppermute(mine3, "grp", up)
+    other2, other3 = after(other2, other3)
     came2 = lax.ppermute(other2, "grp", swap)
     came3 = lax.ppermute(other3, "grp", swap)
 
@@ -284,13 +291,12 @@
 
     sums = forward([rows, mine1, came1, mine2, came2], (0, -1, 1, -2, 2), ())
     sums = forward([mine3, came3], (-3, 3), sums)
-    chunk = CHIP + 2
     terms = pl.pallas_call(
         backward_kernel,
         in_specs=[SMEM] + [VMEM] * 5,
         out_specs=VMEM,
-        out_shape=jax.ShapeDtypeStruct((chips * chunk, slots), BF16),
-        scratch_shapes=[pltpu.VMEM((chips * chunk, slots), F32)],
+        out_shape=jax.ShapeDtypeStruct((groups * BACK, slots), BF16),
+        scratch_shapes=[pltpu.VMEM((groups * BACK, slots), F32)],
         compiler_params=LARGE,
         name="backward",
     )(me_arg, mine4, own_w, peer_w, *sums)
@@ -299,25 +305,17 @@
     part = lax.psum_scatter(
         terms, "grp", scatter_dimension=0, axis_index_groups=same_core, tiled=True
     )
-    ret = lax.all_to_all(
-        part.T.reshape(experts, HALF, chunk), "ex", split_axis=0, concat_axis=0, tiled=True
-    ).reshape(slots, chunk)
-    keep, send = pl.pallas_call(
+    ret = exchange(part.reshape(2, BACK, slots).transpose(0, 2, 1)).reshape(2 * slots, BACK)
+    tok, gate = pl.pallas_call(
         combine_kernel,
-        in_specs=[SMEM] + [VMEM] * 3,
-        out_shape=(jax.ShapeDtypeStruct((FEATS + TOP, count), F32),) * 2,
-        compiler_params=SMALL,
-        name="combine",
-    )(me_arg, ret, select, ids)
-    tok, gate = pl.pallas_call(
-        finish_kernel,
+        in_specs=[VMEM] * 3,
         out_shape=(
             jax.ShapeDtypeStruct((FEATS, count), BF16),
             jax.ShapeDtypeStruct((TOP, count), F32),
         ),
         compiler_params=SMALL,
-        name="finish",
-    )(keep, lax.ppermute(send, "grp", swap))
+        name="combine",
+    )(ret, select, ids)
     return tok.T, gate.T
 
 

time: 148 us -> 139 us (0.939)
  starting transfers between devices: 69.5 us -> 48.9 us
  blocking collectives: 53.8 us -> 69.6 us
  local copies, waits for them, and re-layouts: 7.81 us -> 4.25 us
    ppermute x2 -> x0, starting transfers between devices: 19.6 us -> none  [the longest x1 10.8 us: per_device(): lax.ppermute(send, 'grp', swap)]
    all_to_all x2, blocking collectives: 31.7 us -> 48.1 us  [exchange(): lax.all_to_all(rows.reshape(2 * experts, HALF, rows.shape[-1]), ('grp', '...]
    unnamed x24 -> x16, local copies, waits for them, and re-layouts: 7.64 us -> 4.07 us
    ppermute x1, waiting for transfers between devices: 0.62 us -> 2.76 us  [per_device(): other2 = lax.ppermute(other1, 'grp', up)]
    ppermute x1, starting transfers between devices: 6.21 us -> 8.23 us  [per_device(): mine1 = lax.ppermute(rows, 'grp', up)]
    ppermute x1, starting transfers between devices: 6.36 us -> 4.36 us  [per_device(): other1 = lax.ppermute(rows, 'grp', cross)]
    ppermute x1, starting transfers between devices: 4.51 us -> 2.83 us  [per_device(): mine4 = lax.ppermute(mine3, 'grp', up)]
  transfers between devices with their start and end apart: 14 -> 12, of which waited for: 3 -> 2; matrix products, arithmetic and copies ran while one was open for 1% -> 1% of each run, Pallas kernels for 5% -> 2%
where the time goes in v4:
time: 139 us
  blocking collectives  69.6 us (50%)
  starting transfers between devices  48.9 us (35%)
  Pallas kernels  10.4 us (7%)
  local copies, waits for them, and re-layouts  4.25 us (3%)
  waiting for transfers between devices  3.89 us (3%)
  between operations  1.63 us (1%)
    all_to_all x2, blocking collectives, exchange(): lax.all_to_all(rows.reshape(2 * experts, HALF, rows.shape[-1]), ('grp', '...  48.1 us
    unnamed x1, blocking collectives  21.6 us
    ppermute x1, starting transfers between devices, per_device(): other2 = lax.ppermute(other1, 'grp', up)  11.2 us
    ppermute x1, starting transfers between devices, per_device(): mine1 = lax.ppermute(rows, 'grp', up)  8.23 us
    ppermute x1, starting transfers between devices, per_device(): other3 = lax.ppermute(other2, 'grp', up)  5.01 us
    ppermute x1, starting transfers between devices, per_device(): other1 = lax.ppermute(rows, 'grp', cross)  4.36 us
    ppermute x1, starting transfers between devices, per_device(): mine3 = lax.ppermute(mine2, 'grp', up)  4.19 us
    unnamed x16, local copies, waits for them, and re-layouts  4.07 us
  transfers between devices with their start and end apart: 12, of which 2 were waited for; matrix products, arithmetic and copies ran while one was open for 1% of the time, Pallas kernels for 2%

profile of v4, /device:TPU:1, one launch (start us, length us, event | category | flops | bytes accessed | tf_op | source)
XLA Modules:
  0.0 138.7 jit_solution(4230907434798235071)
XLA Ops:
  0.6 0.0 copy-start.2
  0.6 0.0 copy-start.3
  0.7 0.0 copy-start.4
  0.7 0.0 copy-start.5
  0.7 3.6 %pack.1.refs_5_.refs_2_.own_w = bf16[8,576,384]{2,1,0:T(8,128)(2,1)} custom-call(bf16[180,2880]{1,0:T(8,128)(2,1)} %bitcast.26, bf16[180,2880]{1,0:T(8,128)(2,1)} %bitcast.27, bf16[180,2880]{1,0:T(8,128)(2,1)} %bitcast.28), custom_call_target="tpu_custom_call" | custom-call | tf_op jit(solution)/shard_map/pack/pallas_call | solution.py:236
  4.3 0.0 copy-done.2
  4.3 0.0 copy-done.3
  4.3 0.0 copy-done.4
  4.3 0.0 copy-done.5
  4.3 0.5 dispatch.1
  4.9 26.1 %all_to_all.10 = bf16[64,8,384]{2,1,0:T(8,128)(2,1)S(1)} all-to-all(bf16[64,8,384]{2,1,0:T(8,128)(2,1)S(1)} %bitcast.20), channel_id=1, replica_groups={{0,1,2,3,4,5,6,7,8,9,10,11,12,13,14,15,16,17,18,19,20,21,22,23,24,25,26..., dimensions={0} | all-to-all | bytes 786432 | tf_op jit(solution)/shard_map/all_to_all | solution.py:216
  31.0 0.1 join.1.refs_0_
  31.1 1.9 %collective-permute-start.6 = (bf16[8,576,384]{2,1,0:T(8,128)(2,1)}, bf16[8,576,384]{2,1,0:T(8,128)(2,1)S(1)}, u32[]{:S(2)}, u32[]{:S(2)}) collective-permute-start(bf16[8,576,384]{2,1,0:T(8,128)(2,1)} %pack.1.refs_5_.refs_2_.own_w), channel_id=1, source_target_pairs={{0,32},{32,0},{64,96},{96,64},{128,160},{160,128},{192,224},{224,1... | collective-permute-start | bytes 10616840 | tf_op jit(solution)/shard_map/ppermute | solution.py:261
  33.1 4.4 %collective-permute-start = (bf16[256,768]{1,0:T(8,128)(2,1)S(1)}, bf16[256,768]{1,0:T(8,128)(2,1)S(1)}, u32[]{:S(2)}, u32[]{:S(2)}) collective-permute-start(bf16[256,768]{1,0:T(8,128)(2,1)S(1)} %join.1.refs_0_), channel_id=1, source_target_pairs={{32,64},{0,480},{96,128},{64,32},{160,192},{128,96},{224,256},{192... | collective-permute-start | bytes 1179656 | tf_op jit(solution)/shard_map/ppermute | solution.py:263
  37.4 8.2 %collective-permute-start.1 = (bf16[256,768]{1,0:T(8,128)(2,1)S(1)}, bf16[256,768]{1,0:T(8,128)(2,1)S(1)}, u32[]{:S(2)}, u32[]{:S(2)}) collective-permute-start(bf16[256,768]{1,0:T(8,128)(2,1)S(1)} %join.1.refs_0_), channel_id=1, source_target_pairs={{0,64},{32,480},{64,128},{96,32},{128,192},{160,96},{192,256},{224... | collective-permute-start | bytes 1179656 | tf_op jit(solution)/shard_map/ppermute | solution.py:262
  45.7 0.0 collective-permute-done
  45.7 11.2 %collective-permute-start.7 = (bf16[256,768]{1,0:T(8,128)(2,1)S(1)}, bf16[256,768]{1,0:T(8,128)(2,1)S(1)}, u32[]{:S(2)}, u32[]{:S(2)}) collective-permute-start(bf16[256,768]{1,0:T(8,128)(2,1)S(1)} %collective-permute-done), channel_id=1, source_target_pairs={{0,64},{32,480},{64,128},{96,32},{128,192},{160,96},{192,256},{224... | collective-permute-start | bytes 1179656 | tf_op jit(solution)/shard_map/ppermute | solution.py:265
  56.9 0.0 collective-permute-done.1.refs_1_
  56.9 1.9 %collective-permute-start.2 = (bf16[256,768]{1,0:T(8,128)(2,1)S(1)}, bf16[256,768]{1,0:T(8,128)(2,1)S(1)}, u32[]{:S(2)}, u32[]{:S(2)}) collective-permute-start(bf16[256,768]{1,0:T(8,128)(2,1)S(1)} %collective-permute-done.1.refs_1_), channel_id=1, source_target_pairs={{0,64},{32,480},{64,128},{96,32},{128,192},{160,96},{192,256},{224... | collective-permute-start | bytes 1179656 | tf_op jit(solution)/shard_map/ppermute | solution.py:264
  58.8 2.8 %collective-permute-done.7 = bf16[256,768]{1,0:T(8,128)(2,1)S(1)} collective-permute-done((bf16[256,768]{1,0:T(8,128)(2,1)S(1)}, bf16[256,768]{1,0:T(8,128)(2,1)S(1)}, u32[]{:S(2)}, u32[]{:S(2)}) %collective-permute-start.7) | collective-permute-done | bytes 393248 | tf_op jit(solution)/shard_map/ppermute | solution.py:265
  61.6 5.0 %collective-permute-start.8 = (bf16[256,768]{1,0:T(8,128)(2,1)S(1)}, bf16[256,768]{1,0:T(8,128)(2,1)S(1)}, u32[]{:S(2)}, u32[]{:S(2)}) collective-permute-start(bf16[256,768]{1,0:T(8,128)(2,1)S(1)} %collective-permute-done.7), channel_id=1, source_target_pairs={{0,64},{32,480},{64,128},{96,32},{128,192},{160,96},{192,256},{224... | collective-permute-start | bytes 1179656 | tf_op jit(solution)/shard_map/ppermute | solution.py:269
  66.6 0.0 collective-permute-done.2.refs_3_
  66.6 4.2 %collective-permute-start.3 = (bf16[256,768]{1,0:T(8,128)(2,1)S(1)}, bf16[256,768]{1,0:T(8,128)(2,1)S(1)}, u32[]{:S(2)}, u32[]{:S(2)}) collective-permute-start(bf16[256,768]{1,0:T(8,128)(2,1)S(1)} %collective-permute-done.2.refs_3_), channel_id=1, source_target_pairs={{0,64},{32,480},{64,128},{96,32},{128,192},{160,96},{192,256},{224... | collective-permute-start | bytes 1179656 | tf_op jit(solution)/shard_map/ppermute | solution.py:268
  70.8 1.9 %collective-permute-start.4 = (bf16[256,768]{1,0:T(8,128)(2,1)S(1)}, bf16[256,768]{1,0:T(8,128)(2,1)S(1)}, u32[]{:S(2)}, u32[]{:S(2)}) collective-permute-start(bf16[256,768]{1,0:T(8,128)(2,1)S(1)} %collective-permute-done), channel_id=1, source_target_pairs={{0,32},{32,0},{64,96},{96,64},{128,160},{160,128},{192,224},{224,1... | collective-permute-start | bytes 1179656 | tf_op jit(solution)/shard_map/ppermute | solution.py:267
  72.7 0.0 collective-permute-done.8
  72.7 3.1 %collective-permute-start.10 = (bf16[256,768]{1,0:T(8,128)(2,1)S(1)}, bf16[256,768]{1,0:T(8,128)(2,1)S(1)}, u32[]{:S(2)}, u32[]{:S(2)}) collective-permute-start(bf16[256,768]{1,0:T(8,128)(2,1)S(1)} %collective-permute-done.7), channel_id=1, source_target_pairs={{0,32},{32,0},{64,96},{96,64},{128,160},{160,128},{192,224},{224,1... | collective-permute-start | bytes 1179656 | tf_op jit(solution)/shard_map/ppermute | solution.py:273
  75.9 1.9 %collective-permute-start.9 = (bf16[256,768]{1,0:T(8,128)(2,1)S(1)}, bf16[256,768]{1,0:T(8,128)(2,1)S(1)}, u32[]{:S(2)}, u32[]{:S(2)}) collective-permute-start(bf16[256,768]{1,0:T(8,128)(2,1)S(1)} %collective-permute-done.8), channel_id=1, source_target_pairs={{0,32},{32,0},{64,96},{96,64},{128,160},{160,128},{192,224},{224,1... | collective-permute-start | bytes 1179656 | tf_op jit(solution)/shard_map/ppermute | solution.py:274
  77.8 0.0 collective-permute-done.3.refs_0_
  77.8 0.0 collective-permute-done.4.refs_2_
  77.8 2.8 %collective-permute-start.5 = (bf16[256,768]{1,0:T(8,128)(2,1)S(1)}, bf16[256,768]{1,0:T(8,128)(2,1)S(1)}, u32[]{:S(2)}, u32[]{:S(2)}) collective-permute-start(bf16[256,768]{1,0:T(8,128)(2,1)S(1)} %collective-permute-done.3.refs_0_), channel_id=1, source_target_pairs={{0,64},{32,480},{64,128},{96,32},{128,192},{160,96},{192,256},{224... | collective-permute-start | bytes 1179656 | tf_op jit(solution)/shard_map/ppermute | solution.py:271
  80.7 0.0 collective-permute-done.10.refs_4_
  80.7 0.0 collective-permute-done.6.refs_6_.refs_3_.peer_w
  80.7 0.0 copy-start
  80.7 2.0 %copy-done = bf16[8,576,384]{2,1,0:T(8,128)(2,1)S(1)} copy-done((bf16[8,576,384]{2,1,0:T(8,128)(2,1)S(1)}, bf16[8,576,384]{2,1,0:T(8,128)(2,1)}, u32[]{:S(2)}) %copy-start) | copy-done | bytes 3538968
  82.7 0.0 copy-start.1
  82.7 1.8 %forward.2 = (f32[576,256]{1,0:T(8,128)S(1)}, f32[576,256]{1,0:T(8,128)S(1)}) custom-call(s32[1]{0:T(128)} %bitcast.1.me_ref, bf16[256,768]{1,0:T(8,128)(2,1)S(1)} %join.1.refs_0_, bf16[256,768]{1,0:T(8,128)(2,1)S(1)} %collective-permute-done.1.refs_1_, bf16[256,768]{1,0:T(8,128)(2,1)S(1)} %collective-permute-done.4.refs_2_, ...), custom_call_target="tpu_custom_call" | custom-call | flops 1132462080 | bytes 7569408 | tf_op jit(solution)/shard_map/forward/pallas_call | solution.py:278
  84.5 0.0 collective-permute-done.9.refs_1_
  84.5 0.2 copy-done.1
  84.7 0.8 forward.3
  85.5 1.1 collective-permute-done.5.rows_ref
  86.6 2.4 %backward.1 = bf16[2912,256]{1,0:T(8,128)(2,1)S(1)} custom-call(s32[1]{0:T(128)} %bitcast.1.me_ref, bf16[256,768]{1,0:T(8,128)(2,1)S(1)} %collective-permute-done.5.rows_ref, bf16[8,576,384]{2,1,0:T(8,128)(2,1)S(1)} %copy-done.1, bf16[8,576,384]{2,1,0:T(8,128)(2,1)S(1)} %collective-permute-done.6.refs_6_.refs_3_.peer_w, ...), custom_call_target="tpu_custom_call" | custom-call | tf_op jit(solution)/shard_map/backward/pallas_call | solution.py:294
  89.1 21.6 %fusion = bf16[368,256]{1,0:T(8,128)(2,1)S(1)} fusion(bf16[2912,256]{1,0:T(8,128)(2,1)S(1)} %backward.1), kind=kCustom, calls=%all-reduce-scatter | all-reduce-scatter fusion | flops 753665 | bytes 1681408
  110.7 2.2 %collective-permute-start.11 = (bf16[28,256]{1,0:T(8,128)(2,1)S(1)}, bf16[28,256]{1,0:T(8,128)(2,1)S(1)}, u32[]{:S(2)}, u32[]{:S(2)}) collective-permute-start(bf16[28,256]{1,0:T(8,128)(2,1)S(1)} %slice), channel_id=1, source_target_pairs={{0,64},{64,128},{128,192},{192,256},{256,320},{320,384},{384,448},... | collective-permute-start | bytes 43016
  112.9 1.3 dynamic-slice.4
  114.8 0.0 collective-permute-done.11
  114.8 0.6 concatenate
  115.4 0.1 constant_dynamic-slice_fusion
  115.5 0.1 copy.11
  115.7 21.9 %all_to_all.11 = bf16[64,8,182]{2,1,0:T(8,128)(2,1)S(1)} all-to-all(bf16[64,8,182]{2,1,0:T(8,128)(2,1)S(1)} %bitcast.29), channel_id=1, replica_groups={{0,1,2,3,4,5,6,7,8,9,10,11,12,13,14,15,16,17,18,19,20,21,22,23,24,25,26..., dimensions={0} | all-to-all | bytes 372736 | tf_op jit(solution)/shard_map/all_to_all | solution.py:216
  137.6 1.0 combine.1
  (2 shorter events, 0.0 us)
Async XLA Ops:
  0.6 3.7 %copy-start.2 = (bf16[256,180]{0,1:T(8,128)(2,1)S(1)}, bf16[256,180]{0,1:T(8,128)(2,1)}, u32[]{:S(2)}) copy-start(bf16[256,180]{0,1:T(8,128)(2,1)} %param.7) | copy-start | bytes 276484
  0.6 3.7 %copy-start.3 = (bf16[256,180]{0,1:T(8,128)(2,1)S(1)}, bf16[256,180]{0,1:T(8,128)(2,1)}, u32[]{:S(2)}) copy-start(bf16[256,180]{0,1:T(8,128)(2,1)} %param.8) | copy-start | bytes 276484
  0.7 3.7 %copy-start.4 = (s32[256,4]{0,1:T(4,128)S(1)}, s32[256,4]{0,1:T(4,128)}, u32[]{:S(2)}) copy-start(s32[256,4]{0,1:T(4,128)} %param.9) | copy-start | bytes 12292
  0.7 3.7 %copy-start.5 = (bf16[256,4]{0,1:T(4,128)(2,1)S(1)}, bf16[256,4]{0,1:T(4,128)(2,1)}, u32[]{:S(2)}) copy-start(bf16[256,4]{0,1:T(4,128)(2,1)} %param.10) | copy-start | bytes 6148
  31.1 49.6 %collective-permute-start.6 = (bf16[8,576,384]{2,1,0:T(8,128)(2,1)}, bf16[8,576,384]{2,1,0:T(8,128)(2,1)S(1)}, u32[]{:S(2)}, u32[]{:S(2)}) collective-permute-start(bf16[8,576,384]{2,1,0:T(8,128)(2,1)} %pack.1.refs_5_.refs_2_.own_w), channel_id=1, source_target_pairs={{0,32},{32,0},{64,96},{96,64},{128,160},{160,128},{192,224},{224,1... | collective-permute-start | bytes 10616840 | tf_op jit(solution)/shard_map/ppermute | solution.py:261
  33.1 12.6 %collective-permute-start = (bf16[256,768]{1,0:T(8,128)(2,1)S(1)}, bf16[256,768]{1,0:T(8,128)(2,1)S(1)}, u32[]{:S(2)}, u32[]{:S(2)}) collective-permute-start(bf16[256,768]{1,0:T(8,128)(2,1)S(1)} %join.1.refs_0_), channel_id=1, source_target_pairs={{32,64},{0,480},{96,128},{64,32},{160,192},{128,96},{224,256},{192... | collective-permute-start | bytes 1179656 | tf_op jit(solution)/shard_map/ppermute | solution.py:263
  37.4 19.4 %collective-permute-start.1 = (bf16[256,768]{1,0:T(8,128)(2,1)S(1)}, bf16[256,768]{1,0:T(8,128)(2,1)S(1)}, u32[]{:S(2)}, u32[]{:S(2)}) collective-permute-start(bf16[256,768]{1,0:T(8,128)(2,1)S(1)} %join.1.refs_0_), channel_id=1, source_target_pairs={{0,64},{32,480},{64,128},{96,32},{128,192},{160,96},{192,256},{224... | collective-permute-start | bytes 1179656 | tf_op jit(solution)/shard_map/ppermute | solution.py:262
  45.7 15.9 %collective-permute-start.7 = (bf16[256,768]{1,0:T(8,128)(2,1)S(1)}, bf16[256,768]{1,0:T(8,128)(2,1)S(1)}, u32[]{:S(2)}, u32[]{:S(2)}) collective-permute-start(bf16[256,768]{1,0:T(8,128)(2,1)S(1)} %collective-permute-done), channel_id=1, source_target_pairs={{0,64},{32,480},{64,128},{96,32},{128,192},{160,96},{192,256},{224... | collective-permute-start | bytes 1179656 | tf_op jit(solution)/shard_map/ppermute | solution.py:265
  56.9 9.7 %collective-permute-start.2 = (bf16[256,768]{1,0:T(8,128)(2,1)S(1)}, bf16[256,768]{1,0:T(8,128)(2,1)S(1)}, u32[]{:S(2)}, u32[]{:S(2)}) collective-permute-start(bf16[256,768]{1,0:T(8,128)(2,1)S(1)} %collective-permute-done.1.refs_1_), channel_id=1, source_target_pairs={{0,64},{32,480},{64,128},{96,32},{128,192},{160,96},{192,256},{224... | collective-permute-start | bytes 1179656 | tf_op jit(solution)/shard_map/ppermute | solution.py:264
  61.6 11.2 %collective-permute-start.8 = (bf16[256,768]{1,0:T(8,128)(2,1)S(1)}, bf16[256,768]{1,0:T(8,128)(2,1)S(1)}, u32[]{:S(2)}, u32[]{:S(2)}) collective-permute-start(bf16[256,768]{1,0:T(8,128)(2,1)S(1)} %collective-permute-done.7), channel_id=1, source_target_pairs={{0,64},{32,480},{64,128},{96,32},{128,192},{160,96},{192,256},{224... | collective-permute-start | bytes 1179656 | tf_op jit(solution)/shard_map/ppermute | solution.py:269
  66.6 11.2 %collective-permute-start.3 = (bf16[256,768]{1,0:T(8,128)(2,1)S(1)}, bf16[256,768]{1,0:T(8,128)(2,1)S(1)}, u32[]{:S(2)}, u32[]{:S(2)}) collective-permute-start(bf16[256,768]{1,0:T(8,128)(2,1)S(1)} %collective-permute-done.2.refs_3_), channel_id=1, source_target_pairs={{0,64},{32,480},{64,128},{96,32},{128,192},{160,96},{192,256},{224... | collective-permute-start | bytes 1179656 | tf_op jit(solution)/shard_map/ppermute | solution.py:268
  70.8 7.0 %collective-permute-start.4 = (bf16[256,768]{1,0:T(8,128)(2,1)S(1)}, bf16[256,768]{1,0:T(8,128)(2,1)S(1)}, u32[]{:S(2)}, u32[]{:S(2)}) collective-permute-start(bf16[256,768]{1,0:T(8,128)(2,1)S(1)} %collective-permute-done), channel_id=1, source_target_pairs={{0,32},{32,0},{64,96},{96,64},{128,160},{160,128},{192,224},{224,1... | collective-permute-start | bytes 1179656 | tf_op jit(solution)/shard_map/ppermute | solution.py:267
  72.7 7.9 %collective-permute-start.10 = (bf16[256,768]{1,0:T(8,128)(2,1)S(1)}, bf16[256,768]{1,0:T(8,128)(2,1)S(1)}, u32[]{:S(2)}, u32[]{:S(2)}) collective-permute-start(bf16[256,768]{1,0:T(8,128)(2,1)S(1)} %collective-permute-done.7), channel_id=1, source_target_pairs={{0,32},{32,0},{64,96},{96,64},{128,160},{160,128},{192,224},{224,1... | collective-permute-start | bytes 1179656 | tf_op jit(solution)/shard_map/ppermute | solution.py:273
  75.9 8.6 %collective-permute-start.9 = (bf16[256,768]{1,0:T(8,128)(2,1)S(1)}, bf16[256,768]{1,0:T(8,128)(2,1)S(1)}, u32[]{:S(2)}, u32[]{:S(2)}) collective-permute-start(bf16[256,768]{1,0:T(8,128)(2,1)S(1)} %collective-permute-done.8), channel_id=1, source_target_pairs={{0,32},{32,0},{64,96},{96,64},{128,160},{160,128},{192,224},{224,1... | collective-permute-start | bytes 1179656 | tf_op jit(solution)/shard_map/ppermute | solution.py:274
  77.8 8.8 %collective-permute-start.5 = (bf16[256,768]{1,0:T(8,128)(2,1)S(1)}, bf16[256,768]{1,0:T(8,128)(2,1)S(1)}, u32[]{:S(2)}, u32[]{:S(2)}) collective-permute-start(bf16[256,768]{1,0:T(8,128)(2,1)S(1)} %collective-permute-done.3.refs_0_), channel_id=1, source_target_pairs={{0,64},{32,480},{64,128},{96,32},{128,192},{160,96},{192,256},{224... | collective-permute-start | bytes 1179656 | tf_op jit(solution)/shard_map/ppermute | solution.py:271
  80.7 2.0 %copy-start = (bf16[8,576,384]{2,1,0:T(8,128)(2,1)S(1)}, bf16[8,576,384]{2,1,0:T(8,128)(2,1)}, u32[]{:S(2)}) copy-start(bf16[8,576,384]{2,1,0:T(8,128)(2,1)} %pack.1.refs_5_.refs_2_.own_w) | copy-start | bytes 10616836
  82.7 2.0 %copy-start.1 = (bf16[8,576,384]{2,1,0:T(8,128)(2,1)S(1)}, bf16[8,576,384]{2,1,0:T(8,128)(2,1)}, u32[]{:S(2)}) copy-start(bf16[8,576,384]{2,1,0:T(8,128)(2,1)} %pack.1.refs_5_.refs_2_.own_w) | copy-start | bytes 10616836
  110.7 4.2 %collective-permute-start.11 = (bf16[28,256]{1,0:T(8,128)(2,1)S(1)}, bf16[28,256]{1,0:T(8,128)(2,1)S(1)}, u32[]{:S(2)}, u32[]{:S(2)}) collective-permute-start(bf16[28,256]{1,0:T(8,128)(2,1)S(1)} %slice), channel_id=1, source_target_pairs={{0,64},{64,128},{128,192},{192,256},{256,320},{320,384},{384,448},... | collective-permute-start | bytes 43016

commit v5 on v4

--- a/solution.py
+++ b/solution.py
@@ -129,14 +129,10 @@
         sums[i][2 * HID :, :] = totals[i][1]
 
 
-def backward_kernel(me_ref, rows_ref, own_w, peer_w, own_sum, peer_sum, out_ref, terms):
+def backward_kernel(own_w, peer_w, own_sum, peer_sum, out_ref, terms):
     weights = own_w, peer_w
     chips = own_w.shape[0]
-    chip = chip_of(me_ref, chips // 2, chips)
-    totals = [
-        project(w_ref[chip], rows_ref[...], (sum_ref[: 2 * HID, :], sum_ref[2 * HID :, :]))
-        for w_ref, sum_ref in zip(weights, (own_sum, peer_sum))
-    ]
+    totals = [(ref[: 2 * HID, :], ref[2 * HID :, :]) for ref in (own_sum, peer_sum)]
     grads, probs = [], []
     for pre, back in totals:
         pre_gate, pre_up = pre[:HID], pre[HID:]
@@ -209,6 +205,7 @@
     swap = [(i, i ^ 1) for i in range(groups)]
     up = [(i, (i + 2 - 4 * (i % 2)) % groups) for i in range(groups)]
     cross = [(s ^ 1, t) for s, t in up]
+    leave = [(s, t ^ 1) for s, t in up]
     both_cores = [list(range(2 * z * experts, 2 * (z + 1) * experts)) for z in range(chips)]
     ids, me_arg = after(expert_ids.T, me_arg)
 
@@ -267,8 +264,7 @@
     came1 = lax.ppermute(other1, "grp", swap)
     mine3 = lax.ppermute(mine2, "grp", up)
     other3 = lax.ppermute(other2, "grp", up)
-    mine3, came1 = after(mine3, came1)
-    mine4 = lax.ppermute(mine3, "grp", up)
+    came4 = lax.ppermute(other3, "grp", leave)
     other2, other3 = after(other2, other3)
     came2 = lax.ppermute(other2, "grp", swap)
     came3 = lax.ppermute(other3, "grp", swap)
@@ -289,17 +285,18 @@
             name="forward",
         )(me_arg, *blocks, own_w, peer_w, *sums)
 
-    sums = forward([rows, mine1, came1, mine2, came2], (0, -1, 1, -2, 2), ())
-    sums = forward([mine3, came3], (-3, 3), sums)
+    sums = forward([rows, mine1, mine2, came1], (0, -1, -2, 1), ())
+    sums = forward([mine3, came4], (-3, 4), sums)
+    sums = forward([came2, came3], (2, 3), sums)
     terms = pl.pallas_call(
         backward_kernel,
-        in_specs=[SMEM] + [VMEM] * 5,
+        in_specs=[VMEM] * 4,
         out_specs=VMEM,
         out_shape=jax.ShapeDtypeStruct((groups * BACK, slots), BF16),
         scratch_shapes=[pltpu.VMEM((groups * BACK, slots), F32)],
         compiler_params=LARGE,
         name="backward",
-    )(me_arg, mine4, own_w, peer_w, *sums)
+    )(own_w, peer_w, *sums)
 
     same_core = [list(range(c, groups, 2)) for c in range(2)]
     part = lax.psum_scatter(

time: 139 us -> 137 us (0.986)
    pallas_call x2 -> x3, Pallas kernels: 2.67 us -> 3.2 us  [forward(): pl.pallas_call(functools.partial(forward_kernel, places), in_specs=[SMEM]...]
    unnamed x16 -> x14, local copies, waits for them, and re-layouts: 4.07 us -> 3.92 us
  transfers between devices with their start and end apart: 12 -> 12, of which waited for: 2 -> 1; matrix products, arithmetic and copies ran while one was open for 1% -> 1% of each run, Pallas kernels for 2% -> 2%
where the time goes in v5:
time: 137 us
  blocking collectives  69.6 us (51%)
  starting transfers between devices  48.1 us (35%)
  Pallas kernels  10.4 us (8%)
  local copies, waits for them, and re-layouts  4.09 us (3%)
  waiting for transfers between devices  2.79 us (2%)
  between operations  1.64 us (1%)
    all_to_all x2, blocking collectives, exchange(): lax.all_to_all(rows.reshape(2 * experts, HALF, rows.shape[-1]), ('grp', '...  47.8 us
    unnamed x1, blocking collectives  21.8 us
    ppermute x1, starting transfers between devices, per_device(): other2 = lax.ppermute(other1, 'grp', up)  11.2 us
    ppermute x1, starting transfers between devices, per_device(): mine1 = lax.ppermute(rows, 'grp', up)  8.23 us
    ppermute x1, starting transfers between devices, per_device(): other3 = lax.ppermute(other2, 'grp', up)  5.01 us
    ppermute x1, starting transfers between devices, per_device(): other1 = lax.ppermute(rows, 'grp', cross)  4.36 us
    unnamed x14, local copies, waits for them, and re-layouts  3.92 us
    pallas_call x1, Pallas kernels, per_device(): pl.pallas_call(pack_kernel, in_specs=[HBM] * 3, out_specs=HBM, out_shape=...  3.62 us
  transfers between devices with their start and end apart: 12, of which 1 were waited for; matrix products, arithmetic and copies ran while one was open for 1% of the time, Pallas kernels for 2%

profile of v5, /device:TPU:1, one launch (start us, length us, event | category | flops | bytes accessed | tf_op | source)
XLA Modules:
  0.0 136.6 jit_solution(4393630701022589269)
XLA Ops:
  0.6 0.0 copy-start.1
  0.6 0.0 copy-start.2
  0.7 0.0 copy-start.3
  0.7 0.0 copy-start.4
  0.7 3.6 %pack.1.refs_4_.refs_2_.own_w = bf16[8,576,384]{2,1,0:T(8,128)(2,1)} custom-call(bf16[180,2880]{1,0:T(8,128)(2,1)} %bitcast.26, bf16[180,2880]{1,0:T(8,128)(2,1)} %bitcast.27, bf16[180,2880]{1,0:T(8,128)(2,1)} %bitcast.28), custom_call_target="tpu_custom_call" | custom-call | tf_op jit(solution)/shard_map/pack/pallas_call | solution.py:233
  4.3 0.0 copy-done.1
  4.3 0.0 copy-done.2
  4.3 0.0 copy-done.3
  4.3 0.0 copy-done.4
  4.3 0.5 dispatch.1
  4.9 26.1 %all_to_all.10 = bf16[64,8,384]{2,1,0:T(8,128)(2,1)S(1)} all-to-all(bf16[64,8,384]{2,1,0:T(8,128)(2,1)S(1)} %bitcast.20), channel_id=1, replica_groups={{0,1,2,3,4,5,6,7,8,9,10,11,12,13,14,15,16,17,18,19,20,21,22,23,24,25,26..., dimensions={0} | all-to-all | bytes 786432 | tf_op jit(solution)/shard_map/all_to_all | solution.py:213
  31.0 0.1 join.1.refs_0_
  31.1 1.9 %collective-permute-start = (bf16[8,576,384]{2,1,0:T(8,128)(2,1)}, bf16[8,576,384]{2,1,0:T(8,128)(2,1)S(1)}, u32[]{:S(2)}, u32[]{:S(2)}) collective-permute-start(bf16[8,576,384]{2,1,0:T(8,128)(2,1)} %pack.1.refs_4_.refs_2_.own_w), channel_id=1, source_target_pairs={{0,32},{32,0},{64,96},{96,64},{128,160},{160,128},{192,224},{224,1... | collective-permute-start | bytes 10616840 | tf_op jit(solution)/shard_map/ppermute | solution.py:258
  33.1 4.4 %collective-permute-start.1 = (bf16[256,768]{1,0:T(8,128)(2,1)S(1)}, bf16[256,768]{1,0:T(8,128)(2,1)S(1)}, u32[]{:S(2)}, u32[]{:S(2)}) collective-permute-start(bf16[256,768]{1,0:T(8,128)(2,1)S(1)} %join.1.refs_0_), channel_id=1, source_target_pairs={{32,64},{0,480},{96,128},{64,32},{160,192},{128,96},{224,256},{192... | collective-permute-start | bytes 1179656 | tf_op jit(solution)/shard_map/ppermute | solution.py:260
  37.4 8.2 %collective-permute-start.6 = (bf16[256,768]{1,0:T(8,128)(2,1)S(1)}, bf16[256,768]{1,0:T(8,128)(2,1)S(1)}, u32[]{:S(2)}, u32[]{:S(2)}) collective-permute-start(bf16[256,768]{1,0:T(8,128)(2,1)S(1)} %join.1.refs_0_), channel_id=1, source_target_pairs={{0,64},{32,480},{64,128},{96,32},{128,192},{160,96},{192,256},{224... | collective-permute-start | bytes 1179656 | tf_op jit(solution)/shard_map/ppermute | solution.py:259
  45.7 0.0 collective-permute-done.1
  45.7 11.2 %collective-permute-start.2 = (bf16[256,768]{1,0:T(8,128)(2,1)S(1)}, bf16[256,768]{1,0:T(8,128)(2,1)S(1)}, u32[]{:S(2)}, u32[]{:S(2)}) collective-permute-start(bf16[256,768]{1,0:T(8,128)(2,1)S(1)} %collective-permute-done.1), channel_id=1, source_target_pairs={{0,64},{32,480},{64,128},{96,32},{128,192},{160,96},{192,256},{224... | collective-permute-start | bytes 1179656 | tf_op jit(solution)/shard_map/ppermute | solution.py:262
  56.9 0.0 collective-permute-done.6.refs_1_
  56.9 1.9 %collective-permute-start.7 = (bf16[256,768]{1,0:T(8,128)(2,1)S(1)}, bf16[256,768]{1,0:T(8,128)(2,1)S(1)}, u32[]{:S(2)}, u32[]{:S(2)}) collective-permute-start(bf16[256,768]{1,0:T(8,128)(2,1)S(1)} %collective-permute-done.6.refs_1_), channel_id=1, source_target_pairs={{0,64},{32,480},{64,128},{96,32},{128,192},{160,96},{192,256},{224... | collective-permute-start | bytes 1179656 | tf_op jit(solution)/shard_map/ppermute | solution.py:261
  58.8 2.8 %collective-permute-done.2 = bf16[256,768]{1,0:T(8,128)(2,1)S(1)} collective-permute-done((bf16[256,768]{1,0:T(8,128)(2,1)S(1)}, bf16[256,768]{1,0:T(8,128)(2,1)S(1)}, u32[]{:S(2)}, u32[]{:S(2)}) %collective-permute-start.2) | collective-permute-done | bytes 393248 | tf_op jit(solution)/shard_map/ppermute | solution.py:262
  61.6 5.0 %collective-permute-start.3 = (bf16[256,768]{1,0:T(8,128)(2,1)S(1)}, bf16[256,768]{1,0:T(8,128)(2,1)S(1)}, u32[]{:S(2)}, u32[]{:S(2)}) collective-permute-start(bf16[256,768]{1,0:T(8,128)(2,1)S(1)} %collective-permute-done.2), channel_id=1, source_target_pairs={{0,64},{32,480},{64,128},{96,32},{128,192},{160,96},{192,256},{224... | collective-permute-start | bytes 1179656 | tf_op jit(solution)/shard_map/ppermute | solution.py:266
  66.6 0.0 collective-permute-done.7.refs_2_
  66.6 2.6 %collective-permute-start.10 = (bf16[256,768]{1,0:T(8,128)(2,1)S(1)}, bf16[256,768]{1,0:T(8,128)(2,1)S(1)}, u32[]{:S(2)}, u32[]{:S(2)}) collective-permute-start(bf16[256,768]{1,0:T(8,128)(2,1)S(1)} %collective-permute-done.1), channel_id=1, source_target_pairs={{0,32},{32,0},{64,96},{96,64},{128,160},{160,128},{192,224},{224,1... | collective-permute-start | bytes 1179656 | tf_op jit(solution)/shard_map/ppermute | solution.py:264
  69.2 3.5 %collective-permute-start.8 = (bf16[256,768]{1,0:T(8,128)(2,1)S(1)}, bf16[256,768]{1,0:T(8,128)(2,1)S(1)}, u32[]{:S(2)}, u32[]{:S(2)}) collective-permute-start(bf16[256,768]{1,0:T(8,128)(2,1)S(1)} %collective-permute-done.7.refs_2_), channel_id=1, source_target_pairs={{0,64},{32,480},{64,128},{96,32},{128,192},{160,96},{192,256},{224... | collective-permute-start | bytes 1179656 | tf_op jit(solution)/shard_map/ppermute | solution.py:265
  72.7 0.0 collective-permute-done.3
  72.7 3.2 %collective-permute-start.9 = (bf16[256,768]{1,0:T(8,128)(2,1)S(1)}, bf16[256,768]{1,0:T(8,128)(2,1)S(1)}, u32[]{:S(2)}, u32[]{:S(2)}) collective-permute-start(bf16[256,768]{1,0:T(8,128)(2,1)S(1)} %collective-permute-done.3), channel_id=1, source_target_pairs={{0,96},{32,448},{64,160},{96,0},{128,224},{160,64},{192,288},{224,... | collective-permute-start | bytes 1179656 | tf_op jit(solution)/shard_map/ppermute | solution.py:267
  75.9 1.9 %collective-permute-start.4 = (bf16[256,768]{1,0:T(8,128)(2,1)S(1)}, bf16[256,768]{1,0:T(8,128)(2,1)S(1)}, u32[]{:S(2)}, u32[]{:S(2)}) collective-permute-start(bf16[256,768]{1,0:T(8,128)(2,1)S(1)} %collective-permute-done.2), channel_id=1, source_target_pairs={{0,32},{32,0},{64,96},{96,64},{128,160},{160,128},{192,224},{224,1... | collective-permute-start | bytes 1179656 | tf_op jit(solution)/shard_map/ppermute | solution.py:269
  77.8 0.0 collective-permute-done.10.refs_3_
  77.9 2.4 %collective-permute-start.5 = (bf16[256,768]{1,0:T(8,128)(2,1)S(1)}, bf16[256,768]{1,0:T(8,128)(2,1)S(1)}, u32[]{:S(2)}, u32[]{:S(2)}) collective-permute-start(bf16[256,768]{1,0:T(8,128)(2,1)S(1)} %collective-permute-done.3), channel_id=1, source_target_pairs={{0,32},{32,0},{64,96},{96,64},{128,160},{160,128},{192,224},{224,1... | collective-permute-start | bytes 1179656 | tf_op jit(solution)/shard_map/ppermute | solution.py:270
  80.3 0.0 collective-permute-done.refs_5_.refs_3_.peer_w
  80.3 0.0 copy-start
  80.3 2.0 %copy-done = bf16[8,576,384]{2,1,0:T(8,128)(2,1)S(1)} copy-done((bf16[8,576,384]{2,1,0:T(8,128)(2,1)S(1)}, bf16[8,576,384]{2,1,0:T(8,128)(2,1)}, u32[]{:S(2)}) %copy-start) | copy-done | bytes 3538968
  82.3 1.5 %forward.3 = (f32[576,256]{1,0:T(8,128)S(1)}, f32[576,256]{1,0:T(8,128)S(1)}) custom-call(s32[1]{0:T(128)} %bitcast.1.me_ref, bf16[256,768]{1,0:T(8,128)(2,1)S(1)} %join.1.refs_0_, bf16[256,768]{1,0:T(8,128)(2,1)S(1)} %collective-permute-done.6.refs_1_, bf16[256,768]{1,0:T(8,128)(2,1)S(1)} %collective-permute-done.7.refs_2_, ...), custom_call_target="tpu_custom_call" | custom-call | flops 905969664 | bytes 6291456 | tf_op jit(solution)/shard_map/forward/pallas_call | solution.py:274
  83.8 0.0 collective-permute-done.8.refs_0_
  83.8 0.0 collective-permute-done.9.refs_1_
  83.8 0.8 forward.4
  84.7 0.0 collective-permute-done.4.refs_0_
  84.7 0.0 collective-permute-done.5.refs_1_
  84.7 0.9 forward.5
  85.5 1.9 %backward.1 = bf16[2912,256]{1,0:T(8,128)(2,1)S(1)} custom-call(bf16[8,576,384]{2,1,0:T(8,128)(2,1)S(1)} %copy-done, bf16[8,576,384]{2,1,0:T(8,128)(2,1)S(1)} %collective-permute-done.refs_5_.refs_3_.peer_w, f32[576,256]{1,0:T(8,128)S(1)} %get-tuple-element.37.own_sum, f32[576,256]{1,0:T(8,128)S(1)} %get-tuple-element.38.peer_sum), custom_call_target="tpu_custom_call" | custom-call | tf_op jit(solution)/shard_map/backward/pallas_call | solution.py:291
  87.5 21.8 %fusion = bf16[368,256]{1,0:T(8,128)(2,1)S(1)} fusion(bf16[2912,256]{1,0:T(8,128)(2,1)S(1)} %backward.1), kind=kCustom, calls=%all-reduce-scatter | all-reduce-scatter fusion | flops 753665 | bytes 1681408
  109.3 1.8 %collective-permute-start.11 = (bf16[28,256]{1,0:T(8,128)(2,1)S(1)}, bf16[28,256]{1,0:T(8,128)(2,1)S(1)}, u32[]{:S(2)}, u32[]{:S(2)}) collective-permute-start(bf16[28,256]{1,0:T(8,128)(2,1)S(1)} %slice), channel_id=1, source_target_pairs={{0,64},{64,128},{128,192},{192,256},{256,320},{320,384},{384,448},... | collective-permute-start | bytes 43016
  111.1 1.3 dynamic-slice.4
  113.0 0.0 collective-permute-done.11
  113.1 0.6 concatenate
  113.6 0.1 constant_dynamic-slice_fusion
  113.7 0.1 copy.11
  113.9 21.7 %all_to_all.11 = bf16[64,8,182]{2,1,0:T(8,128)(2,1)S(1)} all-to-all(bf16[64,8,182]{2,1,0:T(8,128)(2,1)S(1)} %bitcast.29), channel_id=1, replica_groups={{0,1,2,3,4,5,6,7,8,9,10,11,12,13,14,15,16,17,18,19,20,21,22,23,24,25,26..., dimensions={0} | all-to-all | bytes 372736 | tf_op jit(solution)/shard_map/all_to_all | solution.py:213
  135.6 1.0 combine.1
  (2 shorter events, 0.0 us)
Async XLA Ops:
  0.6 3.7 %copy-start.1 = (bf16[256,180]{0,1:T(8,128)(2,1)S(1)}, bf16[256,180]{0,1:T(8,128)(2,1)}, u32[]{:S(2)}) copy-start(bf16[256,180]{0,1:T(8,128)(2,1)} %param.7) | copy-start | bytes 276484
  0.6 3.7 %copy-start.2 = (bf16[256,180]{0,1:T(8,128)(2,1)S(1)}, bf16[256,180]{0,1:T(8,128)(2,1)}, u32[]{:S(2)}) copy-start(bf16[256,180]{0,1:T(8,128)(2,1)} %param.8) | copy-start | bytes 276484
  0.7 3.7 %copy-start.3 = (s32[256,4]{0,1:T(4,128)S(1)}, s32[256,4]{0,1:T(4,128)}, u32[]{:S(2)}) copy-start(s32[256,4]{0,1:T(4,128)} %param.9) | copy-start | bytes 12292
  0.7 3.7 %copy-start.4 = (bf16[256,4]{0,1:T(4,128)(2,1)S(1)}, bf16[256,4]{0,1:T(4,128)(2,1)}, u32[]{:S(2)}) copy-start(bf16[256,4]{0,1:T(4,128)(2,1)} %param.10) | copy-start | bytes 6148
  31.1 49.1 %collective-permute-start = (bf16[8,576,384]{2,1,0:T(8,128)(2,1)}, bf16[8,576,384]{2,1,0:T(8,128)(2,1)S(1)}, u32[]{:S(2)}, u32[]{:S(2)}) collective-permute-start(bf16[8,576,384]{2,1,0:T(8,128)(2,1)} %pack.1.refs_4_.refs_2_.own_w), channel_id=1, source_target_pairs={{0,32},{32,0},{64,96},{96,64},{128,160},{160,128},{192,224},{224,1... | collective-permute-start | bytes 10616840 | tf_op jit(solution)/shard_map/ppermute | solution.py:258
  33.1 12.6 %collective-permute-start.1 = (bf16[256,768]{1,0:T(8,128)(2,1)S(1)}, bf16[256,768]{1,0:T(8,128)(2,1)S(1)}, u32[]{:S(2)}, u32[]{:S(2)}) collective-permute-start(bf16[256,768]{1,0:T(8,128)(2,1)S(1)} %join.1.refs_0_), channel_id=1, source_target_pairs={{32,64},{0,480},{96,128},{64,32},{160,192},{128,96},{224,256},{192... | collective-permute-start | bytes 1179656 | tf_op jit(solution)/shard_map/ppermute | solution.py:260
  37.4 19.4 %collective-permute-start.6 = (bf16[256,768]{1,0:T(8,128)(2,1)S(1)}, bf16[256,768]{1,0:T(8,128)(2,1)S(1)}, u32[]{:S(2)}, u32[]{:S(2)}) collective-permute-start(bf16[256,768]{1,0:T(8,128)(2,1)S(1)} %join.1.refs_0_), channel_id=1, source_target_pairs={{0,64},{32,480},{64,128},{96,32},{128,192},{160,96},{192,256},{224... | collective-permute-start | bytes 1179656 | tf_op jit(solution)/shard_map/ppermute | solution.py:259
  45.7 15.9 %collective-permute-start.2 = (bf16[256,768]{1,0:T(8,128)(2,1)S(1)}, bf16[256,768]{1,0:T(8,128)(2,1)S(1)}, u32[]{:S(2)}, u32[]{:S(2)}) collective-permute-start(bf16[256,768]{1,0:T(8,128)(2,1)S(1)} %collective-permute-done.1), channel_id=1, source_target_pairs={{0,64},{32,480},{64,128},{96,32},{128,192},{160,96},{192,256},{224... | collective-permute-start | bytes 1179656 | tf_op jit(solution)/shard_map/ppermute | solution.py:262
  56.9 9.7 %collective-permute-start.7 = (bf16[256,768]{1,0:T(8,128)(2,1)S(1)}, bf16[256,768]{1,0:T(8,128)(2,1)S(1)}, u32[]{:S(2)}, u32[]{:S(2)}) collective-permute-start(bf16[256,768]{1,0:T(8,128)(2,1)S(1)} %collective-permute-done.6.refs_1_), channel_id=1, source_target_pairs={{0,64},{32,480},{64,128},{96,32},{128,192},{160,96},{192,256},{224... | collective-permute-start | bytes 1179656 | tf_op jit(solution)/shard_map/ppermute | solution.py:261
  61.6 11.2 %collective-permute-start.3 = (bf16[256,768]{1,0:T(8,128)(2,1)S(1)}, bf16[256,768]{1,0:T(8,128)(2,1)S(1)}, u32[]{:S(2)}, u32[]{:S(2)}) collective-permute-start(bf16[256,768]{1,0:T(8,128)(2,1)S(1)} %collective-permute-done.2), channel_id=1, source_target_pairs={{0,64},{32,480},{64,128},{96,32},{128,192},{160,96},{192,256},{224... | collective-permute-start | bytes 1179656 | tf_op jit(solution)/shard_map/ppermute | solution.py:266
  66.6 11.3 %collective-permute-start.10 = (bf16[256,768]{1,0:T(8,128)(2,1)S(1)}, bf16[256,768]{1,0:T(8,128)(2,1)S(1)}, u32[]{:S(2)}, u32[]{:S(2)}) collective-permute-start(bf16[256,768]{1,0:T(8,128)(2,1)S(1)} %collective-permute-done.1), channel_id=1, source_target_pairs={{0,32},{32,0},{64,96},{96,64},{128,160},{160,128},{192,224},{224,1... | collective-permute-start | bytes 1179656 | tf_op jit(solution)/shard_map/ppermute | solution.py:264
  69.2 14.6 %collective-permute-start.8 = (bf16[256,768]{1,0:T(8,128)(2,1)S(1)}, bf16[256,768]{1,0:T(8,128)(2,1)S(1)}, u32[]{:S(2)}, u32[]{:S(2)}) collective-permute-start(bf16[256,768]{1,0:T(8,128)(2,1)S(1)} %collective-permute-done.7.refs_2_), channel_id=1, source_target_pairs={{0,64},{32,480},{64,128},{96,32},{128,192},{160,96},{192,256},{224... | collective-permute-start | bytes 1179656 | tf_op jit(solution)/shard_map/ppermute | solution.py:265
  72.7 11.1 %collective-permute-start.9 = (bf16[256,768]{1,0:T(8,128)(2,1)S(1)}, bf16[256,768]{1,0:T(8,128)(2,1)S(1)}, u32[]{:S(2)}, u32[]{:S(2)}) collective-permute-start(bf16[256,768]{1,0:T(8,128)(2,1)S(1)} %collective-permute-done.3), channel_id=1, source_target_pairs={{0,96},{32,448},{64,160},{96,0},{128,224},{160,64},{192,288},{224,... | collective-permute-start | bytes 1179656 | tf_op jit(solution)/shard_map/ppermute | solution.py:267
  75.9 8.7 %collective-permute-start.4 = (bf16[256,768]{1,0:T(8,128)(2,1)S(1)}, bf16[256,768]{1,0:T(8,128)(2,1)S(1)}, u32[]{:S(2)}, u32[]{:S(2)}) collective-permute-start(bf16[256,768]{1,0:T(8,128)(2,1)S(1)} %collective-permute-done.2), channel_id=1, source_target_pairs={{0,32},{32,0},{64,96},{96,64},{128,160},{160,128},{192,224},{224,1... | collective-permute-start | bytes 1179656 | tf_op jit(solution)/shard_map/ppermute | solution.py:269
  77.9 6.8 %collective-permute-start.5 = (bf16[256,768]{1,0:T(8,128)(2,1)S(1)}, bf16[256,768]{1,0:T(8,128)(2,1)S(1)}, u32[]{:S(2)}, u32[]{:S(2)}) collective-permute-start(bf16[256,768]{1,0:T(8,128)(2,1)S(1)} %collective-permute-done.3), channel_id=1, source_target_pairs={{0,32},{32,0},{64,96},{96,64},{128,160},{160,128},{192,224},{224,1... | collective-permute-start | bytes 1179656 | tf_op jit(solution)/shard_map/ppermute | solution.py:270
  80.3 2.0 %copy-start = (bf16[8,576,384]{2,1,0:T(8,128)(2,1)S(1)}, bf16[8,576,384]{2,1,0:T(8,128)(2,1)}, u32[]{:S(2)}) copy-start(bf16[8,576,384]{2,1,0:T(8,128)(2,1)} %pack.1.refs_4_.refs_2_.own_w) | copy-start | bytes 10616836
  109.3 3.8 %collective-permute-start.11 = (bf16[28,256]{1,0:T(8,128)(2,1)S(1)}, bf16[28,256]{1,0:T(8,128)(2,1)S(1)}, u32[]{:S(2)}, u32[]{:S(2)}) collective-permute-start(bf16[28,256]{1,0:T(8,128)(2,1)S(1)} %slice), channel_id=1, source_target_pairs={{0,64},{64,128},{128,192},{192,256},{256,320},{320,384},{384,448},... | collective-permute-start | bytes 43016

commit v6 on v5

--- a/solution.py
+++ b/solution.py
@@ -129,10 +129,16 @@
         sums[i][2 * HID :, :] = totals[i][1]
 
 
-def backward_kernel(own_w, peer_w, own_sum, peer_sum, out_ref, terms):
+def backward_kernel(
+    places, me_ref, first_ref, second_ref, own_w, peer_w, own_sum, peer_sum, out_ref, terms
+):
     weights = own_w, peer_w
     chips = own_w.shape[0]
     totals = [(ref[: 2 * HID, :], ref[2 * HID :, :]) for ref in (own_sum, peer_sum)]
+    for ref, place in zip((first_ref, second_ref), places):
+        chip = chip_of(me_ref, place, chips)
+        for i in range(2):
+            totals[i] = project(weights[i][chip], ref[...], totals[i])
     grads, probs = [], []
     for pre, back in totals:
         pre_gate, pre_up = pre[:HID], pre[HID:]
@@ -256,19 +262,6 @@
 
     rows, own_w = after(rows, own_w)
     peer_w = lax.ppermute(own_w, "grp", swap)
-    mine1 = lax.ppermute(rows, "grp", up)
-    other1 = lax.ppermute(rows, "grp", cross)
-    mine2 = lax.ppermute(mine1, "grp", up)
-    other2 = lax.ppermute(other1, "grp", up)
-    other1, mine2 = after(other1, mine2)
-    came1 = lax.ppermute(other1, "grp", swap)
-    mine3 = lax.ppermute(mine2, "grp", up)
-    other3 = lax.ppermute(other2, "grp", up)
-    came4 = lax.ppermute(other3, "grp", leave)
-    other2, other3 = after(other2, other3)
-    came2 = lax.ppermute(other2, "grp", swap)
-    came3 = lax.ppermute(other3, "grp", swap)
-
     def forward(blocks, places, sums):
         n = len(blocks)
         return pl.pallas_call(
@@ -285,18 +278,32 @@
             name="forward",
         )(me_arg, *blocks, own_w, peer_w, *sums)
 
-    sums = forward([rows, mine1, mine2, came1], (0, -1, -2, 1), ())
+    mine1 = lax.ppermute(rows, "grp", up)
+    other1 = lax.ppermute(rows, "grp", cross)
+    mine2 = lax.ppermute(mine1, "grp", up)
+    other2 = lax.ppermute(other1, "grp", up)
+    other1, mine2 = after(other1, mine2)
+    came1 = lax.ppermute(other1, "grp", swap)
+    mine3 = lax.ppermute(mine2, "grp", up)
+    sums = forward([rows, mine1], (0, -1), ())
+    other2, sums = after(other2, sums)
+    other3 = lax.ppermute(other2, "grp", up)
+    came4 = lax.ppermute(other3, "grp", leave)
+    other2, other3 = after(other2, other3)
+    came2 = lax.ppermute(other2, "grp", swap)
+    came3 = lax.ppermute(other3, "grp", swap)
+
+    sums = forward([mine2, came1], (-2, 1), sums)
     sums = forward([mine3, came4], (-3, 4), sums)
-    sums = forward([came2, came3], (2, 3), sums)
     terms = pl.pallas_call(
-        backward_kernel,
-        in_specs=[VMEM] * 4,
+        functools.partial(backward_kernel, (2, 3)),
+        in_specs=[SMEM] + [VMEM] * 6,
         out_specs=VMEM,
         out_shape=jax.ShapeDtypeStruct((groups * BACK, slots), BF16),
         scratch_shapes=[pltpu.VMEM((groups * BACK, slots), F32)],
         compiler_params=LARGE,
         name="backward",
-    )(own_w, peer_w, *sums)
+    )(me_arg, came2, came3, own_w, peer_w, *sums)
 
     same_core = [list(range(c, groups, 2)) for c in range(2)]
     part = lax.psum_scatter(

time: 137 us -> 136 us (level)
    ppermute x1, waiting for transfers between devices: 2.76 us -> 0.01 us  [per_device(): other2 = lax.ppermute(other1, 'grp', up)]
    ppermute x1, waiting for transfers between devices: 0.01 us -> 2.49 us  [per_device(): came4 = lax.ppermute(other3, 'grp', leave)]
    unnamed x14 -> x16, local copies, waits for them, and re-layouts: 3.92 us -> 3.92 us
where the time goes in v6:
time: 136 us
  blocking collectives  69.7 us (51%)
  starting transfers between devices  47.4 us (35%)
  Pallas kernels  10.5 us (8%)
  local copies, waits for them, and re-layouts  4.09 us (3%)
  waiting for transfers between devices  2.52 us (2%)
  between operations  1.65 us (1%)
    all_to_all x2, blocking collectives, exchange(): lax.all_to_all(rows.reshape(2 * experts, HALF, rows.shape[-1]), ('grp', '...  47.5 us
    unnamed x1, blocking collectives  22.1 us
    ppermute x1, starting transfers between devices, per_device(): other2 = lax.ppermute(other1, 'grp', up)  11.2 us
    ppermute x1, starting transfers between devices, per_device(): mine1 = lax.ppermute(rows, 'grp', up)  8.23 us
    ppermute x1, starting transfers between devices, per_device(): other3 = lax.ppermute(other2, 'grp', up)  4.9 us
    ppermute x1, starting transfers between devices, per_device(): other1 = lax.ppermute(rows, 'grp', cross)  4.36 us
    unnamed x16, local copies, waits for them, and re-layouts  3.92 us
    pallas_call x1, Pallas kernels, per_device(): pl.pallas_call(pack_kernel, in_specs=[HBM] * 3, out_specs=HBM, out_shape=...  3.58 us
  transfers between devices with their start and end apart: 12, of which 1 were waited for; matrix products, arithmetic and copies ran while one was open for 1% of the time, Pallas kernels for 2%

profile of v6, /device:TPU:1, one launch (start us, length us, event | category | flops | bytes accessed | tf_op | source)
XLA Modules:
  0.0 135.9 jit_solution(13904564441867044643)
XLA Ops:
  0.6 0.0 copy-start.2
  0.6 0.0 copy-start.3
  0.7 0.0 copy-start.4
  0.7 0.0 copy-start.5
  0.7 3.6 %pack.1.refs_2_.own_w = bf16[8,576,384]{2,1,0:T(8,128)(2,1)} custom-call(bf16[180,2880]{1,0:T(8,128)(2,1)} %bitcast.26, bf16[180,2880]{1,0:T(8,128)(2,1)} %bitcast.27, bf16[180,2880]{1,0:T(8,128)(2,1)} %bitcast.28), custom_call_target="tpu_custom_call" | custom-call | tf_op jit(solution)/shard_map/pack/pallas_call | solution.py:239
  4.3 0.0 copy-done.2
  4.3 0.0 copy-done.3
  4.3 0.0 copy-done.4
  4.3 0.0 copy-done.5
  4.3 0.5 dispatch.1
  4.8 26.1 %all_to_all.10 = bf16[64,8,384]{2,1,0:T(8,128)(2,1)S(1)} all-to-all(bf16[64,8,384]{2,1,0:T(8,128)(2,1)S(1)} %bitcast.20), channel_id=1, replica_groups={{0,1,2,3,4,5,6,7,8,9,10,11,12,13,14,15,16,17,18,19,20,21,22,23,24,25,26..., dimensions={0} | all-to-all | bytes 786432 | tf_op jit(solution)/shard_map/all_to_all | solution.py:219
  30.9 0.1 join.1.refs_0_
  31.1 1.9 %collective-permute-start.3 = (bf16[8,576,384]{2,1,0:T(8,128)(2,1)}, bf16[8,576,384]{2,1,0:T(8,128)(2,1)S(1)}, u32[]{:S(2)}, u32[]{:S(2)}) collective-permute-start(bf16[8,576,384]{2,1,0:T(8,128)(2,1)} %pack.1.refs_2_.own_w), channel_id=1, source_target_pairs={{0,32},{32,0},{64,96},{96,64},{128,160},{160,128},{192,224},{224,1... | collective-permute-start | bytes 10616840 | tf_op jit(solution)/shard_map/ppermute | solution.py:264
  33.0 4.4 %collective-permute-start = (bf16[256,768]{1,0:T(8,128)(2,1)S(1)}, bf16[256,768]{1,0:T(8,128)(2,1)S(1)}, u32[]{:S(2)}, u32[]{:S(2)}) collective-permute-start(bf16[256,768]{1,0:T(8,128)(2,1)S(1)} %join.1.refs_0_), channel_id=1, source_target_pairs={{32,64},{0,480},{96,128},{64,32},{160,192},{128,96},{224,256},{192... | collective-permute-start | bytes 1179656 | tf_op jit(solution)/shard_map/ppermute | solution.py:282
  37.4 8.2 %collective-permute-start.2 = (bf16[256,768]{1,0:T(8,128)(2,1)S(1)}, bf16[256,768]{1,0:T(8,128)(2,1)S(1)}, u32[]{:S(2)}, u32[]{:S(2)}) collective-permute-start(bf16[256,768]{1,0:T(8,128)(2,1)S(1)} %join.1.refs_0_), channel_id=1, source_target_pairs={{0,64},{32,480},{64,128},{96,32},{128,192},{160,96},{192,256},{224... | collective-permute-start | bytes 1179656 | tf_op jit(solution)/shard_map/ppermute | solution.py:281
  45.6 0.0 collective-permute-done
  45.7 11.2 %collective-permute-start.1 = (bf16[256,768]{1,0:T(8,128)(2,1)S(1)}, bf16[256,768]{1,0:T(8,128)(2,1)S(1)}, u32[]{:S(2)}, u32[]{:S(2)}) collective-permute-start(bf16[256,768]{1,0:T(8,128)(2,1)S(1)} %collective-permute-done), channel_id=1, source_target_pairs={{0,64},{32,480},{64,128},{96,32},{128,192},{160,96},{192,256},{224... | collective-permute-start | bytes 1179656 | tf_op jit(solution)/shard_map/ppermute | solution.py:284
  56.8 0.0 collective-permute-done.2.refs_1_
  56.8 1.9 %collective-permute-start.7 = (bf16[256,768]{1,0:T(8,128)(2,1)S(1)}, bf16[256,768]{1,0:T(8,128)(2,1)S(1)}, u32[]{:S(2)}, u32[]{:S(2)}) collective-permute-start(bf16[256,768]{1,0:T(8,128)(2,1)S(1)} %collective-permute-done.2.refs_1_), channel_id=1, source_target_pairs={{0,64},{32,480},{64,128},{96,32},{128,192},{160,96},{192,256},{224... | collective-permute-start | bytes 1179656 | tf_op jit(solution)/shard_map/ppermute | solution.py:283
  58.8 0.0 collective-permute-done.3.refs_3_.peer_w
  58.8 0.0 copy-start
  58.8 2.0 %copy-done = bf16[8,576,384]{2,1,0:T(8,128)(2,1)S(1)} copy-done((bf16[8,576,384]{2,1,0:T(8,128)(2,1)S(1)}, bf16[8,576,384]{2,1,0:T(8,128)(2,1)}, u32[]{:S(2)}) %copy-start) | copy-done | bytes 3538968
  60.8 0.0 copy-start.1
  60.8 0.8 forward.3
  61.6 0.0 collective-permute-done.1
  61.6 4.9 %collective-permute-start.4 = (bf16[256,768]{1,0:T(8,128)(2,1)S(1)}, bf16[256,768]{1,0:T(8,128)(2,1)S(1)}, u32[]{:S(2)}, u32[]{:S(2)}) collective-permute-start(bf16[256,768]{1,0:T(8,128)(2,1)S(1)} %collective-permute-done.1), channel_id=1, source_target_pairs={{0,64},{32,480},{64,128},{96,32},{128,192},{160,96},{192,256},{224... | collective-permute-start | bytes 1179656 | tf_op jit(solution)/shard_map/ppermute | solution.py:290
  66.5 0.0 collective-permute-done.7.refs_0_
  66.6 2.6 %collective-permute-start.10 = (bf16[256,768]{1,0:T(8,128)(2,1)S(1)}, bf16[256,768]{1,0:T(8,128)(2,1)S(1)}, u32[]{:S(2)}, u32[]{:S(2)}) collective-permute-start(bf16[256,768]{1,0:T(8,128)(2,1)S(1)} %collective-permute-done), channel_id=1, source_target_pairs={{0,32},{32,0},{64,96},{96,64},{128,160},{160,128},{192,224},{224,1... | collective-permute-start | bytes 1179656 | tf_op jit(solution)/shard_map/ppermute | solution.py:286
  69.2 3.5 %collective-permute-start.8 = (bf16[256,768]{1,0:T(8,128)(2,1)S(1)}, bf16[256,768]{1,0:T(8,128)(2,1)S(1)}, u32[]{:S(2)}, u32[]{:S(2)}) collective-permute-start(bf16[256,768]{1,0:T(8,128)(2,1)S(1)} %collective-permute-done.7.refs_0_), channel_id=1, source_target_pairs={{0,64},{32,480},{64,128},{96,32},{128,192},{160,96},{192,256},{224... | collective-permute-start | bytes 1179656 | tf_op jit(solution)/shard_map/ppermute | solution.py:287
  72.7 0.0 collective-permute-done.4
  72.7 3.2 %collective-permute-start.9 = (bf16[256,768]{1,0:T(8,128)(2,1)S(1)}, bf16[256,768]{1,0:T(8,128)(2,1)S(1)}, u32[]{:S(2)}, u32[]{:S(2)}) collective-permute-start(bf16[256,768]{1,0:T(8,128)(2,1)S(1)} %collective-permute-done.4), channel_id=1, source_target_pairs={{0,96},{32,448},{64,160},{96,0},{128,224},{160,64},{192,288},{224,... | collective-permute-start | bytes 1179656 | tf_op jit(solution)/shard_map/ppermute | solution.py:291
  75.9 1.9 %collective-permute-start.5 = (bf16[256,768]{1,0:T(8,128)(2,1)S(1)}, bf16[256,768]{1,0:T(8,128)(2,1)S(1)}, u32[]{:S(2)}, u32[]{:S(2)}) collective-permute-start(bf16[256,768]{1,0:T(8,128)(2,1)S(1)} %collective-permute-done.1), channel_id=1, source_target_pairs={{0,32},{32,0},{64,96},{96,64},{128,160},{160,128},{192,224},{224,1... | collective-permute-start | bytes 1179656 | tf_op jit(solution)/shard_map/ppermute | solution.py:293
  77.8 2.4 %collective-permute-start.6 = (bf16[256,768]{1,0:T(8,128)(2,1)S(1)}, bf16[256,768]{1,0:T(8,128)(2,1)S(1)}, u32[]{:S(2)}, u32[]{:S(2)}) collective-permute-start(bf16[256,768]{1,0:T(8,128)(2,1)S(1)} %collective-permute-done.4), channel_id=1, source_target_pairs={{0,32},{32,0},{64,96},{96,64},{128,160},{160,128},{192,224},{224,1... | collective-permute-start | bytes 1179656 | tf_op jit(solution)/shard_map/ppermute | solution.py:294
  80.2 0.0 collective-permute-done.10.refs_1_
  80.2 0.0 copy-done.1
  80.2 0.9 forward.4
  81.1 0.0 collective-permute-done.8.refs_0_
  81.1 2.5 %collective-permute-done.9.refs_1_ = bf16[256,768]{1,0:T(8,128)(2,1)S(1)} collective-permute-done((bf16[256,768]{1,0:T(8,128)(2,1)S(1)}, bf16[256,768]{1,0:T(8,128)(2,1)S(1)}, u32[]{:S(2)}, u32[]{:S(2)}) %collective-permute-start.9) | collective-permute-done | bytes 393248 | tf_op jit(solution)/shard_map/ppermute | solution.py:291
  83.6 0.8 forward.5
  84.5 0.0 collective-permute-done.5.first_ref
  84.5 0.0 collective-permute-done.6.second_ref
  84.5 2.7 %backward.1 = bf16[2912,256]{1,0:T(8,128)(2,1)S(1)} custom-call(s32[1]{0:T(128)} %bitcast.1.me_ref, bf16[256,768]{1,0:T(8,128)(2,1)S(1)} %collective-permute-done.5.first_ref, bf16[256,768]{1,0:T(8,128)(2,1)S(1)} %collective-permute-done.6.second_ref, bf16[8,576,384]{2,1,0:T(8,128)(2,1)S(1)} %copy-done.1, ...), custom_call_target="tpu_custom_call" | custom-call | tf_op jit(solution)/shard_map/backward/pallas_call | solution.py:298
  87.2 22.1 %fusion = bf16[368,256]{1,0:T(8,128)(2,1)S(1)} fusion(bf16[2912,256]{1,0:T(8,128)(2,1)S(1)} %backward.1), kind=kCustom, calls=%all-reduce-scatter | all-reduce-scatter fusion | flops 753665 | bytes 1681408
  109.4 1.3 collective-permute-start.11
  110.7 1.3 dynamic-slice.4
  112.6 0.0 collective-permute-done.11
  112.6 0.6 concatenate
  113.2 0.1 constant_dynamic-slice_fusion
  113.3 0.1 copy.11
  113.5 21.4 %all_to_all.11 = bf16[64,8,182]{2,1,0:T(8,128)(2,1)S(1)} all-to-all(bf16[64,8,182]{2,1,0:T(8,128)(2,1)S(1)} %bitcast.29), channel_id=1, replica_groups={{0,1,2,3,4,5,6,7,8,9,10,11,12,13,14,15,16,17,18,19,20,21,22,23,24,25,26..., dimensions={0} | all-to-all | bytes 372736 | tf_op jit(solution)/shard_map/all_to_all | solution.py:219
  134.8 1.0 combine.1
  (2 shorter events, 0.0 us)
Async XLA Ops:
  0.6 3.6 %copy-start.2 = (bf16[256,180]{0,1:T(8,128)(2,1)S(1)}, bf16[256,180]{0,1:T(8,128)(2,1)}, u32[]{:S(2)}) copy-start(bf16[256,180]{0,1:T(8,128)(2,1)} %param.7) | copy-start | bytes 276484
  0.6 3.6 %copy-start.3 = (bf16[256,180]{0,1:T(8,128)(2,1)S(1)}, bf16[256,180]{0,1:T(8,128)(2,1)}, u32[]{:S(2)}) copy-start(bf16[256,180]{0,1:T(8,128)(2,1)} %param.8) | copy-start | bytes 276484
  0.7 3.6 %copy-start.4 = (s32[256,4]{0,1:T(4,128)S(1)}, s32[256,4]{0,1:T(4,128)}, u32[]{:S(2)}) copy-start(s32[256,4]{0,1:T(4,128)} %param.9) | copy-start | bytes 12292
  0.7 3.6 %copy-start.5 = (bf16[256,4]{0,1:T(4,128)(2,1)S(1)}, bf16[256,4]{0,1:T(4,128)(2,1)}, u32[]{:S(2)}) copy-start(bf16[256,4]{0,1:T(4,128)(2,1)} %param.10) | copy-start | bytes 6148
  31.1 27.7 %collective-permute-start.3 = (bf16[8,576,384]{2,1,0:T(8,128)(2,1)}, bf16[8,576,384]{2,1,0:T(8,128)(2,1)S(1)}, u32[]{:S(2)}, u32[]{:S(2)}) collective-permute-start(bf16[8,576,384]{2,1,0:T(8,128)(2,1)} %pack.1.refs_2_.own_w), channel_id=1, source_target_pairs={{0,32},{32,0},{64,96},{96,64},{128,160},{160,128},{192,224},{224,1... | collective-permute-start | bytes 10616840 | tf_op jit(solution)/shard_map/ppermute | solution.py:264
  33.0 12.6 %collective-permute-start = (bf16[256,768]{1,0:T(8,128)(2,1)S(1)}, bf16[256,768]{1,0:T(8,128)(2,1)S(1)}, u32[]{:S(2)}, u32[]{:S(2)}) collective-permute-start(bf16[256,768]{1,0:T(8,128)(2,1)S(1)} %join.1.refs_0_), channel_id=1, source_target_pairs={{32,64},{0,480},{96,128},{64,32},{160,192},{128,96},{224,256},{192... | collective-permute-start | bytes 1179656 | tf_op jit(solution)/shard_map/ppermute | solution.py:282
  37.4 19.4 %collective-permute-start.2 = (bf16[256,768]{1,0:T(8,128)(2,1)S(1)}, bf16[256,768]{1,0:T(8,128)(2,1)S(1)}, u32[]{:S(2)}, u32[]{:S(2)}) collective-permute-start(bf16[256,768]{1,0:T(8,128)(2,1)S(1)} %join.1.refs_0_), channel_id=1, source_target_pairs={{0,64},{32,480},{64,128},{96,32},{128,192},{160,96},{192,256},{224... | collective-permute-start | bytes 1179656 | tf_op jit(solution)/shard_map/ppermute | solution.py:281
  45.7 16.0 %collective-permute-start.1 = (bf16[256,768]{1,0:T(8,128)(2,1)S(1)}, bf16[256,768]{1,0:T(8,128)(2,1)S(1)}, u32[]{:S(2)}, u32[]{:S(2)}) collective-permute-start(bf16[256,768]{1,0:T(8,128)(2,1)S(1)} %collective-permute-done), channel_id=1, source_target_pairs={{0,64},{32,480},{64,128},{96,32},{128,192},{160,96},{192,256},{224... | collective-permute-start | bytes 1179656 | tf_op jit(solution)/shard_map/ppermute | solution.py:284
  56.8 9.7 %collective-permute-start.7 = (bf16[256,768]{1,0:T(8,128)(2,1)S(1)}, bf16[256,768]{1,0:T(8,128)(2,1)S(1)}, u32[]{:S(2)}, u32[]{:S(2)}) collective-permute-start(bf16[256,768]{1,0:T(8,128)(2,1)S(1)} %collective-permute-done.2.refs_1_), channel_id=1, source_target_pairs={{0,64},{32,480},{64,128},{96,32},{128,192},{160,96},{192,256},{224... | collective-permute-start | bytes 1179656 | tf_op jit(solution)/shard_map/ppermute | solution.py:283
  58.8 2.0 %copy-start = (bf16[8,576,384]{2,1,0:T(8,128)(2,1)S(1)}, bf16[8,576,384]{2,1,0:T(8,128)(2,1)}, u32[]{:S(2)}) copy-start(bf16[8,576,384]{2,1,0:T(8,128)(2,1)} %pack.1.refs_2_.own_w) | copy-start | bytes 10616836
  60.8 19.5 %copy-start.1 = (bf16[8,576,384]{2,1,0:T(8,128)(2,1)S(1)}, bf16[8,576,384]{2,1,0:T(8,128)(2,1)}, u32[]{:S(2)}) copy-start(bf16[8,576,384]{2,1,0:T(8,128)(2,1)} %pack.1.refs_2_.own_w) | copy-start | bytes 10616836
  61.6 11.0 %collective-permute-start.4 = (bf16[256,768]{1,0:T(8,128)(2,1)S(1)}, bf16[256,768]{1,0:T(8,128)(2,1)S(1)}, u32[]{:S(2)}, u32[]{:S(2)}) collective-permute-start(bf16[256,768]{1,0:T(8,128)(2,1)S(1)} %collective-permute-done.1), channel_id=1, source_target_pairs={{0,64},{32,480},{64,128},{96,32},{128,192},{160,96},{192,256},{224... | collective-permute-start | bytes 1179656 | tf_op jit(solution)/shard_map/ppermute | solution.py:290
  66.6 13.7 %collective-permute-start.10 = (bf16[256,768]{1,0:T(8,128)(2,1)S(1)}, bf16[256,768]{1,0:T(8,128)(2,1)S(1)}, u32[]{:S(2)}, u32[]{:S(2)}) collective-permute-start(bf16[256,768]{1,0:T(8,128)(2,1)S(1)} %collective-permute-done), channel_id=1, source_target_pairs={{0,32},{32,0},{64,96},{96,64},{128,160},{160,128},{192,224},{224,1... | collective-permute-start | bytes 1179656 | tf_op jit(solution)/shard_map/ppermute | solution.py:286
  69.2 11.9 %collective-permute-start.8 = (bf16[256,768]{1,0:T(8,128)(2,1)S(1)}, bf16[256,768]{1,0:T(8,128)(2,1)S(1)}, u32[]{:S(2)}, u32[]{:S(2)}) collective-permute-start(bf16[256,768]{1,0:T(8,128)(2,1)S(1)} %collective-permute-done.7.refs_0_), channel_id=1, source_target_pairs={{0,64},{32,480},{64,128},{96,32},{128,192},{160,96},{192,256},{224... | collective-permute-start | bytes 1179656 | tf_op jit(solution)/shard_map/ppermute | solution.py:287
  72.7 10.9 %collective-permute-start.9 = (bf16[256,768]{1,0:T(8,128)(2,1)S(1)}, bf16[256,768]{1,0:T(8,128)(2,1)S(1)}, u32[]{:S(2)}, u32[]{:S(2)}) collective-permute-start(bf16[256,768]{1,0:T(8,128)(2,1)S(1)} %collective-permute-done.4), channel_id=1, source_target_pairs={{0,96},{32,448},{64,160},{96,0},{128,224},{160,64},{192,288},{224,... | collective-permute-start | bytes 1179656 | tf_op jit(solution)/shard_map/ppermute | solution.py:291
  75.9 8.6 %collective-permute-start.5 = (bf16[256,768]{1,0:T(8,128)(2,1)S(1)}, bf16[256,768]{1,0:T(8,128)(2,1)S(1)}, u32[]{:S(2)}, u32[]{:S(2)}) collective-permute-start(bf16[256,768]{1,0:T(8,128)(2,1)S(1)} %collective-permute-done.1), channel_id=1, source_target_pairs={{0,32},{32,0},{64,96},{96,64},{128,160},{160,128},{192,224},{224,1... | collective-permute-start | bytes 1179656 | tf_op jit(solution)/shard_map/ppermute | solution.py:293
  77.8 6.7 %collective-permute-start.6 = (bf16[256,768]{1,0:T(8,128)(2,1)S(1)}, bf16[256,768]{1,0:T(8,128)(2,1)S(1)}, u32[]{:S(2)}, u32[]{:S(2)}) collective-permute-start(bf16[256,768]{1,0:T(8,128)(2,1)S(1)} %collective-permute-done.4), channel_id=1, source_target_pairs={{0,32},{32,0},{64,96},{96,64},{128,160},{160,128},{192,224},{224,1... | collective-permute-start | bytes 1179656 | tf_op jit(solution)/shard_map/ppermute | solution.py:294
  109.4 3.2 %collective-permute-start.11 = (bf16[28,256]{1,0:T(8,128)(2,1)S(1)}, bf16[28,256]{1,0:T(8,128)(2,1)S(1)}, u32[]{:S(2)}, u32[]{:S(2)}) collective-permute-start(bf16[28,256]{1,0:T(8,128)(2,1)S(1)} %slice), channel_id=1, source_target_pairs={{0,64},{64,128},{128,192},{192,256},{256,320},{320,384},{384,448},... | collective-permute-start | bytes 43016

commit v7 on v6

--- a/solution.py
+++ b/solution.py
@@ -130,7 +130,7 @@
 
 
 def backward_kernel(
-    places, me_ref, first_ref, second_ref, own_w, peer_w, own_sum, peer_sum, out_ref, terms
+    places, me_ref, first_ref, second_ref, own_w, peer_w, own_sum, peer_sum, out_ref
 ):
     weights = own_w, peer_w
     chips = own_w.shape[0]
@@ -157,18 +157,14 @@
     d_gate = jnp.where(row == HIDDEN, high, grads[0][0])
     grads[0][0] = jnp.where(row == HIDDEN + 1, prob - high, d_gate)
     grads = [jnp.concatenate(g, axis=0).astype(BF16) for g in grads]
+    grad = jnp.concatenate(grads, axis=0)
     for k in range(chips):
-        value = None
-        for i in range(2):
-            term = lax.dot_general(
-                weights[i][k, : 2 * HID, :], grads[i], TN, preferred_element_type=F32
-            )
-            value = term if value is None else value + term
+        w = jnp.concatenate([ref[k, : 2 * HID, :] for ref in weights], axis=0)
+        value = lax.dot_general(w, grad, TN, preferred_element_type=F32).astype(BF16)
         for part in range(2):
             start = (2 * k + part) * BACK
-            terms[start : start + FEATS, :] = value[part * FEATS : (part + 1) * FEATS, :]
-            terms[start + FEATS : start + BACK, :] = value[CHIP : CHIP + 2, :]
-    out_ref[...] = terms[...].astype(BF16)
+            out_ref[start : start + FEATS, :] = value[part * FEATS : (part + 1) * FEATS, :]
+            out_ref[start + FEATS : start + BACK, :] = value[CHIP : CHIP + 2, :]
 
 
 def combine_kernel(ret_ref, sel_ref, ids_ref, tok_ref, gate_ref):
@@ -293,14 +289,13 @@
     came2 = lax.ppermute(other2, "grp", swap)
     came3 = lax.ppermute(other3, "grp", swap)
 
-    sums = forward([mine2, came1], (-2, 1), sums)
-    sums = forward([mine3, came4], (-3, 4), sums)
+    sums = forward([mine2, came1, mine3], (-2, 1, -3), sums)
+    sums = forward([came4], (4,), sums)
     terms = pl.pallas_call(
         functools.partial(backward_kernel, (2, 3)),
         in_specs=[SMEM] + [VMEM] * 6,
         out_specs=VMEM,
         out_shape=jax.ShapeDtypeStruct((groups * BACK, slots), BF16),
-        scratch_shapes=[pltpu.VMEM((groups * BACK, slots), F32)],
         compiler_params=LARGE,
         name="backward",
     )(me_arg, came2, came3, own_w, peer_w, *sums)

time: 136 us -> 135 us (level)
    unnamed x1, blocking collectives: 22.1 us -> 20.6 us
where the time goes in v7:
time: 135 us
  blocking collectives  69.3 us (51%)
  starting transfers between devices  48 us (36%)
  Pallas kernels  10.2 us (8%)
  local copies, waits for them, and re-layouts  4.09 us (3%)
  between operations  1.64 us (1%)
  waiting for transfers between devices  1.59 us (1%)
    all_to_all x2, blocking collectives, exchange(): lax.all_to_all(rows.reshape(2 * experts, HALF, rows.shape[-1]), ('grp', '...  48.7 us
    unnamed x1, blocking collectives  20.6 us
    ppermute x1, starting transfers between devices, per_device(): other2 = lax.ppermute(other1, 'grp', up)  11.2 us
    ppermute x1, starting transfers between devices, per_device(): mine1 = lax.ppermute(rows, 'grp', up)  8.23 us
    ppermute x1, starting transfers between devices, per_device(): other3 = lax.ppermute(other2, 'grp', up)  4.9 us
    ppermute x1, starting transfers between devices, per_device(): other1 = lax.ppermute(rows, 'grp', cross)  4.36 us
    ppermute x1, starting transfers between devices, per_device(): mine3 = lax.ppermute(mine2, 'grp', up)  4.19 us
    unnamed x16, local copies, waits for them, and re-layouts  3.92 us
  transfers between devices with their start and end apart: 12, of which 1 were waited for; matrix products, arithmetic and copies ran while one was open for 1% of the time, Pallas kernels for 2%

profile of v7, /device:TPU:1, one launch (start us, length us, event | category | flops | bytes accessed | tf_op | source)
XLA Modules:
  0.0 134.7 jit_solution(16424840136169049887)
XLA Ops:
  0.6 0.0 copy-start.2
  0.6 0.0 copy-start.3
  0.7 0.0 copy-start.4
  0.7 0.0 copy-start.5
  0.7 3.6 %pack.1.refs_2_.refs_3_.refs_1_.own_w = bf16[8,576,384]{2,1,0:T(8,128)(2,1)} custom-call(bf16[180,2880]{1,0:T(8,128)(2,1)} %bitcast.26, bf16[180,2880]{1,0:T(8,128)(2,1)} %bitcast.27, bf16[180,2880]{1,0:T(8,128)(2,1)} %bitcast.28), custom_call_target="tpu_custom_call" | custom-call | tf_op jit(solution)/shard_map/pack/pallas_call | solution.py:235
  4.3 0.0 copy-done.2
  4.3 0.0 copy-done.3
  4.3 0.0 copy-done.4
  4.3 0.0 copy-done.5
  4.3 0.5 dispatch.1
  4.8 26.1 %all_to_all.10 = bf16[64,8,384]{2,1,0:T(8,128)(2,1)S(1)} all-to-all(bf16[64,8,384]{2,1,0:T(8,128)(2,1)S(1)} %bitcast.20), channel_id=1, replica_groups={{0,1,2,3,4,5,6,7,8,9,10,11,12,13,14,15,16,17,18,19,20,21,22,23,24,25,26..., dimensions={0} | all-to-all | bytes 786432 | tf_op jit(solution)/shard_map/all_to_all | solution.py:215
  30.9 0.1 join.1.refs_0_
  31.1 1.9 %collective-permute-start.3 = (bf16[8,576,384]{2,1,0:T(8,128)(2,1)}, bf16[8,576,384]{2,1,0:T(8,128)(2,1)S(1)}, u32[]{:S(2)}, u32[]{:S(2)}) collective-permute-start(bf16[8,576,384]{2,1,0:T(8,128)(2,1)} %pack.1.refs_2_.refs_3_.refs_1_.own_w), channel_id=1, source_target_pairs={{0,32},{32,0},{64,96},{96,64},{128,160},{160,128},{192,224},{224,1... | collective-permute-start | bytes 10616840 | tf_op jit(solution)/shard_map/ppermute | solution.py:260
  33.0 4.4 %collective-permute-start = (bf16[256,768]{1,0:T(8,128)(2,1)S(1)}, bf16[256,768]{1,0:T(8,128)(2,1)S(1)}, u32[]{:S(2)}, u32[]{:S(2)}) collective-permute-start(bf16[256,768]{1,0:T(8,128)(2,1)S(1)} %join.1.refs_0_), channel_id=1, source_target_pairs={{32,64},{0,480},{96,128},{64,32},{160,192},{128,96},{224,256},{192... | collective-permute-start | bytes 1179656 | tf_op jit(solution)/shard_map/ppermute | solution.py:278
  37.4 8.2 %collective-permute-start.2 = (bf16[256,768]{1,0:T(8,128)(2,1)S(1)}, bf16[256,768]{1,0:T(8,128)(2,1)S(1)}, u32[]{:S(2)}, u32[]{:S(2)}) collective-permute-start(bf16[256,768]{1,0:T(8,128)(2,1)S(1)} %join.1.refs_0_), channel_id=1, source_target_pairs={{0,64},{32,480},{64,128},{96,32},{128,192},{160,96},{192,256},{224... | collective-permute-start | bytes 1179656 | tf_op jit(solution)/shard_map/ppermute | solution.py:277
  45.6 0.0 collective-permute-done
  45.7 11.2 %collective-permute-start.1 = (bf16[256,768]{1,0:T(8,128)(2,1)S(1)}, bf16[256,768]{1,0:T(8,128)(2,1)S(1)}, u32[]{:S(2)}, u32[]{:S(2)}) collective-permute-start(bf16[256,768]{1,0:T(8,128)(2,1)S(1)} %collective-permute-done), channel_id=1, source_target_pairs={{0,64},{32,480},{64,128},{96,32},{128,192},{160,96},{192,256},{224... | collective-permute-start | bytes 1179656 | tf_op jit(solution)/shard_map/ppermute | solution.py:280
  56.8 0.0 collective-permute-done.2.refs_1_
  56.8 1.9 %collective-permute-start.8 = (bf16[256,768]{1,0:T(8,128)(2,1)S(1)}, bf16[256,768]{1,0:T(8,128)(2,1)S(1)}, u32[]{:S(2)}, u32[]{:S(2)}) collective-permute-start(bf16[256,768]{1,0:T(8,128)(2,1)S(1)} %collective-permute-done.2.refs_1_), channel_id=1, source_target_pairs={{0,64},{32,480},{64,128},{96,32},{128,192},{160,96},{192,256},{224... | collective-permute-start | bytes 1179656 | tf_op jit(solution)/shard_map/ppermute | solution.py:279
  58.8 0.0 collective-permute-done.3.refs_3_.refs_4_.refs_2_.peer_w
  58.8 0.0 copy-start
  58.8 2.0 %copy-done = bf16[8,576,384]{2,1,0:T(8,128)(2,1)S(1)} copy-done((bf16[8,576,384]{2,1,0:T(8,128)(2,1)S(1)}, bf16[8,576,384]{2,1,0:T(8,128)(2,1)}, u32[]{:S(2)}) %copy-start) | copy-done | bytes 3538968
  60.8 0.0 copy-start.1
  60.8 0.8 forward.3
  61.6 0.0 collective-permute-done.1
  61.6 4.9 %collective-permute-start.4 = (bf16[256,768]{1,0:T(8,128)(2,1)S(1)}, bf16[256,768]{1,0:T(8,128)(2,1)S(1)}, u32[]{:S(2)}, u32[]{:S(2)}) collective-permute-start(bf16[256,768]{1,0:T(8,128)(2,1)S(1)} %collective-permute-done.1), channel_id=1, source_target_pairs={{0,64},{32,480},{64,128},{96,32},{128,192},{160,96},{192,256},{224... | collective-permute-start | bytes 1179656 | tf_op jit(solution)/shard_map/ppermute | solution.py:286
  66.5 0.0 collective-permute-done.8.refs_0_
  66.6 4.2 %collective-permute-start.10 = (bf16[256,768]{1,0:T(8,128)(2,1)S(1)}, bf16[256,768]{1,0:T(8,128)(2,1)S(1)}, u32[]{:S(2)}, u32[]{:S(2)}) collective-permute-start(bf16[256,768]{1,0:T(8,128)(2,1)S(1)} %collective-permute-done.8.refs_0_), channel_id=1, source_target_pairs={{0,64},{32,480},{64,128},{96,32},{128,192},{160,96},{192,256},{224... | collective-permute-start | bytes 1179656 | tf_op jit(solution)/shard_map/ppermute | solution.py:283
  70.8 1.9 %collective-permute-start.9 = (bf16[256,768]{1,0:T(8,128)(2,1)S(1)}, bf16[256,768]{1,0:T(8,128)(2,1)S(1)}, u32[]{:S(2)}, u32[]{:S(2)}) collective-permute-start(bf16[256,768]{1,0:T(8,128)(2,1)S(1)} %collective-permute-done), channel_id=1, source_target_pairs={{0,32},{32,0},{64,96},{96,64},{128,160},{160,128},{192,224},{224,1... | collective-permute-start | bytes 1179656 | tf_op jit(solution)/shard_map/ppermute | solution.py:282
  72.7 0.0 collective-permute-done.4
  72.7 3.2 %collective-permute-start.7 = (bf16[256,768]{1,0:T(8,128)(2,1)S(1)}, bf16[256,768]{1,0:T(8,128)(2,1)S(1)}, u32[]{:S(2)}, u32[]{:S(2)}) collective-permute-start(bf16[256,768]{1,0:T(8,128)(2,1)S(1)} %collective-permute-done.4), channel_id=1, source_target_pairs={{0,96},{32,448},{64,160},{96,0},{128,224},{160,64},{192,288},{224,... | collective-permute-start | bytes 1179656 | tf_op jit(solution)/shard_map/ppermute | solution.py:287
  75.9 1.9 %collective-permute-start.5 = (bf16[256,768]{1,0:T(8,128)(2,1)S(1)}, bf16[256,768]{1,0:T(8,128)(2,1)S(1)}, u32[]{:S(2)}, u32[]{:S(2)}) collective-permute-start(bf16[256,768]{1,0:T(8,128)(2,1)S(1)} %collective-permute-done.1), channel_id=1, source_target_pairs={{0,32},{32,0},{64,96},{96,64},{128,160},{160,128},{192,224},{224,1... | collective-permute-start | bytes 1179656 | tf_op jit(solution)/shard_map/ppermute | solution.py:289
  77.8 2.4 %collective-permute-start.6 = (bf16[256,768]{1,0:T(8,128)(2,1)S(1)}, bf16[256,768]{1,0:T(8,128)(2,1)S(1)}, u32[]{:S(2)}, u32[]{:S(2)}) collective-permute-start(bf16[256,768]{1,0:T(8,128)(2,1)S(1)} %collective-permute-done.4), channel_id=1, source_target_pairs={{0,32},{32,0},{64,96},{96,64},{128,160},{160,128},{192,224},{224,1... | collective-permute-start | bytes 1179656 | tf_op jit(solution)/shard_map/ppermute | solution.py:290
  80.2 0.0 collective-permute-done.10.refs_2_
  80.2 0.0 collective-permute-done.9.refs_1_
  80.2 0.0 copy-done.1
  80.3 1.2 forward.4
  81.4 1.6 %collective-permute-done.7.refs_0_ = bf16[256,768]{1,0:T(8,128)(2,1)S(1)} collective-permute-done((bf16[256,768]{1,0:T(8,128)(2,1)S(1)}, bf16[256,768]{1,0:T(8,128)(2,1)S(1)}, u32[]{:S(2)}, u32[]{:S(2)}) %collective-permute-start.7) | collective-permute-done | bytes 393248 | tf_op jit(solution)/shard_map/ppermute | solution.py:287
  83.0 0.5 forward.5
  83.5 0.0 collective-permute-done.5.first_ref
  83.5 0.0 collective-permute-done.6.second_ref
  83.6 2.3 %backward.1 = bf16[2912,256]{1,0:T(8,128)(2,1)S(1)} custom-call(s32[1]{0:T(128)} %bitcast.1.me_ref, bf16[256,768]{1,0:T(8,128)(2,1)S(1)} %collective-permute-done.5.first_ref, bf16[256,768]{1,0:T(8,128)(2,1)S(1)} %collective-permute-done.6.second_ref, bf16[8,576,384]{2,1,0:T(8,128)(2,1)S(1)} %copy-done.1, ...), custom_call_target="tpu_custom_call" | custom-call | tf_op jit(solution)/shard_map/backward/pallas_call | solution.py:294
  85.9 20.6 %fusion = bf16[368,256]{1,0:T(8,128)(2,1)S(1)} fusion(bf16[2912,256]{1,0:T(8,128)(2,1)S(1)} %backward.1), kind=kCustom, calls=%all-reduce-scatter | all-reduce-scatter fusion | flops 753665 | bytes 1681408
  106.5 1.8 %collective-permute-start.11 = (bf16[28,256]{1,0:T(8,128)(2,1)S(1)}, bf16[28,256]{1,0:T(8,128)(2,1)S(1)}, u32[]{:S(2)}, u32[]{:S(2)}) collective-permute-start(bf16[28,256]{1,0:T(8,128)(2,1)S(1)} %slice), channel_id=1, source_target_pairs={{0,64},{64,128},{128,192},{192,256},{256,320},{320,384},{384,448},... | collective-permute-start | bytes 43016
  108.3 1.3 dynamic-slice.4
  110.2 0.0 collective-permute-done.11
  110.3 0.6 concatenate
  110.8 0.1 constant_dynamic-slice_fusion
  110.9 0.1 copy.11
  111.1 22.6 %all_to_all.11 = bf16[64,8,182]{2,1,0:T(8,128)(2,1)S(1)} all-to-all(bf16[64,8,182]{2,1,0:T(8,128)(2,1)S(1)} %bitcast.29), channel_id=1, replica_groups={{0,1,2,3,4,5,6,7,8,9,10,11,12,13,14,15,16,17,18,19,20,21,22,23,24,25,26..., dimensions={0} | all-to-all | bytes 372736 | tf_op jit(solution)/shard_map/all_to_all | solution.py:215
  133.7 1.0 combine.1
  (2 shorter events, 0.0 us)
Async XLA Ops:
  0.6 3.6 %copy-start.2 = (bf16[256,180]{0,1:T(8,128)(2,1)S(1)}, bf16[256,180]{0,1:T(8,128)(2,1)}, u32[]{:S(2)}) copy-start(bf16[256,180]{0,1:T(8,128)(2,1)} %param.7) | copy-start | bytes 276484
  0.6 3.6 %copy-start.3 = (bf16[256,180]{0,1:T(8,128)(2,1)S(1)}, bf16[256,180]{0,1:T(8,128)(2,1)}, u32[]{:S(2)}) copy-start(bf16[256,180]{0,1:T(8,128)(2,1)} %param.8) | copy-start | bytes 276484
  0.7 3.6 %copy-start.4 = (s32[256,4]{0,1:T(4,128)S(1)}, s32[256,4]{0,1:T(4,128)}, u32[]{:S(2)}) copy-start(s32[256,4]{0,1:T(4,128)} %param.9) | copy-start | bytes 12292
  0.7 3.6 %copy-start.5 = (bf16[256,4]{0,1:T(4,128)(2,1)S(1)}, bf16[256,4]{0,1:T(4,128)(2,1)}, u32[]{:S(2)}) copy-start(bf16[256,4]{0,1:T(4,128)(2,1)} %param.10) | copy-start | bytes 6148
  31.1 27.7 %collective-permute-start.3 = (bf16[8,576,384]{2,1,0:T(8,128)(2,1)}, bf16[8,576,384]{2,1,0:T(8,128)(2,1)S(1)}, u32[]{:S(2)}, u32[]{:S(2)}) collective-permute-start(bf16[8,576,384]{2,1,0:T(8,128)(2,1)} %pack.1.refs_2_.refs_3_.refs_1_.own_w), channel_id=1, source_target_pairs={{0,32},{32,0},{64,96},{96,64},{128,160},{160,128},{192,224},{224,1... | collective-permute-start | bytes 10616840 | tf_op jit(solution)/shard_map/ppermute | solution.py:260
  33.0 12.6 %collective-permute-start = (bf16[256,768]{1,0:T(8,128)(2,1)S(1)}, bf16[256,768]{1,0:T(8,128)(2,1)S(1)}, u32[]{:S(2)}, u32[]{:S(2)}) collective-permute-start(bf16[256,768]{1,0:T(8,128)(2,1)S(1)} %join.1.refs_0_), channel_id=1, source_target_pairs={{32,64},{0,480},{96,128},{64,32},{160,192},{128,96},{224,256},{192... | collective-permute-start | bytes 1179656 | tf_op jit(solution)/shard_map/ppermute | solution.py:278
  37.4 19.4 %collective-permute-start.2 = (bf16[256,768]{1,0:T(8,128)(2,1)S(1)}, bf16[256,768]{1,0:T(8,128)(2,1)S(1)}, u32[]{:S(2)}, u32[]{:S(2)}) collective-permute-start(bf16[256,768]{1,0:T(8,128)(2,1)S(1)} %join.1.refs_0_), channel_id=1, source_target_pairs={{0,64},{32,480},{64,128},{96,32},{128,192},{160,96},{192,256},{224... | collective-permute-start | bytes 1179656 | tf_op jit(solution)/shard_map/ppermute | solution.py:277
  45.7 16.0 %collective-permute-start.1 = (bf16[256,768]{1,0:T(8,128)(2,1)S(1)}, bf16[256,768]{1,0:T(8,128)(2,1)S(1)}, u32[]{:S(2)}, u32[]{:S(2)}) collective-permute-start(bf16[256,768]{1,0:T(8,128)(2,1)S(1)} %collective-permute-done), channel_id=1, source_target_pairs={{0,64},{32,480},{64,128},{96,32},{128,192},{160,96},{192,256},{224... | collective-permute-start | bytes 1179656 | tf_op jit(solution)/shard_map/ppermute | solution.py:280
  56.8 9.7 %collective-permute-start.8 = (bf16[256,768]{1,0:T(8,128)(2,1)S(1)}, bf16[256,768]{1,0:T(8,128)(2,1)S(1)}, u32[]{:S(2)}, u32[]{:S(2)}) collective-permute-start(bf16[256,768]{1,0:T(8,128)(2,1)S(1)} %collective-permute-done.2.refs_1_), channel_id=1, source_target_pairs={{0,64},{32,480},{64,128},{96,32},{128,192},{160,96},{192,256},{224... | collective-permute-start | bytes 1179656 | tf_op jit(solution)/shard_map/ppermute | solution.py:279
  58.8 2.0 %copy-start = (bf16[8,576,384]{2,1,0:T(8,128)(2,1)S(1)}, bf16[8,576,384]{2,1,0:T(8,128)(2,1)}, u32[]{:S(2)}) copy-start(bf16[8,576,384]{2,1,0:T(8,128)(2,1)} %pack.1.refs_2_.refs_3_.refs_1_.own_w) | copy-start | bytes 10616836
  60.8 19.5 %copy-start.1 = (bf16[8,576,384]{2,1,0:T(8,128)(2,1)S(1)}, bf16[8,576,384]{2,1,0:T(8,128)(2,1)}, u32[]{:S(2)}) copy-start(bf16[8,576,384]{2,1,0:T(8,128)(2,1)} %pack.1.refs_2_.refs_3_.refs_1_.own_w) | copy-start | bytes 10616836
  61.6 11.0 %collective-permute-start.4 = (bf16[256,768]{1,0:T(8,128)(2,1)S(1)}, bf16[256,768]{1,0:T(8,128)(2,1)S(1)}, u32[]{:S(2)}, u32[]{:S(2)}) collective-permute-start(bf16[256,768]{1,0:T(8,128)(2,1)S(1)} %collective-permute-done.1), channel_id=1, source_target_pairs={{0,64},{32,480},{64,128},{96,32},{128,192},{160,96},{192,256},{224... | collective-permute-start | bytes 1179656 | tf_op jit(solution)/shard_map/ppermute | solution.py:286
  66.6 13.7 %collective-permute-start.10 = (bf16[256,768]{1,0:T(8,128)(2,1)S(1)}, bf16[256,768]{1,0:T(8,128)(2,1)S(1)}, u32[]{:S(2)}, u32[]{:S(2)}) collective-permute-start(bf16[256,768]{1,0:T(8,128)(2,1)S(1)} %collective-permute-done.8.refs_0_), channel_id=1, source_target_pairs={{0,64},{32,480},{64,128},{96,32},{128,192},{160,96},{192,256},{224... | collective-permute-start | bytes 1179656 | tf_op jit(solution)/shard_map/ppermute | solution.py:283
  70.8 9.5 %collective-permute-start.9 = (bf16[256,768]{1,0:T(8,128)(2,1)S(1)}, bf16[256,768]{1,0:T(8,128)(2,1)S(1)}, u32[]{:S(2)}, u32[]{:S(2)}) collective-permute-start(bf16[256,768]{1,0:T(8,128)(2,1)S(1)} %collective-permute-done), channel_id=1, source_target_pairs={{0,32},{32,0},{64,96},{96,64},{128,160},{160,128},{192,224},{224,1... | collective-permute-start | bytes 1179656 | tf_op jit(solution)/shard_map/ppermute | solution.py:282
  72.7 10.3 %collective-permute-start.7 = (bf16[256,768]{1,0:T(8,128)(2,1)S(1)}, bf16[256,768]{1,0:T(8,128)(2,1)S(1)}, u32[]{:S(2)}, u32[]{:S(2)}) collective-permute-start(bf16[256,768]{1,0:T(8,128)(2,1)S(1)} %collective-permute-done.4), channel_id=1, source_target_pairs={{0,96},{32,448},{64,160},{96,0},{128,224},{160,64},{192,288},{224,... | collective-permute-start | bytes 1179656 | tf_op jit(solution)/shard_map/ppermute | solution.py:287
  75.9 7.7 %collective-permute-start.5 = (bf16[256,768]{1,0:T(8,128)(2,1)S(1)}, bf16[256,768]{1,0:T(8,128)(2,1)S(1)}, u32[]{:S(2)}, u32[]{:S(2)}) collective-permute-start(bf16[256,768]{1,0:T(8,128)(2,1)S(1)} %collective-permute-done.1), channel_id=1, source_target_pairs={{0,32},{32,0},{64,96},{96,64},{128,160},{160,128},{192,224},{224,1... | collective-permute-start | bytes 1179656 | tf_op jit(solution)/shard_map/ppermute | solution.py:289
  77.8 5.7 %collective-permute-start.6 = (bf16[256,768]{1,0:T(8,128)(2,1)S(1)}, bf16[256,768]{1,0:T(8,128)(2,1)S(1)}, u32[]{:S(2)}, u32[]{:S(2)}) collective-permute-start(bf16[256,768]{1,0:T(8,128)(2,1)S(1)} %collective-permute-done.4), channel_id=1, source_target_pairs={{0,32},{32,0},{64,96},{96,64},{128,160},{160,128},{192,224},{224,1... | collective-permute-start | bytes 1179656 | tf_op jit(solution)/shard_map/ppermute | solution.py:290
  106.5 3.8 %collective-permute-start.11 = (bf16[28,256]{1,0:T(8,128)(2,1)S(1)}, bf16[28,256]{1,0:T(8,128)(2,1)S(1)}, u32[]{:S(2)}, u32[]{:S(2)}) collective-permute-start(bf16[28,256]{1,0:T(8,128)(2,1)S(1)} %slice), channel_id=1, source_target_pairs={{0,64},{64,128},{128,192},{192,256},{256,320},{320,384},{384,448},... | collective-permute-start | bytes 43016

commit v8 on v7

--- a/solution.py
+++ b/solution.py
@@ -130,7 +130,7 @@
 
 
 def backward_kernel(
-    places, me_ref, first_ref, second_ref, own_w, peer_w, own_sum, peer_sum, out_ref
+    places, me_ref, first_ref, second_ref, own_w, peer_w, own_sum, peer_sum, out_ref, terms
 ):
     weights = own_w, peer_w
     chips = own_w.shape[0]
@@ -160,11 +160,12 @@
     grad = jnp.concatenate(grads, axis=0)
     for k in range(chips):
         w = jnp.concatenate([ref[k, : 2 * HID, :] for ref in weights], axis=0)
-        value = lax.dot_general(w, grad, TN, preferred_element_type=F32).astype(BF16)
+        value = lax.dot_general(w, grad, TN, preferred_element_type=F32)
         for part in range(2):
             start = (2 * k + part) * BACK
-            out_ref[start : start + FEATS, :] = value[part * FEATS : (part + 1) * FEATS, :]
-            out_ref[start + FEATS : start + BACK, :] = value[CHIP : CHIP + 2, :]
+            terms[start : start + FEATS, :] = value[part * FEATS : (part + 1) * FEATS, :]
+            terms[start + FEATS : start + BACK, :] = value[CHIP : CHIP + 2, :]
+    out_ref[...] = terms[...].astype(BF16)
 
 
 def combine_kernel(ret_ref, sel_ref, ids_ref, tok_ref, gate_ref):
@@ -296,6 +297,7 @@
         in_specs=[SMEM] + [VMEM] * 6,
         out_specs=VMEM,
         out_shape=jax.ShapeDtypeStruct((groups * BACK, slots), BF16),
+        scratch_shapes=[pltpu.VMEM((groups * BACK, slots), F32)],
         compiler_params=LARGE,
         name="backward",
     )(me_arg, came2, came3, own_w, peer_w, *sums)

time: 135 us -> 135 us (level)
  no operation moved by 1% of the time
where the time goes in v8:
time: 135 us
  blocking collectives  69.3 us (51%)
  starting transfers between devices  48 us (36%)
  Pallas kernels  10.2 us (8%)
  local copies, waits for them, and re-layouts  4.09 us (3%)
  between operations  1.65 us (1%)
  waiting for transfers between devices  1.59 us (1%)
    all_to_all x2, blocking collectives, exchange(): lax.all_to_all(rows.reshape(2 * experts, HALF, rows.shape[-1]), ('grp', '...  48.7 us
    unnamed x1, blocking collectives  20.6 us
    ppermute x1, starting transfers between devices, per_device(): other2 = lax.ppermute(other1, 'grp', up)  11.2 us
    ppermute x1, starting transfers between devices, per_device(): mine1 = lax.ppermute(rows, 'grp', up)  8.23 us
    ppermute x1, starting transfers between devices, per_device(): other3 = lax.ppermute(other2, 'grp', up)  4.9 us
    ppermute x1, starting transfers between devices, per_device(): other1 = lax.ppermute(rows, 'grp', cross)  4.36 us
    ppermute x1, starting transfers between devices, per_device(): mine3 = lax.ppermute(mine2, 'grp', up)  4.19 us
    unnamed x16, local copies, waits for them, and re-layouts  3.92 us
  transfers between devices with their start and end apart: 12, of which 1 were waited for; matrix products, arithmetic and copies ran while one was open for 1% of the time, Pallas kernels for 2%

profile of v8, /device:TPU:1, one launch (start us, length us, event | category | flops | bytes accessed | tf_op | source)
XLA Modules:
  0.0 134.7 jit_solution(5249725230650047223)
XLA Ops:
  0.6 0.0 copy-start.2
  0.6 0.0 copy-start.3
  0.7 0.0 copy-start.4
  0.7 0.0 copy-start.5
  0.7 3.6 %pack.1.refs_2_.refs_3_.refs_1_.own_w = bf16[8,576,384]{2,1,0:T(8,128)(2,1)} custom-call(bf16[180,2880]{1,0:T(8,128)(2,1)} %bitcast.26, bf16[180,2880]{1,0:T(8,128)(2,1)} %bitcast.27, bf16[180,2880]{1,0:T(8,128)(2,1)} %bitcast.28), custom_call_target="tpu_custom_call" | custom-call | tf_op jit(solution)/shard_map/pack/pallas_call | solution.py:236
  4.3 0.0 copy-done.2
  4.3 0.0 copy-done.3
  4.3 0.0 copy-done.4
  4.3 0.0 copy-done.5
  4.3 0.5 dispatch.1
  4.8 26.1 %all_to_all.10 = bf16[64,8,384]{2,1,0:T(8,128)(2,1)S(1)} all-to-all(bf16[64,8,384]{2,1,0:T(8,128)(2,1)S(1)} %bitcast.20), channel_id=1, replica_groups={{0,1,2,3,4,5,6,7,8,9,10,11,12,13,14,15,16,17,18,19,20,21,22,23,24,25,26..., dimensions={0} | all-to-all | bytes 786432 | tf_op jit(solution)/shard_map/all_to_all | solution.py:216
  30.9 0.1 join.1.refs_0_
  31.1 1.9 %collective-permute-start.3 = (bf16[8,576,384]{2,1,0:T(8,128)(2,1)}, bf16[8,576,384]{2,1,0:T(8,128)(2,1)S(1)}, u32[]{:S(2)}, u32[]{:S(2)}) collective-permute-start(bf16[8,576,384]{2,1,0:T(8,128)(2,1)} %pack.1.refs_2_.refs_3_.refs_1_.own_w), channel_id=1, source_target_pairs={{0,32},{32,0},{64,96},{96,64},{128,160},{160,128},{192,224},{224,1... | collective-permute-start | bytes 10616840 | tf_op jit(solution)/shard_map/ppermute | solution.py:261
  33.0 4.4 %collective-permute-start = (bf16[256,768]{1,0:T(8,128)(2,1)S(1)}, bf16[256,768]{1,0:T(8,128)(2,1)S(1)}, u32[]{:S(2)}, u32[]{:S(2)}) collective-permute-start(bf16[256,768]{1,0:T(8,128)(2,1)S(1)} %join.1.refs_0_), channel_id=1, source_target_pairs={{32,64},{0,480},{96,128},{64,32},{160,192},{128,96},{224,256},{192... | collective-permute-start | bytes 1179656 | tf_op jit(solution)/shard_map/ppermute | solution.py:279
  37.4 8.2 %collective-permute-start.2 = (bf16[256,768]{1,0:T(8,128)(2,1)S(1)}, bf16[256,768]{1,0:T(8,128)(2,1)S(1)}, u32[]{:S(2)}, u32[]{:S(2)}) collective-permute-start(bf16[256,768]{1,0:T(8,128)(2,1)S(1)} %join.1.refs_0_), channel_id=1, source_target_pairs={{0,64},{32,480},{64,128},{96,32},{128,192},{160,96},{192,256},{224... | collective-permute-start | bytes 1179656 | tf_op jit(solution)/shard_map/ppermute | solution.py:278
  45.6 0.0 collective-permute-done
  45.7 11.2 %collective-permute-start.1 = (bf16[256,768]{1,0:T(8,128)(2,1)S(1)}, bf16[256,768]{1,0:T(8,128)(2,1)S(1)}, u32[]{:S(2)}, u32[]{:S(2)}) collective-permute-start(bf16[256,768]{1,0:T(8,128)(2,1)S(1)} %collective-permute-done), channel_id=1, source_target_pairs={{0,64},{32,480},{64,128},{96,32},{128,192},{160,96},{192,256},{224... | collective-permute-start | bytes 1179656 | tf_op jit(solution)/shard_map/ppermute | solution.py:281
  56.8 0.0 collective-permute-done.2.refs_1_
  56.8 1.9 %collective-permute-start.8 = (bf16[256,768]{1,0:T(8,128)(2,1)S(1)}, bf16[256,768]{1,0:T(8,128)(2,1)S(1)}, u32[]{:S(2)}, u32[]{:S(2)}) collective-permute-start(bf16[256,768]{1,0:T(8,128)(2,1)S(1)} %collective-permute-done.2.refs_1_), channel_id=1, source_target_pairs={{0,64},{32,480},{64,128},{96,32},{128,192},{160,96},{192,256},{224... | collective-permute-start | bytes 1179656 | tf_op jit(solution)/shard_map/ppermute | solution.py:280
  58.8 0.0 collective-permute-done.3.refs_3_.refs_4_.refs_2_.peer_w
  58.8 0.0 copy-start
  58.8 2.0 %copy-done = bf16[8,576,384]{2,1,0:T(8,128)(2,1)S(1)} copy-done((bf16[8,576,384]{2,1,0:T(8,128)(2,1)S(1)}, bf16[8,576,384]{2,1,0:T(8,128)(2,1)}, u32[]{:S(2)}) %copy-start) | copy-done | bytes 3538968
  60.8 0.0 copy-start.1
  60.8 0.8 forward.3
  61.6 0.0 collective-permute-done.1
  61.6 4.9 %collective-permute-start.4 = (bf16[256,768]{1,0:T(8,128)(2,1)S(1)}, bf16[256,768]{1,0:T(8,128)(2,1)S(1)}, u32[]{:S(2)}, u32[]{:S(2)}) collective-permute-start(bf16[256,768]{1,0:T(8,128)(2,1)S(1)} %collective-permute-done.1), channel_id=1, source_target_pairs={{0,64},{32,480},{64,128},{96,32},{128,192},{160,96},{192,256},{224... | collective-permute-start | bytes 1179656 | tf_op jit(solution)/shard_map/ppermute | solution.py:287
  66.5 0.0 collective-permute-done.8.refs_0_
  66.6 4.2 %collective-permute-start.10 = (bf16[256,768]{1,0:T(8,128)(2,1)S(1)}, bf16[256,768]{1,0:T(8,128)(2,1)S(1)}, u32[]{:S(2)}, u32[]{:S(2)}) collective-permute-start(bf16[256,768]{1,0:T(8,128)(2,1)S(1)} %collective-permute-done.8.refs_0_), channel_id=1, source_target_pairs={{0,64},{32,480},{64,128},{96,32},{128,192},{160,96},{192,256},{224... | collective-permute-start | bytes 1179656 | tf_op jit(solution)/shard_map/ppermute | solution.py:284
  70.8 1.9 %collective-permute-start.9 = (bf16[256,768]{1,0:T(8,128)(2,1)S(1)}, bf16[256,768]{1,0:T(8,128)(2,1)S(1)}, u32[]{:S(2)}, u32[]{:S(2)}) collective-permute-start(bf16[256,768]{1,0:T(8,128)(2,1)S(1)} %collective-permute-done), channel_id=1, source_target_pairs={{0,32},{32,0},{64,96},{96,64},{128,160},{160,128},{192,224},{224,1... | collective-permute-start | bytes 1179656 | tf_op jit(solution)/shard_map/ppermute | solution.py:283
  72.7 0.0 collective-permute-done.4
  72.7 3.2 %collective-permute-start.7 = (bf16[256,768]{1,0:T(8,128)(2,1)S(1)}, bf16[256,768]{1,0:T(8,128)(2,1)S(1)}, u32[]{:S(2)}, u32[]{:S(2)}) collective-permute-start(bf16[256,768]{1,0:T(8,128)(2,1)S(1)} %collective-permute-done.4), channel_id=1, source_target_pairs={{0,96},{32,448},{64,160},{96,0},{128,224},{160,64},{192,288},{224,... | collective-permute-start | bytes 1179656 | tf_op jit(solution)/shard_map/ppermute | solution.py:288
  75.9 1.9 %collective-permute-start.5 = (bf16[256,768]{1,0:T(8,128)(2,1)S(1)}, bf16[256,768]{1,0:T(8,128)(2,1)S(1)}, u32[]{:S(2)}, u32[]{:S(2)}) collective-permute-start(bf16[256,768]{1,0:T(8,128)(2,1)S(1)} %collective-permute-done.1), channel_id=1, source_target_pairs={{0,32},{32,0},{64,96},{96,64},{128,160},{160,128},{192,224},{224,1... | collective-permute-start | bytes 1179656 | tf_op jit(solution)/shard_map/ppermute | solution.py:290
  77.8 2.4 %collective-permute-start.6 = (bf16[256,768]{1,0:T(8,128)(2,1)S(1)}, bf16[256,768]{1,0:T(8,128)(2,1)S(1)}, u32[]{:S(2)}, u32[]{:S(2)}) collective-permute-start(bf16[256,768]{1,0:T(8,128)(2,1)S(1)} %collective-permute-done.4), channel_id=1, source_target_pairs={{0,32},{32,0},{64,96},{96,64},{128,160},{160,128},{192,224},{224,1... | collective-permute-start | bytes 1179656 | tf_op jit(solution)/shard_map/ppermute | solution.py:291
  80.2 0.0 collective-permute-done.10.refs_2_
  80.2 0.0 collective-permute-done.9.refs_1_
  80.2 0.0 copy-done.1
  80.3 1.2 forward.4
  81.4 1.6 %collective-permute-done.7.refs_0_ = bf16[256,768]{1,0:T(8,128)(2,1)S(1)} collective-permute-done((bf16[256,768]{1,0:T(8,128)(2,1)S(1)}, bf16[256,768]{1,0:T(8,128)(2,1)S(1)}, u32[]{:S(2)}, u32[]{:S(2)}) %collective-permute-start.7) | collective-permute-done | bytes 393248 | tf_op jit(solution)/shard_map/ppermute | solution.py:288
  83.0 0.5 forward.5
  83.5 0.0 collective-permute-done.5.first_ref
  83.5 0.0 collective-permute-done.6.second_ref
  83.6 2.4 %backward.1 = bf16[2912,256]{1,0:T(8,128)(2,1)S(1)} custom-call(s32[1]{0:T(128)} %bitcast.1.me_ref, bf16[256,768]{1,0:T(8,128)(2,1)S(1)} %collective-permute-done.5.first_ref, bf16[256,768]{1,0:T(8,128)(2,1)S(1)} %collective-permute-done.6.second_ref, bf16[8,576,384]{2,1,0:T(8,128)(2,1)S(1)} %copy-done.1, ...), custom_call_target="tpu_custom_call" | custom-call | tf_op jit(solution)/shard_map/backward/pallas_call | solution.py:295
  85.9 20.6 %fusion = bf16[368,256]{1,0:T(8,128)(2,1)S(1)} fusion(bf16[2912,256]{1,0:T(8,128)(2,1)S(1)} %backward.1), kind=kCustom, calls=%all-reduce-scatter | all-reduce-scatter fusion | flops 753665 | bytes 1681408
  106.5 1.8 %collective-permute-start.11 = (bf16[28,256]{1,0:T(8,128)(2,1)S(1)}, bf16[28,256]{1,0:T(8,128)(2,1)S(1)}, u32[]{:S(2)}, u32[]{:S(2)}) collective-permute-start(bf16[28,256]{1,0:T(8,128)(2,1)S(1)} %slice), channel_id=1, source_target_pairs={{0,64},{64,128},{128,192},{192,256},{256,320},{320,384},{384,448},... | collective-permute-start | bytes 43016
  108.3 1.3 dynamic-slice.4
  110.3 0.0 collective-permute-done.11
  110.3 0.6 concatenate
  110.9 0.1 constant_dynamic-slice_fusion
  111.0 0.1 copy.11
  111.1 22.6 %all_to_all.11 = bf16[64,8,182]{2,1,0:T(8,128)(2,1)S(1)} all-to-all(bf16[64,8,182]{2,1,0:T(8,128)(2,1)S(1)} %bitcast.29), channel_id=1, replica_groups={{0,1,2,3,4,5,6,7,8,9,10,11,12,13,14,15,16,17,18,19,20,21,22,23,24,25,26..., dimensions={0} | all-to-all | bytes 372736 | tf_op jit(solution)/shard_map/all_to_all | solution.py:216
  133.7 1.0 combine.1
  (2 shorter events, 0.0 us)
Async XLA Ops:
  0.6 3.6 %copy-start.2 = (bf16[256,180]{0,1:T(8,128)(2,1)S(1)}, bf16[256,180]{0,1:T(8,128)(2,1)}, u32[]{:S(2)}) copy-start(bf16[256,180]{0,1:T(8,128)(2,1)} %param.7) | copy-start | bytes 276484
  0.6 3.6 %copy-start.3 = (bf16[256,180]{0,1:T(8,128)(2,1)S(1)}, bf16[256,180]{0,1:T(8,128)(2,1)}, u32[]{:S(2)}) copy-start(bf16[256,180]{0,1:T(8,128)(2,1)} %param.8) | copy-start | bytes 276484
  0.7 3.6 %copy-start.4 = (s32[256,4]{0,1:T(4,128)S(1)}, s32[256,4]{0,1:T(4,128)}, u32[]{:S(2)}) copy-start(s32[256,4]{0,1:T(4,128)} %param.9) | copy-start | bytes 12292
  0.7 3.6 %copy-start.5 = (bf16[256,4]{0,1:T(4,128)(2,1)S(1)}, bf16[256,4]{0,1:T(4,128)(2,1)}, u32[]{:S(2)}) copy-start(bf16[256,4]{0,1:T(4,128)(2,1)} %param.10) | copy-start | bytes 6148
  31.1 27.7 %collective-permute-start.3 = (bf16[8,576,384]{2,1,0:T(8,128)(2,1)}, bf16[8,576,384]{2,1,0:T(8,128)(2,1)S(1)}, u32[]{:S(2)}, u32[]{:S(2)}) collective-permute-start(bf16[8,576,384]{2,1,0:T(8,128)(2,1)} %pack.1.refs_2_.refs_3_.refs_1_.own_w), channel_id=1, source_target_pairs={{0,32},{32,0},{64,96},{96,64},{128,160},{160,128},{192,224},{224,1... | collective-permute-start | bytes 10616840 | tf_op jit(solution)/shard_map/ppermute | solution.py:261
  33.0 12.6 %collective-permute-start = (bf16[256,768]{1,0:T(8,128)(2,1)S(1)}, bf16[256,768]{1,0:T(8,128)(2,1)S(1)}, u32[]{:S(2)}, u32[]{:S(2)}) collective-permute-start(bf16[256,768]{1,0:T(8,128)(2,1)S(1)} %join.1.refs_0_), channel_id=1, source_target_pairs={{32,64},{0,480},{96,128},{64,32},{160,192},{128,96},{224,256},{192... | collective-permute-start | bytes 1179656 | tf_op jit(solution)/shard_map/ppermute | solution.py:279
  37.4 19.4 %collective-permute-start.2 = (bf16[256,768]{1,0:T(8,128)(2,1)S(1)}, bf16[256,768]{1,0:T(8,128)(2,1)S(1)}, u32[]{:S(2)}, u32[]{:S(2)}) collective-permute-start(bf16[256,768]{1,0:T(8,128)(2,1)S(1)} %join.1.refs_0_), channel_id=1, source_target_pairs={{0,64},{32,480},{64,128},{96,32},{128,192},{160,96},{192,256},{224... | collective-permute-start | bytes 1179656 | tf_op jit(solution)/shard_map/ppermute | solution.py:278
  45.7 16.0 %collective-permute-start.1 = (bf16[256,768]{1,0:T(8,128)(2,1)S(1)}, bf16[256,768]{1,0:T(8,128)(2,1)S(1)}, u32[]{:S(2)}, u32[]{:S(2)}) collective-permute-start(bf16[256,768]{1,0:T(8,128)(2,1)S(1)} %collective-permute-done), channel_id=1, source_target_pairs={{0,64},{32,480},{64,128},{96,32},{128,192},{160,96},{192,256},{224... | collective-permute-start | bytes 1179656 | tf_op jit(solution)/shard_map/ppermute | solution.py:281
  56.8 9.7 %collective-permute-start.8 = (bf16[256,768]{1,0:T(8,128)(2,1)S(1)}, bf16[256,768]{1,0:T(8,128)(2,1)S(1)}, u32[]{:S(2)}, u32[]{:S(2)}) collective-permute-start(bf16[256,768]{1,0:T(8,128)(2,1)S(1)} %collective-permute-done.2.refs_1_), channel_id=1, source_target_pairs={{0,64},{32,480},{64,128},{96,32},{128,192},{160,96},{192,256},{224... | collective-permute-start | bytes 1179656 | tf_op jit(solution)/shard_map/ppermute | solution.py:280
  58.8 2.0 %copy-start = (bf16[8,576,384]{2,1,0:T(8,128)(2,1)S(1)}, bf16[8,576,384]{2,1,0:T(8,128)(2,1)}, u32[]{:S(2)}) copy-start(bf16[8,576,384]{2,1,0:T(8,128)(2,1)} %pack.1.refs_2_.refs_3_.refs_1_.own_w) | copy-start | bytes 10616836
  60.8 19.5 %copy-start.1 = (bf16[8,576,384]{2,1,0:T(8,128)(2,1)S(1)}, bf16[8,576,384]{2,1,0:T(8,128)(2,1)}, u32[]{:S(2)}) copy-start(bf16[8,576,384]{2,1,0:T(8,128)(2,1)} %pack.1.refs_2_.refs_3_.refs_1_.own_w) | copy-start | bytes 10616836
  61.6 11.0 %collective-permute-start.4 = (bf16[256,768]{1,0:T(8,128)(2,1)S(1)}, bf16[256,768]{1,0:T(8,128)(2,1)S(1)}, u32[]{:S(2)}, u32[]{:S(2)}) collective-permute-start(bf16[256,768]{1,0:T(8,128)(2,1)S(1)} %collective-permute-done.1), channel_id=1, source_target_pairs={{0,64},{32,480},{64,128},{96,32},{128,192},{160,96},{192,256},{224... | collective-permute-start | bytes 1179656 | tf_op jit(solution)/shard_map/ppermute | solution.py:287
  66.6 13.7 %collective-permute-start.10 = (bf16[256,768]{1,0:T(8,128)(2,1)S(1)}, bf16[256,768]{1,0:T(8,128)(2,1)S(1)}, u32[]{:S(2)}, u32[]{:S(2)}) collective-permute-start(bf16[256,768]{1,0:T(8,128)(2,1)S(1)} %collective-permute-done.8.refs_0_), channel_id=1, source_target_pairs={{0,64},{32,480},{64,128},{96,32},{128,192},{160,96},{192,256},{224... | collective-permute-start | bytes 1179656 | tf_op jit(solution)/shard_map/ppermute | solution.py:284
  70.8 9.5 %collective-permute-start.9 = (bf16[256,768]{1,0:T(8,128)(2,1)S(1)}, bf16[256,768]{1,0:T(8,128)(2,1)S(1)}, u32[]{:S(2)}, u32[]{:S(2)}) collective-permute-start(bf16[256,768]{1,0:T(8,128)(2,1)S(1)} %collective-permute-done), channel_id=1, source_target_pairs={{0,32},{32,0},{64,96},{96,64},{128,160},{160,128},{192,224},{224,1... | collective-permute-start | bytes 1179656 | tf_op jit(solution)/shard_map/ppermute | solution.py:283
  72.7 10.3 %collective-permute-start.7 = (bf16[256,768]{1,0:T(8,128)(2,1)S(1)}, bf16[256,768]{1,0:T(8,128)(2,1)S(1)}, u32[]{:S(2)}, u32[]{:S(2)}) collective-permute-start(bf16[256,768]{1,0:T(8,128)(2,1)S(1)} %collective-permute-done.4), channel_id=1, source_target_pairs={{0,96},{32,448},{64,160},{96,0},{128,224},{160,64},{192,288},{224,... | collective-permute-start | bytes 1179656 | tf_op jit(solution)/shard_map/ppermute | solution.py:288
  75.9 7.7 %collective-permute-start.5 = (bf16[256,768]{1,0:T(8,128)(2,1)S(1)}, bf16[256,768]{1,0:T(8,128)(2,1)S(1)}, u32[]{:S(2)}, u32[]{:S(2)}) collective-permute-start(bf16[256,768]{1,0:T(8,128)(2,1)S(1)} %collective-permute-done.1), channel_id=1, source_target_pairs={{0,32},{32,0},{64,96},{96,64},{128,160},{160,128},{192,224},{224,1... | collective-permute-start | bytes 1179656 | tf_op jit(solution)/shard_map/ppermute | solution.py:290
  77.8 5.7 %collective-permute-start.6 = (bf16[256,768]{1,0:T(8,128)(2,1)S(1)}, bf16[256,768]{1,0:T(8,128)(2,1)S(1)}, u32[]{:S(2)}, u32[]{:S(2)}) collective-permute-start(bf16[256,768]{1,0:T(8,128)(2,1)S(1)} %collective-permute-done.4), channel_id=1, source_target_pairs={{0,32},{32,0},{64,96},{96,64},{128,160},{160,128},{192,224},{224,1... | collective-permute-start | bytes 1179656 | tf_op jit(solution)/shard_map/ppermute | solution.py:291
  106.5 3.8 %collective-permute-start.11 = (bf16[28,256]{1,0:T(8,128)(2,1)S(1)}, bf16[28,256]{1,0:T(8,128)(2,1)S(1)}, u32[]{:S(2)}, u32[]{:S(2)}) collective-permute-start(bf16[28,256]{1,0:T(8,128)(2,1)S(1)} %slice), channel_id=1, source_target_pairs={{0,64},{64,128},{128,192},{192,256},{256,320},{320,384},{384,448},... | collective-permute-start | bytes 43016
